TPU v7x, 32 devices: a whole 2x2x4 slice. The times are simulated.
32 devices in a mesh: tm: 8 (over z, x), tile: 4 (over y, core).
Axes of the slice: x: 2, y: 2, z: 4, core: 2. Of those that a mesh axis runs over, the one named last changes fastest.
Arguments:
- frames: bfloat16 [32, 64, 64, 128], P('tm', 'tile'), may hold values from -6 to 6
- cotangent: bfloat16 [32, 64, 64, 128], P('tm', 'tile'), may hold values from -6 to 6
- w_in: bfloat16 [3, 3, 128, 128], replicated, may hold values from -0.1875 to 0.1875
- w_out: bfloat16 [3, 3, 128, 128], replicated, may hold values from -0.1875 to 0.1875
- skip: float32 [128], replicated, may hold values from 0.5 to 1.5
- log_decay: float32 [32, 128], P('tm'), may hold values from -1 to 0
Outputs:
- output: bfloat16 [32, 64, 64, 128], P('tm', 'tile')
- grad_frames: bfloat16 [32, 64, 64, 128], P('tm', 'tile')
- grad_w_in: float32 [3, 3, 128, 128], replicated
- grad_w_out: float32 [3, 3, 128, 128], replicated
All inputs are finite; a program needn't handle non-finite values.
Results may differ from a plain program's by a relative error of at most 0.0029.
Values may be sent and summed in bfloat16 or wider, within the bound.
No kernel may reach another device: no remote copies, remote signals or barrier semaphores. Data moves between devices by JAX's collectives and lax.ppermute only.
A program may use at most 64 MiB of HBM per device.

v0:
```python
import math

import jax
import jax.numpy as jnp
from jax import lax
from jax.sharding import PartitionSpec as P


def extended(block, sides, width):
    for axis, dim in sides:
        count = lax.axis_size(axis)
        forward = [(i, i + 1) for i in range(count - 1)]
        backward = [(target, source) for source, target in forward]
        low = lax.ppermute(
            lax.slice_in_dim(block, block.shape[dim] - width, None, axis=dim), axis, forward
        )
        high = lax.ppermute(lax.slice_in_dim(block, 0, width, axis=dim), axis, backward)
        block = jnp.concatenate([low, block, high], axis=dim)
    return block


def flipped(weight):
    return jnp.transpose(weight[::-1, ::-1], (0, 1, 3, 2))


def widen_cols(field):
    return jnp.pad(field, ((0, 0), (0, 0), (1, 1), (0, 0)))


def convolve(padded, weight):
    rows = padded.shape[1] - 2
    cols = padded.shape[2] - 2
    result = jnp.zeros((padded.shape[0], rows, cols, weight.shape[3]), jnp.float32)
    for row_off in range(3):
        for col_off in range(3):
            piece = padded[:, row_off : row_off + rows, col_off : col_off + cols, :].reshape(
                -1, weight.shape[2]
            )
            result = result + jnp.dot(
                piece, weight[row_off, col_off], preferred_element_type=jnp.float32
            ).reshape(result.shape)
    return result


def weight_grad(padded, target):
    rows = target.shape[1]
    cols = target.shape[2]
    flat = target.reshape(-1, target.shape[3])
    pieces = []
    for row_off in range(3):
        line = []
        for col_off in range(3):
            piece = padded[:, row_off : row_off + rows, col_off : col_off + cols, :].reshape(
                -1, padded.shape[3]
            )
            line.append(
                lax.dot_general(
                    piece, flat, (((0,), (0,)), ((), ())), preferred_element_type=jnp.float32
                )
            )
        pieces.append(jnp.stack(line))
    return jnp.stack(pieces)


def shards(frames, cotangent, w_in, w_out, skip, log_decay):
    decay = jnp.exp(log_decay)
    frames_padded = widen_cols(extended(frames, (("tile", 1),), 1))
    drive = convolve(frames_padded, w_in)
    cot_padded = widen_cols(extended(cotangent, (("tile", 1),), 1))
    state_grad = convolve(cot_padded, flipped(w_out))

    def advance(state, item):
        rate, inflow = item
        state = rate * state + (1.0 - rate) * inflow
        return (state, state)

    blank = jnp.zeros(drive.shape[1:], jnp.float32)
    _, local_states = lax.scan(advance, blank, (decay, drive))
    cumulative = jnp.cumsum(log_decay, axis=0)
    whole_decay = jnp.exp(cumulative[-1])
    reach = jnp.exp(cumulative)
    tail = jnp.exp(cumulative[-1][None, :] - cumulative)

    def retreat(carry, item):
        rate, grad_here = item
        adjoint = grad_here + carry
        return (rate * adjoint, adjoint)

    outflow, local_adjoints = lax.scan(retreat, blank, (decay, state_grad), reverse=True)
    totals, ends, leaving = (
        lax.all_gather(whole_decay[None], "tm", axis=0, tiled=True),
        lax.all_gather(local_states[-1][None], "tm", axis=0, tiled=True),
        lax.all_gather(outflow[None], "tm", axis=0, tiled=True),
    )
    place = lax.axis_index("tm")
    count = lax.axis_size("tm")

    def forward_fold(step, carry):
        return jnp.where(step < place, totals[step] * carry + ends[step], carry)

    def backward_fold(step, carry):
        other = count - 1 - step
        return jnp.where(other > place, leaving[other] + totals[other] * carry, carry)

    incoming_state = lax.fori_loop(0, count, forward_fold, blank)
    incoming_adjoint = lax.fori_loop(0, count, backward_fold, blank)
    states = local_states + reach[:, None, None, :] * incoming_state[None]
    states_bf = states.astype(jnp.bfloat16)
    states_padded = widen_cols(extended(states_bf, (("tile", 1),), 1))
    output = (convolve(states_padded, w_out) + skip * frames.astype(jnp.float32)).astype(
        jnp.bfloat16
    )
    factor = 1.0 / math.sqrt(
        frames.shape[0]
        * lax.axis_size("tm")
        * frames.shape[1]
        * lax.axis_size("tile")
        * frames.shape[2]
    )
    out_partial = weight_grad(states_padded, cotangent)
    adjoints = local_adjoints + tail[:, None, None, :] * incoming_adjoint[None]
    inflow_wide = ((1.0 - decay)[:, None, None, :] * adjoints).astype(jnp.bfloat16)
    inflow_padded = widen_cols(extended(inflow_wide, (("tile", 1),), 1))
    grad_frames = (
        convolve(inflow_padded, flipped(w_in)) + skip * cotangent.astype(jnp.float32)
    ).astype(jnp.bfloat16)
    in_partial = weight_grad(frames_padded, inflow_wide)
    in_summed, out_summed = lax.psum((in_partial, out_partial), ("tm", "tile"))
    return (output, grad_frames, in_summed * factor, out_summed * factor)


def solution(mesh):
    placed = (
        P("tm", "tile", None, None),
        P("tm", "tile", None, None),
        P(),
        P(),
        P(),
        P("tm", None),
    )
    return jax.shard_map(
        shards,
        mesh=mesh,
        in_specs=placed,
        out_specs=(P("tm", "tile", None, None), P("tm", "tile", None, None), P(), P()),
        check_vma=False,
    )
```

profile of v0, /device:TPU:0, one launch (start us, length us, event | category | flops | bytes accessed | tf_op | source)
XLA Modules:
  0.0 388.0 jit_solution(5049280285538315346)
XLA Ops:
  8.2 2.4 collective-permute-start
  10.6 1.4 collective-permute-start.1
  12.0 3.0 fusion.114
  21.9 2.4 add_add_fusion.1
  24.3 1.7 broadcast.32.clone
  26.0 8.6 %while.60 = (s32[]{:T(128)}, f32[16,64,128]{2,1,0:T(8,128)S(1)}, f32[4,16,64,128]{3,2,1,0:T(8,128)}, f32[4,128]{1,0:T(4,128)S(1)}, f32[4,16,64,128]{3,2,1,0:T(8,128)}, /*index=5*/s32[]{:T(128)}, s32[]{:T(128)}) while((s32[]{:T(128)}, f32[16,64,128]{2,1,0:T(8,128)S(1)}, f32[4,16,64,128]{3,2,1,0:T(8,128)}, f32[4,128]{1,0:T(4,128)S(1)}, ...), condition=%wide.region_1.2_spmd.clone, body=%wide.region_0.1_spmd.clone.sunk | while | flops 524419 | bytes 2100315 | solution.py:78
  26.0 2.2 bitcast_dynamic-update-slice_fusion.4
  28.2 2.1 bitcast_dynamic-update-slice_fusion.4
  30.3 2.1 bitcast_dynamic-update-slice_fusion.4
  32.4 2.1 bitcast_dynamic-update-slice_fusion.4
  34.6 1.9 slice.297
  37.2 4.8 %collective-permute-start.4 = (bf16[4,1,64,128]{3,2,1,0:T(8,128)(2,1)}, bf16[4,1,64,128]{3,2,1,0:T(8,128)(2,1)S(1)}, u32[]{:S(2)}, u32[]{:S(2)}) collective-permute-start(bf16[4,1,64,128]{3,2,1,0:T(8,128)(2,1)} %get-tuple-element.486), channel_id=1, source_target_pairs={{0,1},{1,2},{2,3},{4,5},{5,6},{6,7},{8,9},{9,10},{10,11},{12,13},{... | collective-permute-start | bytes 196616 | tf_op jit(solution)/shard_map/ppermute | solution.py:14
  43.6 1.8 fusion.98
  46.7 1.5 select_maximum_fusion.2
  53.1 2.4 add_add_fusion
  55.5 1.6 broadcast.32.clone.1
  57.1 15.3 %while.62 = (s32[]{:T(128)}, f32[16,64,128]{2,1,0:T(8,128)S(1)}, f32[4,16,64,128]{3,2,1,0:T(8,128)}, f32[4,128]{1,0:T(4,128)}, f32[4,16,64,128]{3,2,1,0:T(8,128)}, /*index=5*/s32[]{:T(128)}, s32[]{:T(128)}, s32[]{:T(128)}) while((s32[]{:T(128)}, f32[16,64,128]{2,1,0:T(8,128)S(1)}, f32[4,16,64,128]{3,2,1,0:T(8,128)}, ...), condition=%wide.region_6.7_spmd.clone, body=%wide.region_5.6_spmd.clone.sunk | while | flops 655364 | bytes 3147384 | solution.py:89
  57.1 1.9 bitcast_dynamic-update-slice_fusion.5
  60.9 1.9 bitcast_dynamic-update-slice_fusion.5
  64.8 1.9 bitcast_dynamic-update-slice_fusion.5
  68.6 1.9 bitcast_dynamic-update-slice_fusion.5
  73.3 1.8 copy.14
  75.2 21.1 %all-gather.1 = f32[8,1,128]{2,1,0:T(1,128)S(1)} all-gather(f32[1,1,128]{2,1,0:T(1,128)S(1)} %get-tuple-element.499), channel_id=1, replica_groups=mesh['tm'=8,'tile'=4] {'tm'}, dimensions={0}, use_global_device_ids=true | all-gather | bytes 4608 | tf_op jit(solution)/shard_map/all_gather | solution.py:91
  96.3 1.7 reverse_bitcast_fusion
  98.0 16.3 %all-gather.5.cloned.1.call-done = f32[8,16,64,128]{3,2,1,0:T(8,128)} async-done(((f32[1,16,64,128]{3,2,1,0:T(8,128)}), f32[8,16,64,128]{3,2,1,0:T(8,128)}) %all-gather.5.cloned.1.call-update) | async-done | bytes 4194320 | tf_op jit(solution)/shard_map/all_gather | solution.py:92
  114.3 12.2 %while.61 = (s32[]{:T(128)}, f32[16,64,128]{2,1,0:T(8,128)S(1)}, s32[]{:T(128)}, f32[8,128]{1,0:T(8,128)S(1)}, f32[8,16,64,128]{3,2,1,0:T(8,128)}, /*index=5*/s32[]{:T(128)}, s32[]{:T(128)}) while((s32[]{:T(128)}, f32[16,64,128]{2,1,0:T(8,128)S(1)}, s32[]{:T(128)}, f32[8,128]{1,0:T(8,128)S(1)}, f32[8,16,64,128]{3,2,1,0:T(8,128)}, ...), condition=%wide.region_4.5_spmd.clone, body=%wide.region_3.4_spmd.clone.sunk | while | flops 524292 | bytes 1574505 | solution.py:105
  114.3 1.5 fusion.184
  115.8 1.5 fusion.184
  117.3 1.5 fusion.184
  118.8 1.5 fusion.184
  120.4 1.5 fusion.184
  121.9 1.5 fusion.184
  123.4 1.5 fusion.184
  125.0 1.5 fusion.184
  126.5 1.9 add_convert_fusion.2
  129.5 59.1 %all-gather.7.cloned.1.call-done = f32[128,64,128]{2,1,0:T(8,128)} async-done(((f32[16,64,128]{2,1,0:T(8,128)}), f32[128,64,128]{2,1,0:T(8,128)}) %all-gather.7.cloned.1.call-update) | async-done | bytes 4194320 | tf_op jit(solution)/shard_map/all_gather | solution.py:93
  188.7 11.0 %while.63 = (s32[]{:T(128)}, f32[16,64,128]{2,1,0:T(8,128)S(1)}, s32[]{:T(128)}, f32[8,16,64,128]{3,2,1,0:T(8,128)}, f32[8,128]{1,0:T(8,128)S(1)}, /*index=5*/s32[]{:T(128)}, s32[]{:T(128)}, s32[]{:T(128)}, s32[]{:T(128)}) while((s32[]{:T(128)}, f32[16,64,128]{2,1,0:T(8,128)S(1)}, s32[]{:T(128)}, f32[8,16,64,128]{3,2,1,0:T(8,128)}, ...), condition=%wide.region_8.9_spmd.clone, body=%wide.region_7.8_spmd.clone.sunk | while | flops 524296 | bytes 1574567 | solution.py:106
  190.1 1.3 fusion.186
  191.4 1.3 fusion.186
  192.8 1.3 fusion.186
  194.2 1.3 fusion.186
  195.6 1.3 fusion.186
  197.0 1.3 fusion.186
  199.7 2.0 multiply_convert_fusion
  207.7 1.8 fusion.103
  212.1 4.7 %collective-permute-start.6 = (bf16[4,1,64,128]{3,2,1,0:T(8,128)(2,1)S(1)}, bf16[4,1,64,128]{3,2,1,0:T(8,128)(2,1)S(1)}, u32[]{:S(2)}, u32[]{:S(2)}) collective-permute-start(bf16[4,1,64,128]{3,2,1,0:T(8,128)(2,1)S(1)} %get-tuple-element.484), channel_id=1, source_target_pairs={{0,1},{1,2},{2,3},{4,5},{5,6},{6,7},{8,9},{9,10},{10,11},{12,13},{... | collective-permute-start | bytes 196616 | tf_op jit(solution)/shard_map/ppermute | solution.py:14
  216.8 1.5 collective-permute-start.7
  218.3 1.8 fusion.97
  225.3 1.8 fusion.33
  227.2 1.8 fusion.35
  228.9 1.8 fusion.37
  230.7 1.8 fusion.39
  232.5 1.7 fusion.31
  234.2 1.7 fusion.61
  235.9 1.8 fusion.64
  237.8 1.7 fusion.67
  239.5 1.9 fusion.70
  241.3 1.7 fusion.73
  245.4 1.8 fusion.19
  249.2 6.3 %add_convert_fusion = bf16[4,16,64,128]{3,2,1,0:T(8,128)(2,1)} fusion(bf16[4,16,64,128]{3,2,1,0:T(8,128)(2,1)S(1)} %copy-done.5, f32[4,16,64,128]{3,2,1,0:T(8,128)S(1)} %fusion.23, f32[4,16,64,128]{3,2,1,0:T(8,128)} %fusion.31, f32[4,16,64,128]{3,2,1,0:T(8,128)S(1)} %copy-done.21, f32[4,16,64,128]{3,2,1,0:T(8,128)S(1)} %copy-done.15, ...), kind=kOutput, calls=%fused_computation.21 | convolution fusion | flops 140509184 | bytes 19956224 | tf_op jit(solution)/shard_map/dot_general | solution.py:39
  258.4 2.2 add_convert_fusion.1
  260.6 117.0 %all-reduce.7.cloned.1.call-done = (f32[3,3,128,128]{3,2,1,0:T(8,128)}, f32[3,3,128,128]{3,2,1,0:T(8,128)}) async-done(((f32[3,3,128,128]{3,2,1,0:T(8,128)}, f32[3,3,128,128]{3,2,1,0:T(8,128)}), (f32[3,3,128,128]{3,2,1,0:T(8,128)}, f32[3,3,128,128]{3,2,1,0:T(8,128)})) %all-reduce.7.cloned.1.call-update) | async-done | bytes 1179664 | tf_op jit(solution)/shard_map/psum | solution.py:128
  377.6 1.9 broadcast_multiply_fusion.1
  379.5 1.9 broadcast_multiply_fusion.2
  (190 shorter events, 49.5 us)
Async XLA Ops:
  7.2 8.8 %copy-start.6 = (bf16[4,16,64,128]{3,2,1,0:T(8,128)(2,1)S(1)}, bf16[4,16,64,128]{3,2,1,0:T(8,128)(2,1)}, u32[]{:S(2)}) copy-start(bf16[4,16,64,128]{3,2,1,0:T(8,128)(2,1)} %param.14) | copy-start | bytes 3145732
  7.2 7.8 %copy-start.38 = (f32[4,128]{1,0:T(4,128)S(1)}, f32[4,128]{1,0:T(4,128)}, u32[]{:S(2)}) copy-start(f32[4,128]{1,0:T(4,128)} %param.19) | copy-start | bytes 6148
  7.2 107.1 %all-gather.5.cloned.1.call-start = ((), (), s32[]{:S(2)}) async-start(), calls=%async_computation | async-start | bytes 4718592 | tf_op jit(solution)/shard_map/all_gather | solution.py:92
  8.2 7.3 %collective-permute-start = (bf16[4,1,64,128]{3,2,1,0:T(8,128)(2,1)S(1)}, bf16[4,1,64,128]{3,2,1,0:T(8,128)(2,1)S(1)}, u32[]{:S(2)}, u32[]{:S(2)}) collective-permute-start(bf16[4,1,64,128]{3,2,1,0:T(8,128)(2,1)S(1)} %get-tuple-element.492), channel_id=1, source_target_pairs={{0,1},{1,2},{2,3},{4,5},{5,6},{6,7},{8,9},{9,10},{10,11},{12,13},{... | collective-permute-start | bytes 196616 | tf_op jit(solution)/shard_map/ppermute | solution.py:14
  10.6 6.1 %copy-start.26 = (bf16[3,3,128,128]{3,2,1,0:T(8,128)(2,1)S(1)}, bf16[3,3,128,128]{3,2,1,0:T(8,128)(2,1)}, u32[]{:S(2)}) copy-start(bf16[3,3,128,128]{3,2,1,0:T(8,128)(2,1)} %param.16) | copy-start | bytes 884740
  10.6 5.4 %collective-permute-start.1 = (bf16[4,1,64,128]{3,2,1,0:T(8,128)(2,1)S(1)}, bf16[4,1,64,128]{3,2,1,0:T(8,128)(2,1)S(1)}, u32[]{:S(2)}, u32[]{:S(2)}) collective-permute-start(bf16[4,1,64,128]{3,2,1,0:T(8,128)(2,1)S(1)} %get-tuple-element.493), channel_id=1, source_target_pairs={{1,0},{2,1},{3,2},{5,4},{6,5},{7,6},{9,8},{10,9},{11,10},{13,12},{... | collective-permute-start | bytes 196616 | tf_op jit(solution)/shard_map/ppermute | solution.py:17
  19.2 1.4 copy-start.24
  19.3 1.0 copy-start.22
  20.3 1.6 copy-start.12
  26.0 10.6 %copy-start.3 = (bf16[4,16,64,128]{3,2,1,0:T(8,128)(2,1)S(1)}, bf16[4,16,64,128]{3,2,1,0:T(8,128)(2,1)}, u32[]{:S(2)}) copy-start(bf16[4,16,64,128]{3,2,1,0:T(8,128)(2,1)} %param.15) | copy-start | bytes 3145732
  26.0 17.4 %copy-start.27 = (bf16[3,3,128,128]{3,2,1,0:T(8,128)(2,1)S(1)}, bf16[3,3,128,128]{3,2,1,0:T(8,128)(2,1)}, u32[]{:S(2)}) copy-start(bf16[3,3,128,128]{3,2,1,0:T(8,128)(2,1)} %param.17) | copy-start | bytes 884740
  34.6 7.5 %copy-start.36 = (f32[4,128]{1,0:T(4,128)}, f32[4,128]{1,0:T(4,128)S(1)}, u32[]{:S(2)}) copy-start(f32[4,128]{1,0:T(4,128)S(1)} %get-tuple-element.760) | copy-start | bytes 6148
  36.5 152.2 %all-gather.7.cloned.1.call-start = ((), (), s32[]{:S(2)}) async-start(), calls=%async_computation.1 | async-start | bytes 4718592 | tf_op jit(solution)/shard_map/all_gather | solution.py:93
  37.2 8.2 %collective-permute-start.4 = (bf16[4,1,64,128]{3,2,1,0:T(8,128)(2,1)}, bf16[4,1,64,128]{3,2,1,0:T(8,128)(2,1)S(1)}, u32[]{:S(2)}, u32[]{:S(2)}) collective-permute-start(bf16[4,1,64,128]{3,2,1,0:T(8,128)(2,1)} %get-tuple-element.486), channel_id=1, source_target_pairs={{0,1},{1,2},{2,3},{4,5},{5,6},{6,7},{8,9},{9,10},{10,11},{12,13},{... | collective-permute-start | bytes 196616 | tf_op jit(solution)/shard_map/ppermute | solution.py:14
  42.0 4.6 %collective-permute-start.5 = (bf16[4,1,64,128]{3,2,1,0:T(8,128)(2,1)}, bf16[4,1,64,128]{3,2,1,0:T(8,128)(2,1)}, u32[]{:S(2)}, u32[]{:S(2)}) collective-permute-start(bf16[4,1,64,128]{3,2,1,0:T(8,128)(2,1)} %get-tuple-element.487), channel_id=1, source_target_pairs={{1,0},{2,1},{3,2},{5,4},{6,5},{7,6},{9,8},{10,9},{11,10},{13,12},{... | collective-permute-start | bytes 196616 | tf_op jit(solution)/shard_map/ppermute | solution.py:17
  51.5 1.6 copy-start.13
  57.1 18.1 %copy-start.39 = (f32[4,128]{1,0:T(4,128)S(1)}, f32[4,128]{1,0:T(4,128)}, u32[]{:S(2)}) copy-start(f32[4,128]{1,0:T(4,128)} %param.19) | copy-start | bytes 6148
  72.4 0.8 copy-start
  73.3 304.4 %all-reduce.7.cloned.1.call-start = ((), (), s32[]{:S(2)}) async-start(), calls=%async_computation.2 | async-start | bytes 2359296 | tf_op jit(solution)/shard_map/psum | solution.py:128
  128.4 1.2 copy-start.9
  188.7 11.0 %copy-start.37 = (f32[4,128]{1,0:T(4,128)S(1)}, f32[4,128]{1,0:T(4,128)}, u32[]{:S(2)}) copy-start(f32[4,128]{1,0:T(4,128)} %get-tuple-element.494) | copy-start | bytes 6148
  199.7 2.1 copy-start.25
  201.8 22.9 %copy-start.1 = (bf16[4,16,64,128]{3,2,1,0:T(8,128)(2,1)}, bf16[4,16,64,128]{3,2,1,0:T(8,128)(2,1)S(1)}, u32[]{:S(2)}) copy-start(bf16[4,16,64,128]{3,2,1,0:T(8,128)(2,1)S(1)} %multiply_convert_fusion) | copy-start | bytes 3145732
  203.7 1.2 copy-start.7
  203.7 1.7 copy-start.23
  206.4 1.2 copy-start.10
  206.4 1.3 copy-start.28
  207.0 11.4 %copy-start.29 = (bf16[3,3,128,128]{3,2,1,0:T(8,128)(2,1)S(1)}, bf16[3,3,128,128]{3,2,1,0:T(8,128)(2,1)}, u32[]{:S(2)}) copy-start(bf16[3,3,128,128]{3,2,1,0:T(8,128)(2,1)} %reverse_bitcast_fusion) | copy-start | bytes 884740
  209.5 11.6 %collective-permute-start.2 = (bf16[4,1,64,128]{3,2,1,0:T(8,128)(2,1)S(1)}, bf16[4,1,64,128]{3,2,1,0:T(8,128)(2,1)S(1)}, u32[]{:S(2)}, u32[]{:S(2)}) collective-permute-start(bf16[4,1,64,128]{3,2,1,0:T(8,128)(2,1)S(1)} %get-tuple-element.488), channel_id=1, source_target_pairs={{0,1},{1,2},{2,3},{4,5},{5,6},{6,7},{8,9},{9,10},{10,11},{12,13},{... | collective-permute-start | bytes 196616 | tf_op jit(solution)/shard_map/ppermute | solution.py:14
  210.8 10.3 %collective-permute-start.3 = (bf16[4,1,64,128]{3,2,1,0:T(8,128)(2,1)S(1)}, bf16[4,1,64,128]{3,2,1,0:T(8,128)(2,1)S(1)}, u32[]{:S(2)}, u32[]{:S(2)}) collective-permute-start(bf16[4,1,64,128]{3,2,1,0:T(8,128)(2,1)S(1)} %get-tuple-element.489), channel_id=1, source_target_pairs={{1,0},{2,1},{3,2},{5,4},{6,5},{7,6},{9,8},{10,9},{11,10},{13,12},{... | collective-permute-start | bytes 196616 | tf_op jit(solution)/shard_map/ppermute | solution.py:17
  212.1 12.6 %collective-permute-start.6 = (bf16[4,1,64,128]{3,2,1,0:T(8,128)(2,1)S(1)}, bf16[4,1,64,128]{3,2,1,0:T(8,128)(2,1)S(1)}, u32[]{:S(2)}, u32[]{:S(2)}) collective-permute-start(bf16[4,1,64,128]{3,2,1,0:T(8,128)(2,1)S(1)} %get-tuple-element.484), channel_id=1, source_target_pairs={{0,1},{1,2},{2,3},{4,5},{5,6},{6,7},{8,9},{9,10},{10,11},{12,13},{... | collective-permute-start | bytes 196616 | tf_op jit(solution)/shard_map/ppermute | solution.py:14
  216.8 7.8 %collective-permute-start.7 = (bf16[4,1,64,128]{3,2,1,0:T(8,128)(2,1)S(1)}, bf16[4,1,64,128]{3,2,1,0:T(8,128)(2,1)S(1)}, u32[]{:S(2)}, u32[]{:S(2)}) collective-permute-start(bf16[4,1,64,128]{3,2,1,0:T(8,128)(2,1)S(1)} %get-tuple-element.485), channel_id=1, source_target_pairs={{1,0},{2,1},{3,2},{5,4},{6,5},{7,6},{9,8},{10,9},{11,10},{13,12},{... | collective-permute-start | bytes 196616 | tf_op jit(solution)/shard_map/ppermute | solution.py:17
  221.1 22.0 %copy-start.30 = (bf16[4,1,64,128]{3,2,1,0:T(8,128)(2,1)}, bf16[4,1,64,128]{3,2,1,0:T(8,128)(2,1)S(1)}, u32[]{:S(2)}) copy-start(bf16[4,1,64,128]{3,2,1,0:T(8,128)(2,1)S(1)} %collective-permute-done.3) | copy-start | bytes 196612
  224.6 2.5 copy-start.32
  224.7 2.5 copy-start.33
  241.3 1.7 copy-start.4
  243.6 0.8 copy-start.35
  245.3 1.8 copy-start.34
  245.3 1.8 copy-start.2
  245.3 2.3 copy-start.21
  247.1 1.3 copy-start.5
  247.2 2.0 copy-start.15
  247.2 2.0 copy-start.40
  249.2 6.3 %copy-start.11 = (bf16[4,16,64,128]{3,2,1,0:T(8,128)(2,1)S(1)}, bf16[4,16,64,128]{3,2,1,0:T(8,128)(2,1)}, u32[]{:S(2)}) copy-start(bf16[4,16,64,128]{3,2,1,0:T(8,128)(2,1)} %copy-done.9) | copy-start | bytes 3145732
  249.2 7.6 %copy-start.17 = (f32[4,16,64,128]{3,2,1,0:T(8,128)S(1)}, f32[4,16,64,128]{3,2,1,0:T(8,128)}, u32[]{:S(2)}) copy-start(f32[4,16,64,128]{3,2,1,0:T(8,128)} %fusion.64) | copy-start | bytes 6291460
  249.2 7.6 %copy-start.18 = (f32[4,16,64,128]{3,2,1,0:T(8,128)S(1)}, f32[4,16,64,128]{3,2,1,0:T(8,128)}, u32[]{:S(2)}) copy-start(f32[4,16,64,128]{3,2,1,0:T(8,128)} %fusion.67) | copy-start | bytes 6291460
  249.2 7.6 %copy-start.19 = (f32[4,16,64,128]{3,2,1,0:T(8,128)S(1)}, f32[4,16,64,128]{3,2,1,0:T(8,128)}, u32[]{:S(2)}) copy-start(f32[4,16,64,128]{3,2,1,0:T(8,128)} %fusion.70) | copy-start | bytes 6291460
  249.2 7.6 %copy-start.20 = (f32[4,16,64,128]{3,2,1,0:T(8,128)S(1)}, f32[4,16,64,128]{3,2,1,0:T(8,128)}, u32[]{:S(2)}) copy-start(f32[4,16,64,128]{3,2,1,0:T(8,128)} %fusion.73) | copy-start | bytes 6291460
  255.5 0.8 copy-start.31
  255.5 1.7 copy-start.16
  256.3 1.4 copy-start.8
  256.3 2.1 copy-start.14
Sparse Core Ops, SparseCore 0:
  36.6 77.6 all-gather.4
  117.0 71.6 all-gather.6
  245.5 132.1 all-reduce.6
where the time goes:
time: 390 us; the launch traced here: 388 us
  waiting for transfers between devices  194 us (50%)
  matrix products  58.3 us (15%)
  other arithmetic  57.3 us (15%)
  local copies, waits for them, and re-layouts  23.2 us (6%)
  blocking collectives  21.1 us (5%)
  starting transfers between devices  18.8 us (5%)
  between operations  14.5 us (4%)
    psum x1, waiting for transfers between devices, shards(): in_summed, out_summed = lax.psum((in_partial, out_partial), ('tm', 'tile'))  117 us
    all_gather x1, waiting for transfers between devices, shards(): lax.all_gather(outflow[None], 'tm', axis=0, tiled=True)  59.1 us
    dot_general x36, matrix products, convolve(): jnp.dot(piece, weight[row_off, col_off], preferred_element_type=jnp.float32)  48.9 us
    all_gather x1, blocking collectives, shards(): lax.all_gather(whole_decay[None], 'tm', axis=0, tiled=True)  21.1 us
    all_gather x1, waiting for transfers between devices, shards(): lax.all_gather(local_states[-1][None], 'tm', axis=0, tiled=True)  16.3 us
    dynamic_update_slice x8, other arithmetic, shards(): _, local_states = lax.scan(advance, blank, (decay, drive))  16.2 us
    ppermute x4, starting transfers between devices, extended(): lax.ppermute(lax.slice_in_dim(block, block.shape[dim] - width, None, axis...  13.2 us
    select_n x8, other arithmetic, forward_fold(): return jnp.where(step < place, totals[step] * carry + ends[step], carry)  11.9 us
  transfers between devices with their start and end apart: 11, of which 5 were waited for; matrix products, arithmetic and copies ran while one was open for 17% of the time, Pallas kernels for 0%

commit v1 on v0

v1 whole, which is shorter than its diff:
```python
import functools
import math

import jax
import jax.numpy as jnp
from jax import lax
from jax.experimental import pallas as pl
from jax.experimental.pallas import tpu as pltpu
from jax.sharding import PartitionSpec as P

F32 = jnp.float32
BF16 = jnp.bfloat16
VMEM_LIMIT = 40 * 1024 * 1024


def fill_pairs(pairs, field, top, bottom):
    half = field.shape[1] // 2
    ch = field.shape[3]
    pairs[:, 0, :, :ch] = top[:, 0]
    pairs[:, half, :, ch:] = bottom[:, 0]
    for i in range(half):
        pairs[:, i, :, ch:] = field[:, 2 * i]
        pairs[:, i + 1, :, :ch] = field[:, 2 * i + 1]


def fill_pairs_from_pairs(pairs, field, top, bottom):
    half = field.shape[1]
    ch = field.shape[3] // 2
    pairs[:, 0, :, :ch] = top[:, 0]
    pairs[:, half, :, ch:] = bottom[:, 0]
    pairs[:, :half, :, ch:] = field[:, :, :, :ch]
    pairs[:, 1:, :, :ch] = field[:, :, :, ch:]


def column_taps(flat, cols):
    wide = flat.astype(F32)
    count = wide.shape[0]
    col = lax.broadcasted_iota(jnp.int32, wide.shape, 0) % cols
    left = jnp.where(col == 0, 0.0, pltpu.roll(wide, 1, 0)).astype(flat.dtype)
    right = jnp.where(col == cols - 1, 0.0, pltpu.roll(wide, count - 1, 0)).astype(flat.dtype)
    return left, flat, right


def fill_weights(blocks, weight, flip):
    ch = weight.shape[2]
    zero = jnp.zeros((ch, ch), weight.dtype)
    for j in range(3):
        for b in range(2):
            for k in range(2):
                for n in range(2):
                    tap = 2 * b + k - n
                    ok = 0 <= tap <= 2
                    if flip:
                        value = weight[2 - tap, 2 - j] if ok else zero
                        blocks[j, b, n * ch : (n + 1) * ch, k * ch : (k + 1) * ch] = value
                    else:
                        value = weight[tap, j] if ok else zero
                        blocks[j, b, k * ch : (k + 1) * ch, n * ch : (n + 1) * ch] = value


def conv_pairs(taps, blocks, rows_out, cols, flip):
    dims = (((1,), (1,)), ((), ())) if flip else (((1,), (0,)), ((), ()))
    total = None
    for j in range(3):
        for b in range(2):
            part = lax.dot_general(
                taps[j][b * cols : b * cols + rows_out],
                blocks[j, b],
                dims,
                preferred_element_type=F32,
            )
            total = part if total is None else total + part
    return total


def drive_kernel(field, top, bottom, weight, rate, local, end, taps_out, pairs, blocks, *, flip):
    times, rows, cols, ch = field.shape
    half = rows // 2
    fill_weights(blocks, weight, flip)
    fill_pairs(pairs, field, top, bottom)
    carry = None
    for step in range(times):
        t = times - 1 - step if flip else step
        taps = column_taps(pairs[t].reshape((half + 1) * cols, 2 * ch), cols)
        for j in range(3):
            taps_out[j, t] = taps[j]
        value = conv_pairs(taps, blocks, half * cols, cols, flip)
        d = rate[t : t + 1, :]
        if flip:
            value = value if carry is None else value + carry
            carry = d * value
        else:
            value = (1.0 - d) * value
            value = value if carry is None else d * carry + value
            carry = value
        local[t] = value
    end[...] = carry


def drive_call(field, top, bottom, weight, rate, flip):
    times, rows, cols, ch = field.shape
    half = rows // 2
    return pl.pallas_call(
        functools.partial(drive_kernel, flip=flip),
        out_shape=(
            jax.ShapeDtypeStruct((times, half * cols, 2 * ch), F32),
            jax.ShapeDtypeStruct((half * cols, 2 * ch), F32),
            jax.ShapeDtypeStruct((3, times, (half + 1) * cols, 2 * ch), BF16),
        ),
        scratch_shapes=[
            pltpu.VMEM((times, half + 1, cols, 2 * ch), BF16),
            pltpu.VMEM((3, 2, 2 * ch, 2 * ch), BF16),
        ],
        compiler_params=pltpu.CompilerParams(vmem_limit_bytes=VMEM_LIMIT),
        cost_estimate=pl.CostEstimate(
            flops=times * rows * cols * ch * ch * 24, bytes_accessed=6 << 20, transcendentals=0
        ),
        name="drive_adjoint" if flip else "drive_state",
    )(field, top, bottom, weight, rate)


def grads_kernel(local, incoming, reach, gain, taps, rounded, grads, *, flip):
    times, count, width = local.shape
    ch = width // 2
    cols = taps.shape[2] - count
    add = incoming[...]
    turned = []
    for t in range(times):
        value = local[t] + reach[t : t + 1, :] * add
        if not flip:
            value = gain[t : t + 1, :] * value
        value = value.astype(BF16)
        rounded[t] = value
        turned.append(value.T)
    for j in range(3):
        blocks = []
        for b in range(2):
            total = None
            for t in range(times):
                part = jnp.dot(
                    turned[t], taps[j, t, b * cols : b * cols + count], preferred_element_type=F32
                )
                total = part if total is None else total + part
            blocks.append(total)
        for tap in range(3):
            total = None
            for b in range(2):
                for c in range(2):
                    a = 2 * b + c - tap
                    if a in (0, 1):
                        part = blocks[b][a * ch : (a + 1) * ch, c * ch : (c + 1) * ch]
                        total = part if total is None else total + part
            if flip:
                grads[2 - tap, 2 - j] = total
            else:
                grads[tap, j] = total.T


def grads_call(local, incoming, reach, gain, taps, flip):
    times, count, width = local.shape
    ch = width // 2
    return pl.pallas_call(
        functools.partial(grads_kernel, flip=flip),
        out_shape=(
            jax.ShapeDtypeStruct((times, count, width), BF16),
            jax.ShapeDtypeStruct((3, 3, ch, ch), F32),
        ),
        compiler_params=pltpu.CompilerParams(vmem_limit_bytes=VMEM_LIMIT),
        cost_estimate=pl.CostEstimate(
            flops=times * count * ch * ch * 48, bytes_accessed=6 << 20, transcendentals=0
        ),
        name="grads_out" if flip else "grads_in",
    )(local, incoming, reach, gain, taps)


def output_kernel(field, top, bottom, weight, skip, direct, out, pairs, blocks, *, flip):
    times, half, cols, width = field.shape
    ch = width // 2
    fill_weights(blocks, weight, flip)
    fill_pairs_from_pairs(pairs, field, top, bottom)
    gain = skip[...]
    for t in range(times):
        taps = column_taps(pairs[t].reshape((half + 1) * cols, width), cols)
        value = conv_pairs(taps, blocks, half * cols, cols, flip).reshape(half, cols, width)
        for i in range(half):
            for c in range(2):
                base = gain * direct[t, 2 * i + c].astype(F32)
                out[t, 2 * i + c] = (value[i, :, c * ch : (c + 1) * ch] + base).astype(BF16)


def output_call(field, top, bottom, weight, skip, direct, flip):
    times, half, cols, width = field.shape
    ch = width // 2
    return pl.pallas_call(
        functools.partial(output_kernel, flip=flip),
        out_shape=jax.ShapeDtypeStruct(direct.shape, BF16),
        scratch_shapes=[
            pltpu.VMEM((times, half + 1, cols, width), BF16),
            pltpu.VMEM((3, 2, width, width), BF16),
        ],
        compiler_params=pltpu.CompilerParams(vmem_limit_bytes=VMEM_LIMIT),
        cost_estimate=pl.CostEstimate(
            flops=times * half * cols * ch * ch * 48, bytes_accessed=4 << 20, transcendentals=0
        ),
        name="grad_frames" if flip else "output",
    )(field, top, bottom, weight, skip, direct)


def neighbours(axis, low, high):
    count = lax.axis_size(axis)
    forward = [(i, i + 1) for i in range(count - 1)]
    backward = [(i + 1, i) for i in range(count - 1)]
    return lax.ppermute(low, axis, forward), lax.ppermute(high, axis, backward)


def swap(value, axis, bit):
    count = lax.axis_size(axis)
    return lax.ppermute(value, axis, [(i, i ^ bit) for i in range(count)])


def shift(value, axis, by):
    count = lax.axis_size(axis)
    return lax.ppermute(value, axis, [(i, i + by) for i in range(count) if 0 <= i + by < count])


def carry_over(end, total, axis, sign):
    count = lax.axis_size(axis)
    place = lax.axis_index(axis)
    odd = place % 2 == 1
    half = end.shape[0] // 2
    width = end.shape[1]

    def message(value, decay):
        return jnp.concatenate([value, jnp.broadcast_to(decay, (8, width))], 0)

    low, high = end[:half], end[half:]
    mine = jnp.where(odd, high, low)
    got = swap(message(jnp.where(odd, low, high), total), axis, 1)
    theirs, their_total = got[:half], got[half : half + 1]
    late = odd if sign > 0 else jnp.logical_not(odd)
    first = jnp.where(late, theirs, mine)
    first_total = jnp.where(late, their_total, total)
    second = jnp.where(late, mine, theirs)
    second_total = jnp.where(late, total, their_total)
    pair = second_total * first + second
    pair_total = first_total * second_total

    before = jnp.zeros_like(pair)
    before_total = jnp.ones_like(pair_total)
    reached = 1
    while reached < count // 2:
        upto = pair + pair_total * before
        got = shift(message(upto, pair_total * before_total), axis, 2 * reached * sign)
        before = before + before_total * got[:half]
        before_total = before_total * got[half : half + 1]
        reached *= 2
    inner = first + first_total * before
    own = jnp.where(late, inner, before)
    other = swap(jnp.where(late, before, inner), axis, 1)
    return jnp.concatenate([jnp.where(odd, other, own), jnp.where(odd, own, other)], 0)


def summed(in_part, out_part):
    ch_in, ch_out = in_part.shape[2:]
    core = lax.axis_index("tile") % 2 == 1
    flat_in = in_part.reshape(-1, ch_out)
    flat_out = out_part.reshape(-1, ch_out)
    got = swap(jnp.where(core, flat_in, flat_out), "tile", 1)
    value = jnp.where(core, flat_out, flat_in) + got
    steps = []
    bit = 1
    while bit < lax.axis_size("tm"):
        steps.append(("tm", bit))
        bit *= 2
    bit = 2
    while bit < lax.axis_size("tile"):
        steps.insert(1, ("tile", bit))
        bit *= 2
    for axis, bit in steps:
        half = value.shape[0] // 2
        high = (lax.axis_index(axis) // bit) % 2 == 1
        low_part, high_part = value[:half], value[half:]
        got = swap(jnp.where(high, low_part, high_part), axis, bit)
        value = jnp.where(high, high_part, low_part) + got
    for axis, bit in reversed(steps):
        high = (lax.axis_index(axis) // bit) % 2 == 1
        got = swap(value, axis, bit)
        value = jnp.concatenate([jnp.where(high, got, value), jnp.where(high, value, got)], 0)
    got = swap(value, "tile", 1)
    shape = in_part.shape
    return (
        jnp.where(core, got, value).reshape(shape),
        jnp.where(core, value, got).reshape(shape),
    )


def shards(frames, cotangent, w_in, w_out, skip, log_decay):
    times, rows, cols, ch = frames.shape
    half = rows // 2
    decay = jnp.exp(log_decay)
    wide = jnp.concatenate([decay, decay], 1)
    cumulative = jnp.cumsum(log_decay, axis=0)
    reach = jnp.exp(cumulative)
    tail = jnp.exp(cumulative[-1][None, :] - cumulative)
    reach = jnp.concatenate([reach, reach], 1)
    tail = jnp.concatenate([tail, tail], 1)
    total = reach[-1:]

    frames_top, frames_bottom = neighbours("tile", frames[:, -1:], frames[:, :1])
    cot_top, cot_bottom = neighbours("tile", cotangent[:, -1:], cotangent[:, :1])

    states, state_end, frame_taps = drive_call(
        frames, frames_top, frames_bottom, w_in, wide, False
    )
    adjoints, adjoint_end, cot_taps = drive_call(
        cotangent, cot_top, cot_bottom, w_out, wide, True
    )
    state_in = carry_over(state_end, total, "tm", 1)
    adjoint_in = carry_over(adjoint_end, total, "tm", -1)

    states_bf, out_part = grads_call(states, state_in, reach, reach, cot_taps, True)
    inflow_bf, in_part = grads_call(adjoints, adjoint_in, tail, 1.0 - wide, frame_taps, False)

    factor = 1.0 / math.sqrt(
        times * lax.axis_size("tm") * rows * lax.axis_size("tile") * cols
    )
    in_sum, out_sum = summed(in_part, out_part)

    states_bf = states_bf.reshape(times, half, cols, 2 * ch)
    inflow_bf = inflow_bf.reshape(times, half, cols, 2 * ch)
    gain = skip[None, :]
    states_top, states_bottom = neighbours(
        "tile", states_bf[:, -1:, :, ch:], states_bf[:, :1, :, :ch]
    )
    inflow_top, inflow_bottom = neighbours(
        "tile", inflow_bf[:, -1:, :, ch:], inflow_bf[:, :1, :, :ch]
    )
    output = output_call(states_bf, states_top, states_bottom, w_out, gain, frames, False)
    grad_frames = output_call(
        inflow_bf, inflow_top, inflow_bottom, w_in, gain, cotangent, True
    )
    return (output, grad_frames, in_sum * factor, out_sum * factor)


def solution(mesh):
    placed = (
        P("tm", "tile", None, None),
        P("tm", "tile", None, None),
        P(),
        P(),
        P(),
        P("tm", None),
    )
    return jax.shard_map(
        shards,
        mesh=mesh,
        in_specs=placed,
        out_specs=(P("tm", "tile", None, None), P("tm", "tile", None, None), P(), P()),
        check_vma=False,
    )
```

time: 390 us -> 171 us (0.44)
  waiting for transfers between devices: 194 us -> 71.1 us
  matrix products: 58.3 us -> 0 us
  other arithmetic: 57.3 us -> 18 us
  starting transfers between devices: 18.8 us -> 48 us
  blocking collectives: 21.1 us -> 0 us
  Pallas kernels: 0 us -> 15.3 us
  between operations: 14.5 us -> 1.25 us
  local copies, waits for them, and re-layouts: 23.2 us -> 15.1 us
    psum x1 -> x0, waiting for transfers between devices: 117 us -> none  [shards(): in_summed, out_summed = lax.psum((in_partial, out_partial), ('tm', 'tile'))]
    all_gather x2 -> x0, waiting for transfers between devices: 75.4 us -> none  [the longest x1 59.1 us: shards(): lax.all_gather(outflow[None], 'tm', axis=0, tiled=True)]
    ppermute x8 -> x26, waiting for transfers between devices: 1.73 us -> 71.1 us  [the longest x14 54.2 us: swap(): return lax.ppermute(value, axis, [(i, i ^ bit) for i in range(count)])]
    dot_general x54 -> x0, matrix products: 58.3 us -> none  [the longest x36 48.9 us: convolve(): jnp.dot(piece, weight[row_off, col_off], preferred_element_type=jnp.float32)]
    ppermute x8 -> x26, starting transfers between devices: 18.7 us -> 48 us  [the longest x14 15.7 us: swap(): return lax.ppermute(value, axis, [(i, i ^ bit) for i in range(count)])]
    all_gather x1 -> x0, blocking collectives: 21.1 us -> none  [shards(): lax.all_gather(whole_decay[None], 'tm', axis=0, tiled=True)]
    select_n x16 -> x14, other arithmetic: 22.6 us -> 5.96 us  [the longest x2 2.04 us: carry_over(): other = swap(jnp.where(late, before, inner), axis, 1)]
    dynamic_update_slice x8 -> x0, other arithmetic: 16.2 us -> none  [shards(): _, local_states = lax.scan(advance, blank, (decay, drive))]
  transfers between devices with their start and end apart: 11 -> 26, of which waited for: 5 -> 16; matrix products, arithmetic and copies ran while one was open for 17% -> 6% of each run, Pallas kernels for 0% -> 5%
where the time goes in v1:
time: 171 us; the launch traced here: 169 us
  waiting for transfers between devices  71.1 us (42%)
  starting transfers between devices  48 us (28%)
  other arithmetic  18 us (11%)
  Pallas kernels  15.3 us (9%)
  local copies, waits for them, and re-layouts  15.1 us (9%)
    ppermute x14, waiting for transfers between devices, swap(): return lax.ppermute(value, axis, [(i, i ^ bit) for i in range(count)])  54.2 us
    ppermute x4, waiting for transfers between devices, shift(): lax.ppermute(value, axis, [(i, i + by) for i in range(count) if 0 <= i +...  16.8 us
    ppermute x14, starting transfers between devices, swap(): return lax.ppermute(value, axis, [(i, i ^ bit) for i in range(count)])  15.7 us
    ppermute x4, starting transfers between devices, neighbours(): lax.ppermute(low, axis, forward)  15.5 us
    unnamed x58, local copies, waits for them, and re-layouts  11.9 us
    ppermute x4, starting transfers between devices, shift(): lax.ppermute(value, axis, [(i, i + by) for i in range(count) if 0 <= i +...  11.5 us
    pallas_call x2, Pallas kernels, output_call(): pl.pallas_call(functools.partial(output_kernel, flip=flip), out_shape=jax...  5.95 us
    pallas_call x2, Pallas kernels, drive_call(): pl.pallas_call(functools.partial(drive_kernel, flip=flip), out_shape=(jax...  5.57 us
  transfers between devices with their start and end apart: 26, of which 16 were waited for; matrix products, arithmetic and copies ran while one was open for 6% of the time, Pallas kernels for 5%

profile of v1, /device:TPU:0, one launch (start us, length us, event | category | flops | bytes accessed | tf_op | source)
XLA Modules:
  0.0 168.7 jit_solution(15537307405724357708)
XLA Ops:
  0.6 1.5 fusion.14
  2.2 1.3 collective-permute-start.1
  3.5 3.7 %collective-permute-start = (bf16[4,1,64,128]{3,2,1,0:T(8,128)(2,1)}, bf16[4,1,64,128]{3,2,1,0:T(8,128)(2,1)}, u32[]{:S(2)}, u32[]{:S(2)}) collective-permute-start(bf16[4,1,64,128]{3,2,1,0:T(8,128)(2,1)} %get-tuple-element.51), channel_id=1, source_target_pairs={{0,1},{1,2},{2,3},{4,5},{5,6},{6,7},{8,9},{9,10},{10,11},{12,13},{... | collective-permute-start | bytes 196616 | tf_op jit(solution)/shard_map/ppermute | solution.py:213
  7.1 0.9 fusion.13
  8.0 1.3 collective-permute-start.7
  9.3 4.5 %collective-permute-start.6 = (bf16[4,1,64,128]{3,2,1,0:T(8,128)(2,1)S(1)}, bf16[4,1,64,128]{3,2,1,0:T(8,128)(2,1)S(1)}, u32[]{:S(2)}, u32[]{:S(2)}) collective-permute-start(bf16[4,1,64,128]{3,2,1,0:T(8,128)(2,1)S(1)} %get-tuple-element.49), channel_id=1, source_target_pairs={{0,1},{1,2},{2,3},{4,5},{5,6},{6,7},{8,9},{9,10},{10,11},{12,13},{... | collective-permute-start | bytes 196616 | tf_op jit(solution)/shard_map/ppermute | solution.py:213
  17.1 1.2 copy-done.10
  18.3 1.0 copy-done.14
  19.3 0.8 copy-done.19
  20.1 0.8 copy-done.21
  21.0 2.3 %drive_adjoint.1 = (f32[4,512,256]{2,1,0:T(8,128)S(1)}, f32[512,256]{1,0:T(8,128)S(1)}, bf16[3,4,576,256]{3,2,1,0:T(8,128)(2,1)S(1)}) custom-call(bf16[4,16,64,128]{3,2,1,0:T(8,128)(2,1)S(1)} %copy-done.10, bf16[4,1,64,128]{3,2,1,0:T(8,128)(2,1)S(1)} %copy-done.21, bf16[4,1,64,128]{3,2,1,0:T(8,128)(2,1)S(1)} %copy-done.19, ...), custom_call_target="tpu_custom_call" | custom-call | flops 1610612736 | bytes 6291456 | tf_op jit(solution)/shard_map/drive_adjoint/pallas_call | solution.py:103
  23.3 1.4 copy-done.3
  24.7 3.3 %drive_state.1 = (f32[4,512,256]{2,1,0:T(8,128)S(1)}, f32[512,256]{1,0:T(8,128)S(1)}, bf16[3,4,576,256]{3,2,1,0:T(8,128)(2,1)S(1)}) custom-call(bf16[4,16,64,128]{3,2,1,0:T(8,128)(2,1)S(1)} %copy-done.8, bf16[4,1,64,128]{3,2,1,0:T(8,128)(2,1)} %collective-permute-done.top, bf16[4,1,64,128]{3,2,1,0:T(8,128)(2,1)} %collective-permute-done.1.bottom, ...), custom_call_target="tpu_custom_call" | custom-call | flops 1610612736 | bytes 6291456 | tf_op jit(solution)/shard_map/drive_state/pallas_call | solution.py:103
  28.0 1.8 %copy-done = bf16[3,4,576,256]{3,2,1,0:T(8,128)(2,1)} copy-done((bf16[3,4,576,256]{3,2,1,0:T(8,128)(2,1)}, bf16[3,4,576,256]{3,2,1,0:T(8,128)(2,1)S(1)}, u32[]{:S(2)}) %copy-start) | copy-done | bytes 3538968
  29.7 1.4 copy-done.5
  31.1 0.8 copy-done.2
  32.0 0.8 pad_maximum_fusion.3
  32.9 1.5 collective-permute-start.10
  34.9 6.9 %collective-permute-done.10 = f32[264,256]{1,0:T(8,128)} collective-permute-done((f32[264,256]{1,0:T(8,128)}, f32[264,256]{1,0:T(8,128)}, u32[]{:S(2)}, u32[]{:S(2)}) %collective-permute-start.10) | collective-permute-done | bytes 270368 | tf_op jit(solution)/shard_map/ppermute | solution.py:218
  41.8 5.8 %collective-permute-done.2 = f32[264,256]{1,0:T(8,128)} collective-permute-done((f32[264,256]{1,0:T(8,128)}, f32[264,256]{1,0:T(8,128)}, u32[]{:S(2)}, u32[]{:S(2)}) %collective-permute-start.2) | collective-permute-done | bytes 270368 | tf_op jit(solution)/shard_map/ppermute | solution.py:218
  47.6 1.3 fusion.8
  48.9 1.2 broadcast_add_fusion.1
  50.1 3.5 %collective-permute-start.3 = (f32[264,256]{1,0:T(8,128)S(1)}, f32[264,256]{1,0:T(8,128)S(1)}, u32[]{:S(2)}, u32[]{:S(2)}) collective-permute-start(f32[264,256]{1,0:T(8,128)S(1)} %pad_maximum_fusion.6), channel_id=1, source_target_pairs={{0,8},{4,12},{8,16},{12,20},{16,24},{20,28},{1,9},{5,13},{9,17},{1... | collective-permute-start | bytes 811016 | tf_op jit(solution)/shard_map/ppermute | solution.py:223
  53.6 1.9 %broadcast_add_fusion = (f32[256,256]{1,0:T(8,128)S(1)}, f32[256,256]{1,0:T(8,128)S(1)}, f32[256,256]{1,0:T(8,128)}) fusion(f32[256]{0:T(256)S(1)} %broadcast_multiply_fusion, f32[264,256]{1,0:T(8,128)} %collective-permute-done.10, f32[512,256]{1,0:T(8,128)} %copy-done.7, pred[]{:T(512)S(6)} %eq.33, pred[]{:T(512)S(6)} %not.3, f32[256]{0:T(256)S(1)} %bitcast.45), kind=kLoop, calls=%fused_computation.42 | loop fusion | flops 393216 | bytes 1574914 | tf_op jit(solution)/shard_map/add | solution.py:252
  55.5 1.3 collective-permute-start.11
  56.8 3.2 %collective-permute-done.3 = f32[264,256]{1,0:T(8,128)S(1)} collective-permute-done((f32[264,256]{1,0:T(8,128)S(1)}, f32[264,256]{1,0:T(8,128)S(1)}, u32[]{:S(2)}, u32[]{:S(2)}) %collective-permute-start.3) | collective-permute-done | bytes 270368 | tf_op jit(solution)/shard_map/ppermute | solution.py:223
  60.1 5.4 %collective-permute-start.4 = (f32[264,256]{1,0:T(8,128)S(1)}, f32[264,256]{1,0:T(8,128)S(1)}, u32[]{:S(2)}, u32[]{:S(2)}) collective-permute-start(f32[264,256]{1,0:T(8,128)S(1)} %pad_maximum_fusion.7), channel_id=1, source_target_pairs={{0,16},{4,20},{8,24},{12,28},{1,17},{5,21},{9,25},{13,29},{2,18},{... | collective-permute-start | bytes 811016 | tf_op jit(solution)/shard_map/ppermute | solution.py:223
  67.5 1.3 collective-permute-start.12
  68.7 2.5 %collective-permute-done.4 = f32[264,256]{1,0:T(8,128)S(1)} collective-permute-done((f32[264,256]{1,0:T(8,128)S(1)}, f32[264,256]{1,0:T(8,128)S(1)}, u32[]{:S(2)}, u32[]{:S(2)}) %collective-permute-start.4) | collective-permute-done | bytes 270368 | tf_op jit(solution)/shard_map/ppermute | solution.py:223
  71.2 0.9 fusion.5
  72.1 1.5 collective-permute-start.5
  73.6 10.6 %collective-permute-done.12 = f32[264,256]{1,0:T(8,128)} collective-permute-done((f32[264,256]{1,0:T(8,128)}, f32[264,256]{1,0:T(8,128)}, u32[]{:S(2)}, u32[]{:S(2)}) %collective-permute-start.12) | collective-permute-done | bytes 270368 | tf_op jit(solution)/shard_map/ppermute | solution.py:223
  84.2 1.2 fusion.3
  85.4 1.5 collective-permute-start.13
  86.9 1.2 broadcast_select_fusion.7
  88.1 4.5 %collective-permute-done.13 = f32[256,256]{1,0:T(8,128)S(1)} collective-permute-done((f32[256,256]{1,0:T(8,128)S(1)}, f32[256,256]{1,0:T(8,128)S(1)}, u32[]{:S(2)}, u32[]{:S(2)}) %collective-permute-start.13) | collective-permute-done | bytes 262176 | tf_op jit(solution)/shard_map/ppermute | solution.py:218
  93.4 1.8 %grads_out.1 = (bf16[4,512,256]{2,1,0:T(8,128)(2,1)S(1)}, f32[3,3,128,128]{3,2,1,0:T(8,128)S(1)}) custom-call(f32[4,512,256]{2,1,0:T(8,128)S(1)} %copy-done.6, f32[512,256]{1,0:T(8,128)S(1)} %pad_maximum_fusion.1.incoming, f32[4,256]{1,0:T(4,128)S(1)} %get-tuple-element.77.reach.gain, f32[4,256]{1,0:T(4,128)S(1)} %get-tuple-element.77.reach.gain, ...), custom_call_target="tpu_custom_call" | custom-call | flops 1610612736 | bytes 6291456 | tf_op jit(solution)/shard_map/grads_out/pallas_call | solution.py:162
  96.0 1.9 %grads_in.1 = (bf16[4,512,256]{2,1,0:T(8,128)(2,1)S(1)}, f32[3,3,128,128]{3,2,1,0:T(8,128)S(1)}) custom-call(f32[4,512,256]{2,1,0:T(8,128)S(1)} %copy-done.4, f32[512,256]{1,0:T(8,128)S(1)} %pad_maximum_fusion.2.incoming, f32[4,256]{1,0:T(4,128)S(1)} %get-tuple-element.78.reach, f32[4,256]{1,0:T(4,128)S(1)} %get-tuple-element.70.gain, ...), custom_call_target="tpu_custom_call" | custom-call | flops 1610612736 | bytes 6291456 | tf_op jit(solution)/shard_map/grads_in/pallas_call | solution.py:162
  98.1 2.0 %collective-permute-done.16 = f32[1152,128]{1,0:T(8,128)S(1)} collective-permute-done((f32[1152,128]{1,0:T(8,128)S(1)}, f32[1152,128]{1,0:T(8,128)S(1)}, u32[]{:S(2)}, u32[]{:S(2)}) %collective-permute-start.16) | collective-permute-done | bytes 589856 | tf_op jit(solution)/shard_map/ppermute | solution.py:218
  100.2 1.5 collective-permute-start.17
  101.7 7.6 %collective-permute-done.17 = f32[576,128]{1,0:T(8,128)S(1)} collective-permute-done((f32[576,128]{1,0:T(8,128)S(1)}, f32[576,128]{1,0:T(8,128)S(1)}, u32[]{:S(2)}, u32[]{:S(2)}) %collective-permute-start.17) | collective-permute-done | bytes 294944 | tf_op jit(solution)/shard_map/ppermute | solution.py:218
  109.3 0.8 select_add_fusion
  110.1 1.8 %slice_select_fusion.7 = f32[288,128]{1,0:T(8,128)} fusion(f32[576,128]{1,0:T(8,128)} %select_add_fusion, pred[]{:T(512)S(6)} %eq.35), kind=kLoop, calls=%fused_computation.41 | loop fusion | flops 36864 | bytes 442369 | tf_op jit(solution)/shard_map/jit(_where)/select_n | solution.py:283
  111.8 5.5 %collective-permute-done.18 = f32[288,128]{1,0:T(8,128)} collective-permute-done((f32[288,128]{1,0:T(8,128)}, f32[288,128]{1,0:T(8,128)}, u32[]{:S(2)}, u32[]{:S(2)}) %collective-permute-start.18) | collective-permute-done | bytes 147488 | tf_op jit(solution)/shard_map/ppermute | solution.py:218
  117.3 1.1 select_add_fusion.3
  119.1 0.8 collective-permute-start.19
  119.9 3.7 %collective-permute-done.19 = f32[144,128]{1,0:T(8,128)} collective-permute-done((f32[144,128]{1,0:T(8,128)S(1)}, f32[144,128]{1,0:T(8,128)}, u32[]{:S(2)}, u32[]{:S(2)}) %collective-permute-start.19) | collective-permute-done | bytes 73760 | tf_op jit(solution)/shard_map/ppermute | solution.py:218
  123.6 1.0 select_add_fusion.4
  124.6 2.2 %collective-permute-start.20 = (f32[72,128]{1,0:T(8,128)S(1)}, f32[72,128]{1,0:T(8,128)S(1)}, u32[]{:S(2)}, u32[]{:S(2)}) collective-permute-start(f32[72,128]{1,0:T(8,128)S(1)} %slice_select_fusion.9), channel_id=1, source_target_pairs={{0,16},{4,20},{8,24},{12,28},{16,0},{20,4},{24,8},{28,12},{1,17},{... | collective-permute-start | bytes 110600 | tf_op jit(solution)/shard_map/ppermute | solution.py:218
  126.8 2.9 %collective-permute-done.20 = f32[72,128]{1,0:T(8,128)S(1)} collective-permute-done((f32[72,128]{1,0:T(8,128)S(1)}, f32[72,128]{1,0:T(8,128)S(1)}, u32[]{:S(2)}, u32[]{:S(2)}) %collective-permute-start.20) | collective-permute-done | bytes 36896 | tf_op jit(solution)/shard_map/ppermute | solution.py:218
  129.7 2.3 %collective-permute-start.21 = (f32[72,128]{1,0:T(8,128)S(1)}, f32[72,128]{1,0:T(8,128)S(1)}, u32[]{:S(2)}, u32[]{:S(2)}) collective-permute-start(f32[72,128]{1,0:T(8,128)S(1)} %select_add_fusion.5), channel_id=1, source_target_pairs={{0,16},{4,20},{8,24},{12,28},{16,0},{20,4},{24,8},{28,12},{1,17},{... | collective-permute-start | bytes 110600 | tf_op jit(solution)/shard_map/ppermute | solution.py:218
  132.0 2.6 %collective-permute-done.21 = f32[72,128]{1,0:T(8,128)S(1)} collective-permute-done((f32[72,128]{1,0:T(8,128)S(1)}, f32[72,128]{1,0:T(8,128)S(1)}, u32[]{:S(2)}, u32[]{:S(2)}) %collective-permute-start.21) | collective-permute-done | bytes 36896 | tf_op jit(solution)/shard_map/ppermute | solution.py:218
  134.7 1.9 %collective-permute-start.22 = (f32[144,128]{1,0:T(8,128)S(1)}, f32[144,128]{1,0:T(8,128)S(1)}, u32[]{:S(2)}, u32[]{:S(2)}) collective-permute-start(f32[144,128]{1,0:T(8,128)S(1)} %pad_maximum_fusion.11), channel_id=1, source_target_pairs={{0,8},{4,12},{8,0},{12,4},{16,24},{20,28},{24,16},{28,20},{1,9},{5... | collective-permute-start | bytes 221192 | tf_op jit(solution)/shard_map/ppermute | solution.py:218
  136.6 2.5 %collective-permute-done.22 = f32[144,128]{1,0:T(8,128)S(1)} collective-permute-done((f32[144,128]{1,0:T(8,128)S(1)}, f32[144,128]{1,0:T(8,128)S(1)}, u32[]{:S(2)}, u32[]{:S(2)}) %collective-permute-start.22) | collective-permute-done | bytes 73760 | tf_op jit(solution)/shard_map/ppermute | solution.py:218
  139.3 5.0 %collective-permute-done.23 = f32[288,128]{1,0:T(8,128)S(1)} collective-permute-done((f32[288,128]{1,0:T(8,128)S(1)}, f32[288,128]{1,0:T(8,128)S(1)}, u32[]{:S(2)}, u32[]{:S(2)}) %collective-permute-start.23) | collective-permute-done | bytes 147488 | tf_op jit(solution)/shard_map/ppermute | solution.py:218
  144.4 1.5 collective-permute-start.24
  145.9 5.3 %collective-permute-done.24 = f32[576,128]{1,0:T(8,128)S(1)} collective-permute-done((f32[576,128]{1,0:T(8,128)S(1)}, f32[576,128]{1,0:T(8,128)S(1)}, u32[]{:S(2)}, u32[]{:S(2)}) %collective-permute-start.24) | collective-permute-done | bytes 294944 | tf_op jit(solution)/shard_map/ppermute | solution.py:218
  151.4 1.4 collective-permute-start.9
  152.8 3.0 %collective-permute-start.8 = (bf16[4,1,64,128]{3,2,1,0:T(8,128)(2,1)S(1)}, bf16[4,1,64,128]{3,2,1,0:T(8,128)(2,1)S(1)}, u32[]{:S(2)}, u32[]{:S(2)}) collective-permute-start(bf16[4,1,64,128]{3,2,1,0:T(8,128)(2,1)S(1)} %get-tuple-element.47), channel_id=1, source_target_pairs={{0,1},{1,2},{2,3},{4,5},{5,6},{6,7},{8,9},{9,10},{10,11},{12,13},{... | collective-permute-start | bytes 196616 | tf_op jit(solution)/shard_map/ppermute | solution.py:213
  155.9 1.3 collective-permute-start.15
  157.2 4.3 %collective-permute-start.14 = (bf16[4,1,64,128]{3,2,1,0:T(8,128)(2,1)S(1)}, bf16[4,1,64,128]{3,2,1,0:T(8,128)(2,1)S(1)}, u32[]{:S(2)}, u32[]{:S(2)}) collective-permute-start(bf16[4,1,64,128]{3,2,1,0:T(8,128)(2,1)S(1)} %get-tuple-element.45), channel_id=1, source_target_pairs={{0,1},{1,2},{2,3},{4,5},{5,6},{6,7},{8,9},{9,10},{10,11},{12,13},{... | collective-permute-start | bytes 196616 | tf_op jit(solution)/shard_map/ppermute | solution.py:213
  161.6 3.0 %output.1 = bf16[4,16,64,128]{3,2,1,0:T(8,128)(2,1)} custom-call(bf16[4,8,64,256]{3,2,1,0:T(8,128)(2,1)S(1)} %bitcast.24, bf16[4,1,64,128]{3,2,1,0:T(8,128)(2,1)S(1)} %collective-permute-done.8.top, bf16[4,1,64,128]{3,2,1,0:T(8,128)(2,1)S(1)} %collective-permute-done.9.bottom, bf16[3,3,128,128]{3,2,1,0:T(8,128)(2,1)S(1)} %copy-done.15, ...), custom_call_target="tpu_custom_call" | custom-call | flops 1610612736 | bytes 4194304 | tf_op jit(solution)/shard_map/output/pallas_call | solution.py:194
  164.6 3.0 %grad_frames.1 = bf16[4,16,64,128]{3,2,1,0:T(8,128)(2,1)} custom-call(bf16[4,8,64,256]{3,2,1,0:T(8,128)(2,1)S(1)} %bitcast.22, bf16[4,1,64,128]{3,2,1,0:T(8,128)(2,1)S(1)} %collective-permute-done.14.top, bf16[4,1,64,128]{3,2,1,0:T(8,128)(2,1)S(1)} %collective-permute-done.15.bottom, bf16[3,3,128,128]{3,2,1,0:T(8,128)(2,1)S(1)} %copy-done.17, ...), custom_call_target="tpu_custom_call" | custom-call | flops 1610612736 | bytes 4194304 | tf_op jit(solution)/shard_map/grad_frames/pallas_call | solution.py:194
  167.6 1.1 select_multiply_fusion
  (108 shorter events, 8.9 us)
Async XLA Ops:
  2.2 22.5 %collective-permute-start.1 = (bf16[4,1,64,128]{3,2,1,0:T(8,128)(2,1)}, bf16[4,1,64,128]{3,2,1,0:T(8,128)(2,1)}, u32[]{:S(2)}, u32[]{:S(2)}) collective-permute-start(bf16[4,1,64,128]{3,2,1,0:T(8,128)(2,1)} %get-tuple-element.50), channel_id=1, source_target_pairs={{1,0},{2,1},{3,2},{5,4},{6,5},{7,6},{9,8},{10,9},{11,10},{13,12},{... | collective-permute-start | bytes 196616 | tf_op jit(solution)/shard_map/ppermute | solution.py:213
  3.5 21.2 %collective-permute-start = (bf16[4,1,64,128]{3,2,1,0:T(8,128)(2,1)}, bf16[4,1,64,128]{3,2,1,0:T(8,128)(2,1)}, u32[]{:S(2)}, u32[]{:S(2)}) collective-permute-start(bf16[4,1,64,128]{3,2,1,0:T(8,128)(2,1)} %get-tuple-element.51), channel_id=1, source_target_pairs={{0,1},{1,2},{2,3},{4,5},{5,6},{6,7},{8,9},{9,10},{10,11},{12,13},{... | collective-permute-start | bytes 196616 | tf_op jit(solution)/shard_map/ppermute | solution.py:213
  8.0 7.8 %collective-permute-start.7 = (bf16[4,1,64,128]{3,2,1,0:T(8,128)(2,1)S(1)}, bf16[4,1,64,128]{3,2,1,0:T(8,128)(2,1)S(1)}, u32[]{:S(2)}, u32[]{:S(2)}) collective-permute-start(bf16[4,1,64,128]{3,2,1,0:T(8,128)(2,1)S(1)} %get-tuple-element.48), channel_id=1, source_target_pairs={{1,0},{2,1},{3,2},{5,4},{6,5},{7,6},{9,8},{10,9},{11,10},{13,12},{... | collective-permute-start | bytes 196616 | tf_op jit(solution)/shard_map/ppermute | solution.py:213
  9.3 7.2 %collective-permute-start.6 = (bf16[4,1,64,128]{3,2,1,0:T(8,128)(2,1)S(1)}, bf16[4,1,64,128]{3,2,1,0:T(8,128)(2,1)S(1)}, u32[]{:S(2)}, u32[]{:S(2)}) collective-permute-start(bf16[4,1,64,128]{3,2,1,0:T(8,128)(2,1)S(1)} %get-tuple-element.49), channel_id=1, source_target_pairs={{0,1},{1,2},{2,3},{4,5},{5,6},{6,7},{8,9},{9,10},{10,11},{12,13},{... | collective-permute-start | bytes 196616 | tf_op jit(solution)/shard_map/ppermute | solution.py:213
  15.2 9.4 %copy-start.8 = (bf16[4,16,64,128]{3,2,1,0:T(8,128)(2,1)S(1)}, bf16[4,16,64,128]{3,2,1,0:T(8,128)(2,1)}, u32[]{:S(2)}) copy-start(bf16[4,16,64,128]{3,2,1,0:T(8,128)(2,1)} %direct.2) | copy-start | bytes 3145732
  15.8 0.6 copy-start.18
  16.5 0.6 copy-start.20
  17.1 1.2 copy-start.10
  18.3 1.0 copy-start.14
  19.3 0.8 copy-start.19
  20.1 0.8 copy-start.21
  21.0 3.7 %copy-start.16 = (bf16[3,3,128,128]{3,2,1,0:T(8,128)(2,1)S(1)}, bf16[3,3,128,128]{3,2,1,0:T(8,128)(2,1)}, u32[]{:S(2)}) copy-start(bf16[3,3,128,128]{3,2,1,0:T(8,128)(2,1)} %weight.7) | copy-start | bytes 884740
  23.3 1.4 copy-start.3
  24.6 7.3 %copy-start.7 = (f32[512,256]{1,0:T(8,128)}, f32[512,256]{1,0:T(8,128)S(1)}, u32[]{:S(2)}) copy-start(f32[512,256]{1,0:T(8,128)S(1)} %get-tuple-element.19) | copy-start | bytes 1572868
  28.0 1.8 %copy-start = (bf16[3,4,576,256]{3,2,1,0:T(8,128)(2,1)}, bf16[3,4,576,256]{3,2,1,0:T(8,128)(2,1)S(1)}, u32[]{:S(2)}) copy-start(bf16[3,4,576,256]{3,2,1,0:T(8,128)(2,1)S(1)} %get-tuple-element.20.taps) | copy-start | bytes 10616836
  29.7 1.4 copy-start.5
  31.1 0.8 copy-start.2
  32.9 8.9 %collective-permute-start.10 = (f32[264,256]{1,0:T(8,128)}, f32[264,256]{1,0:T(8,128)}, u32[]{:S(2)}, u32[]{:S(2)}) collective-permute-start(f32[264,256]{1,0:T(8,128)} %get-tuple-element.68), channel_id=1, source_target_pairs={{0,4},{4,0},{8,12},{12,8},{16,20},{20,16},{24,28},{28,24},{1,5},{5... | collective-permute-start | bytes 811016 | tf_op jit(solution)/shard_map/ppermute | solution.py:218
  34.3 13.3 %collective-permute-start.2 = (f32[264,256]{1,0:T(8,128)}, f32[264,256]{1,0:T(8,128)}, u32[]{:S(2)}, u32[]{:S(2)}) collective-permute-start(f32[264,256]{1,0:T(8,128)} %get-tuple-element.69), channel_id=1, source_target_pairs={{0,4},{4,0},{8,12},{12,8},{16,20},{20,16},{24,28},{28,24},{1,5},{5... | collective-permute-start | bytes 811016 | tf_op jit(solution)/shard_map/ppermute | solution.py:218
  48.9 23.2 %copy-start.27 = (f32[1,256]{1,0:T(1,128)}, f32[1,256]{1,0:T(1,128)S(1)}, u32[]{:S(2)}) copy-start(f32[1,256]{1,0:T(1,128)S(1)} %get-tuple-element.76) | copy-start | bytes 3076
  50.1 23.5 %copy-start.24 = (f32[256,256]{1,0:T(8,128)}, f32[256,256]{1,0:T(8,128)S(1)}, u32[]{:S(2)}) copy-start(f32[256,256]{1,0:T(8,128)S(1)} %get-tuple-element.36) | copy-start | bytes 786436
  50.1 23.5 %copy-start.28 = (f32[4,128]{1,0:T(4,128)S(1)}, f32[4,128]{1,0:T(4,128)}, u32[]{:S(2)}) copy-start(f32[4,128]{1,0:T(4,128)} %get-tuple-element.72) | copy-start | bytes 6148
  50.1 9.9 %collective-permute-start.3 = (f32[264,256]{1,0:T(8,128)S(1)}, f32[264,256]{1,0:T(8,128)S(1)}, u32[]{:S(2)}, u32[]{:S(2)}) collective-permute-start(f32[264,256]{1,0:T(8,128)S(1)} %pad_maximum_fusion.6), channel_id=1, source_target_pairs={{0,8},{4,12},{8,16},{12,20},{16,24},{20,28},{1,9},{5,13},{9,17},{1... | collective-permute-start | bytes 811016 | tf_op jit(solution)/shard_map/ppermute | solution.py:223
  55.5 10.6 %collective-permute-start.11 = (f32[264,256]{1,0:T(8,128)S(1)}, f32[264,256]{1,0:T(8,128)S(1)}, u32[]{:S(2)}, u32[]{:S(2)}) collective-permute-start(f32[264,256]{1,0:T(8,128)S(1)} %pad_maximum_fusion.8), channel_id=1, source_target_pairs={{8,0},{12,4},{16,8},{20,12},{24,16},{28,20},{9,1},{13,5},{17,9},{2... | collective-permute-start | bytes 811016 | tf_op jit(solution)/shard_map/ppermute | solution.py:223
  60.1 11.1 %collective-permute-start.4 = (f32[264,256]{1,0:T(8,128)S(1)}, f32[264,256]{1,0:T(8,128)S(1)}, u32[]{:S(2)}, u32[]{:S(2)}) collective-permute-start(f32[264,256]{1,0:T(8,128)S(1)} %pad_maximum_fusion.7), channel_id=1, source_target_pairs={{0,16},{4,20},{8,24},{12,28},{1,17},{5,21},{9,25},{13,29},{2,18},{... | collective-permute-start | bytes 811016 | tf_op jit(solution)/shard_map/ppermute | solution.py:223
  66.1 1.4 copy-start.26
  67.5 16.7 %collective-permute-start.12 = (f32[264,256]{1,0:T(8,128)}, f32[264,256]{1,0:T(8,128)}, u32[]{:S(2)}, u32[]{:S(2)}) collective-permute-start(f32[264,256]{1,0:T(8,128)} %pad_maximum_fusion.9), channel_id=1, source_target_pairs={{16,0},{20,4},{24,8},{28,12},{17,1},{21,5},{25,9},{29,13},{18,2},{... | collective-permute-start | bytes 811016 | tf_op jit(solution)/shard_map/ppermute | solution.py:223
  72.1 14.8 %collective-permute-start.5 = (f32[256,256]{1,0:T(8,128)}, f32[256,256]{1,0:T(8,128)}, u32[]{:S(2)}, u32[]{:S(2)}) collective-permute-start(f32[256,256]{1,0:T(8,128)} %get-tuple-element.32), channel_id=1, source_target_pairs={{0,4},{4,0},{8,12},{12,8},{16,20},{20,16},{24,28},{28,24},{1,5},{5... | collective-permute-start | bytes 786440 | tf_op jit(solution)/shard_map/ppermute | solution.py:218
  73.6 19.0 %copy-start.23 = (f32[256,256]{1,0:T(8,128)S(1)}, f32[256,256]{1,0:T(8,128)}, u32[]{:S(2)}) copy-start(f32[256,256]{1,0:T(8,128)} %get-tuple-element.28) | copy-start | bytes 786436
  73.6 19.7 %copy-start.6 = (f32[4,512,256]{2,1,0:T(8,128)S(1)}, f32[4,512,256]{2,1,0:T(8,128)}, u32[]{:S(2)}) copy-start(f32[4,512,256]{2,1,0:T(8,128)} %copy-done.5) | copy-start | bytes 6291460
  85.4 7.2 %collective-permute-start.13 = (f32[256,256]{1,0:T(8,128)S(1)}, f32[256,256]{1,0:T(8,128)S(1)}, u32[]{:S(2)}, u32[]{:S(2)}) collective-permute-start(f32[256,256]{1,0:T(8,128)S(1)} %get-tuple-element.24), channel_id=1, source_target_pairs={{0,4},{4,0},{8,12},{12,8},{16,20},{20,16},{24,28},{28,24},{1,5},{5... | collective-permute-start | bytes 786440 | tf_op jit(solution)/shard_map/ppermute | solution.py:218
  93.3 2.0 %copy-start.1 = (bf16[3,4,576,256]{3,2,1,0:T(8,128)(2,1)S(1)}, bf16[3,4,576,256]{3,2,1,0:T(8,128)(2,1)}, u32[]{:S(2)}) copy-start(bf16[3,4,576,256]{3,2,1,0:T(8,128)(2,1)} %copy-done) | copy-start | bytes 10616836
  93.3 2.7 %copy-start.4 = (f32[4,512,256]{2,1,0:T(8,128)S(1)}, f32[4,512,256]{2,1,0:T(8,128)}, u32[]{:S(2)}) copy-start(f32[4,512,256]{2,1,0:T(8,128)} %copy-done.3) | copy-start | bytes 6291460
  95.2 2.8 %copy-start.12 = (bf16[4,512,256]{2,1,0:T(8,128)(2,1)}, bf16[4,512,256]{2,1,0:T(8,128)(2,1)S(1)}, u32[]{:S(2)}) copy-start(bf16[4,512,256]{2,1,0:T(8,128)(2,1)S(1)} %get-tuple-element.17) | copy-start | bytes 3145732
  98.0 2.1 %collective-permute-start.16 = (f32[1152,128]{1,0:T(8,128)S(1)}, f32[1152,128]{1,0:T(8,128)S(1)}, u32[]{:S(2)}, u32[]{:S(2)}) collective-permute-start(f32[1152,128]{1,0:T(8,128)S(1)} %bitcast.29), channel_id=1, source_target_pairs={{0,1},{1,0},{2,3},{3,2},{4,5},{5,4},{6,7},{7,6},{8,9},{9,8},{10,11... | collective-permute-start | bytes 1769480 | tf_op jit(solution)/shard_map/ppermute | solution.py:218
  100.2 9.1 %collective-permute-start.17 = (f32[576,128]{1,0:T(8,128)S(1)}, f32[576,128]{1,0:T(8,128)S(1)}, u32[]{:S(2)}, u32[]{:S(2)}) collective-permute-start(f32[576,128]{1,0:T(8,128)S(1)} %slice_select_fusion), channel_id=1, source_target_pairs={{0,4},{4,0},{8,12},{12,8},{16,20},{20,16},{24,28},{28,24},{1,5},{5... | collective-permute-start | bytes 884744 | tf_op jit(solution)/shard_map/ppermute | solution.py:218
  101.7 49.6 %copy-start.13 = (bf16[4,512,256]{2,1,0:T(8,128)(2,1)S(1)}, bf16[4,512,256]{2,1,0:T(8,128)(2,1)}, u32[]{:S(2)}) copy-start(bf16[4,512,256]{2,1,0:T(8,128)(2,1)} %copy-done.12) | copy-start | bytes 3145732
  110.1 51.5 %copy-start.9 = (bf16[4,16,64,128]{3,2,1,0:T(8,128)(2,1)S(1)}, bf16[4,16,64,128]{3,2,1,0:T(8,128)(2,1)}, u32[]{:S(2)}) copy-start(bf16[4,16,64,128]{3,2,1,0:T(8,128)(2,1)} %direct.2) | copy-start | bytes 3145732
  110.1 51.5 %copy-start.15 = (bf16[3,3,128,128]{3,2,1,0:T(8,128)(2,1)S(1)}, bf16[3,3,128,128]{3,2,1,0:T(8,128)(2,1)}, u32[]{:S(2)}) copy-start(bf16[3,3,128,128]{3,2,1,0:T(8,128)(2,1)} %weight.6) | copy-start | bytes 884740
  110.1 51.5 %copy-start.22 = (f32[128]{0:T(128)S(1)}, f32[128]{0:T(128)}, u32[]{:S(2)}) copy-start(f32[128]{0:T(128)} %param.10) | copy-start | bytes 1540
  111.8 5.5 %collective-permute-start.18 = (f32[288,128]{1,0:T(8,128)}, f32[288,128]{1,0:T(8,128)}, u32[]{:S(2)}, u32[]{:S(2)}) collective-permute-start(f32[288,128]{1,0:T(8,128)} %slice_select_fusion.7), channel_id=1, source_target_pairs={{0,2},{1,3},{2,0},{3,1},{4,6},{5,7},{6,4},{7,5},{8,10},{9,11},{10,... | collective-permute-start | bytes 442376 | tf_op jit(solution)/shard_map/ppermute | solution.py:218
  118.4 0.7 copy-start.25
  119.1 4.5 %collective-permute-start.19 = (f32[144,128]{1,0:T(8,128)S(1)}, f32[144,128]{1,0:T(8,128)}, u32[]{:S(2)}, u32[]{:S(2)}) collective-permute-start(f32[144,128]{1,0:T(8,128)S(1)} %slice_select_fusion.8), channel_id=1, source_target_pairs={{0,8},{4,12},{8,0},{12,4},{16,24},{20,28},{24,16},{28,20},{1,9},{5... | collective-permute-start | bytes 221192 | tf_op jit(solution)/shard_map/ppermute | solution.py:218
  124.6 5.1 %collective-permute-start.20 = (f32[72,128]{1,0:T(8,128)S(1)}, f32[72,128]{1,0:T(8,128)S(1)}, u32[]{:S(2)}, u32[]{:S(2)}) collective-permute-start(f32[72,128]{1,0:T(8,128)S(1)} %slice_select_fusion.9), channel_id=1, source_target_pairs={{0,16},{4,20},{8,24},{12,28},{16,0},{20,4},{24,8},{28,12},{1,17},{... | collective-permute-start | bytes 110600 | tf_op jit(solution)/shard_map/ppermute | solution.py:218
  129.7 4.9 %collective-permute-start.21 = (f32[72,128]{1,0:T(8,128)S(1)}, f32[72,128]{1,0:T(8,128)S(1)}, u32[]{:S(2)}, u32[]{:S(2)}) collective-permute-start(f32[72,128]{1,0:T(8,128)S(1)} %select_add_fusion.5), channel_id=1, source_target_pairs={{0,16},{4,20},{8,24},{12,28},{16,0},{20,4},{24,8},{28,12},{1,17},{... | collective-permute-start | bytes 110600 | tf_op jit(solution)/shard_map/ppermute | solution.py:218
  134.7 4.4 %collective-permute-start.22 = (f32[144,128]{1,0:T(8,128)S(1)}, f32[144,128]{1,0:T(8,128)S(1)}, u32[]{:S(2)}, u32[]{:S(2)}) collective-permute-start(f32[144,128]{1,0:T(8,128)S(1)} %pad_maximum_fusion.11), channel_id=1, source_target_pairs={{0,8},{4,12},{8,0},{12,4},{16,24},{20,28},{24,16},{28,20},{1,9},{5... | collective-permute-start | bytes 221192 | tf_op jit(solution)/shard_map/ppermute | solution.py:218
  139.1 5.2 %collective-permute-start.23 = (f32[288,128]{1,0:T(8,128)S(1)}, f32[288,128]{1,0:T(8,128)S(1)}, u32[]{:S(2)}, u32[]{:S(2)}) collective-permute-start(f32[288,128]{1,0:T(8,128)S(1)} %pad_maximum_fusion.10), channel_id=1, source_target_pairs={{0,2},{1,3},{2,0},{3,1},{4,6},{5,7},{6,4},{7,5},{8,10},{9,11},{10,... | collective-permute-start | bytes 442376 | tf_op jit(solution)/shard_map/ppermute | solution.py:218
  144.4 6.8 %collective-permute-start.24 = (f32[576,128]{1,0:T(8,128)S(1)}, f32[576,128]{1,0:T(8,128)S(1)}, u32[]{:S(2)}, u32[]{:S(2)}) collective-permute-start(f32[576,128]{1,0:T(8,128)S(1)} %pad_maximum_fusion.5), channel_id=1, source_target_pairs={{0,4},{4,0},{8,12},{12,8},{16,20},{20,16},{24,28},{28,24},{1,5},{5... | collective-permute-start | bytes 884744 | tf_op jit(solution)/shard_map/ppermute | solution.py:218
  151.3 13.3 %copy-start.11 = (bf16[4,16,64,128]{3,2,1,0:T(8,128)(2,1)S(1)}, bf16[4,16,64,128]{3,2,1,0:T(8,128)(2,1)}, u32[]{:S(2)}) copy-start(bf16[4,16,64,128]{3,2,1,0:T(8,128)(2,1)} %direct.3) | copy-start | bytes 3145732
  151.3 13.3 %copy-start.17 = (bf16[3,3,128,128]{3,2,1,0:T(8,128)(2,1)S(1)}, bf16[3,3,128,128]{3,2,1,0:T(8,128)(2,1)}, u32[]{:S(2)}) copy-start(bf16[3,3,128,128]{3,2,1,0:T(8,128)(2,1)} %weight.7) | copy-start | bytes 884740
  151.3 16.3 %collective-permute-start.25 = (f32[1152,128]{1,0:T(8,128)S(1)}, f32[1152,128]{1,0:T(8,128)S(1)}, u32[]{:S(2)}, u32[]{:S(2)}) collective-permute-start(f32[1152,128]{1,0:T(8,128)S(1)} %pad_maximum_fusion), channel_id=1, source_target_pairs={{0,1},{1,0},{2,3},{3,2},{4,5},{5,4},{6,7},{7,6},{8,9},{9,8},{10,11... | collective-permute-start | bytes 1769480 | tf_op jit(solution)/shard_map/ppermute | solution.py:218
  151.4 10.1 %collective-permute-start.9 = (bf16[4,1,64,128]{3,2,1,0:T(8,128)(2,1)S(1)}, bf16[4,1,64,128]{3,2,1,0:T(8,128)(2,1)S(1)}, u32[]{:S(2)}, u32[]{:S(2)}) collective-permute-start(bf16[4,1,64,128]{3,2,1,0:T(8,128)(2,1)S(1)} %get-tuple-element.46), channel_id=1, source_target_pairs={{1,0},{2,1},{3,2},{5,4},{6,5},{7,6},{9,8},{10,9},{11,10},{13,12},{... | collective-permute-start | bytes 196616 | tf_op jit(solution)/shard_map/ppermute | solution.py:213
  152.8 8.7 %collective-permute-start.8 = (bf16[4,1,64,128]{3,2,1,0:T(8,128)(2,1)S(1)}, bf16[4,1,64,128]{3,2,1,0:T(8,128)(2,1)S(1)}, u32[]{:S(2)}, u32[]{:S(2)}) collective-permute-start(bf16[4,1,64,128]{3,2,1,0:T(8,128)(2,1)S(1)} %get-tuple-element.47), channel_id=1, source_target_pairs={{0,1},{1,2},{2,3},{4,5},{5,6},{6,7},{8,9},{9,10},{10,11},{12,13},{... | collective-permute-start | bytes 196616 | tf_op jit(solution)/shard_map/ppermute | solution.py:213
  155.9 8.6 %collective-permute-start.15 = (bf16[4,1,64,128]{3,2,1,0:T(8,128)(2,1)S(1)}, bf16[4,1,64,128]{3,2,1,0:T(8,128)(2,1)S(1)}, u32[]{:S(2)}, u32[]{:S(2)}) collective-permute-start(bf16[4,1,64,128]{3,2,1,0:T(8,128)(2,1)S(1)} %get-tuple-element.44), channel_id=1, source_target_pairs={{1,0},{2,1},{3,2},{5,4},{6,5},{7,6},{9,8},{10,9},{11,10},{13,12},{... | collective-permute-start | bytes 196616 | tf_op jit(solution)/shard_map/ppermute | solution.py:213
  157.2 7.3 %collective-permute-start.14 = (bf16[4,1,64,128]{3,2,1,0:T(8,128)(2,1)S(1)}, bf16[4,1,64,128]{3,2,1,0:T(8,128)(2,1)S(1)}, u32[]{:S(2)}, u32[]{:S(2)}) collective-permute-start(bf16[4,1,64,128]{3,2,1,0:T(8,128)(2,1)S(1)} %get-tuple-element.45), channel_id=1, source_target_pairs={{0,1},{1,2},{2,3},{4,5},{5,6},{6,7},{8,9},{9,10},{10,11},{12,13},{... | collective-permute-start | bytes 196616 | tf_op jit(solution)/shard_map/ppermute | solution.py:213

commit v2 on v1

v2 whole, which is shorter than its diff:
```python
import functools
import math

import jax
import jax.numpy as jnp
from jax import lax
from jax.experimental import pallas as pl
from jax.experimental.pallas import tpu as pltpu
from jax.sharding import PartitionSpec as P

F32 = jnp.float32
BF16 = jnp.bfloat16
VMEM_LIMIT = 40 * 1024 * 1024


def fill_pairs(pairs, field, top, bottom):
    half = field.shape[1] // 2
    ch = field.shape[3]
    pairs[:, 0, :, :ch] = top[:, 0]
    pairs[:, half, :, ch:] = bottom[:, 0]
    for i in range(half):
        pairs[:, i, :, ch:] = field[:, 2 * i]
        pairs[:, i + 1, :, :ch] = field[:, 2 * i + 1]


def fill_pairs_from_pairs(pairs, field, top, bottom):
    half = field.shape[1]
    ch = field.shape[3] // 2
    pairs[:, 0, :, :ch] = top[:, 0]
    pairs[:, half, :, ch:] = bottom[:, 0]
    pairs[:, :half, :, ch:] = field[:, :, :, :ch]
    pairs[:, 1:, :, :ch] = field[:, :, :, ch:]


def column_taps(flat, cols):
    wide = flat.astype(F32)
    count = wide.shape[0]
    col = lax.broadcasted_iota(jnp.int32, wide.shape, 0) % cols
    left = jnp.where(col == 0, 0.0, pltpu.roll(wide, 1, 0)).astype(flat.dtype)
    right = jnp.where(col == cols - 1, 0.0, pltpu.roll(wide, count - 1, 0)).astype(flat.dtype)
    return left, flat, right


def fill_weights(blocks, weight, flip):
    ch = weight.shape[2]
    zero = jnp.zeros((ch, ch), weight.dtype)
    for j in range(3):
        for b in range(2):
            for k in range(2):
                for n in range(2):
                    tap = 2 * b + k - n
                    ok = 0 <= tap <= 2
                    if flip:
                        value = weight[2 - tap, 2 - j] if ok else zero
                        blocks[j, b, n * ch : (n + 1) * ch, k * ch : (k + 1) * ch] = value
                    else:
                        value = weight[tap, j] if ok else zero
                        blocks[j, b, k * ch : (k + 1) * ch, n * ch : (n + 1) * ch] = value


def conv_pairs(taps, blocks, rows_out, cols, flip):
    dims = (((1,), (1,)), ((), ())) if flip else (((1,), (0,)), ((), ()))
    total = None
    for j in range(3):
        for b in range(2):
            part = lax.dot_general(
                taps[j][b * cols : b * cols + rows_out],
                blocks[j, b],
                dims,
                preferred_element_type=F32,
            )
            total = part if total is None else total + part
    return total


def pick_halos(first, second, index, odd, times):
    one = first[index].astype(F32)
    two = second[index].astype(F32)
    upper = jnp.where(odd, one, two).astype(BF16)
    lower = jnp.where(odd, two, one).astype(BF16)
    return upper[:, None], lower[:, None]


def exponent(value):
    top = jnp.max(jnp.abs(value), axis=0, keepdims=True)
    return jnp.ceil(jnp.log2(jnp.maximum(top, 1e-30)))


def decays(log_decay):
    wide = jnp.concatenate([log_decay, log_decay], 1)
    times = wide.shape[0]
    sums = [wide[0:1]]
    for t in range(1, times):
        sums.append(sums[-1] + wide[t : t + 1])
    rate = [jnp.exp(wide[t : t + 1]) for t in range(times)]
    reach = [jnp.exp(total) for total in sums]
    tail = [jnp.exp(sums[-1] - total) for total in sums]
    return rate, reach, tail


def drive_kernel(
    parity,
    frames,
    cotangent,
    first,
    second,
    w_in,
    w_out,
    log_decay,
    states,
    adjoints,
    leaving,
    frame_taps,
    cot_taps,
    info,
    pairs,
    blocks,
):
    times, rows, cols, ch = frames.shape
    half = rows // 2
    odd = parity[0] == 1
    rate, reach, _ = decays(log_decay[...])
    fields = ((frames, w_in, states, frame_taps), (cotangent, w_out, adjoints, cot_taps))
    for index, (field, weight, result, taps_out) in enumerate(fields):
        flip = index == 1
        top, bottom = pick_halos(first, second, index, odd, times)
        fill_weights(blocks.at[index], weight, flip)
        fill_pairs(pairs.at[index], field, top, bottom)
        carry = None
        for step in range(times):
            t = times - 1 - step if flip else step
            taps = column_taps(pairs[index, t].reshape((half + 1) * cols, 2 * ch), cols)
            for j in range(3):
                taps_out[j, t] = taps[j]
            value = conv_pairs(taps, blocks.at[index], half * cols, cols, flip)
            if flip:
                value = value if carry is None else value + carry
                carry = rate[t] * value
            else:
                value = (1.0 - rate[t]) * value
                value = value if carry is None else rate[t] * carry + value
                carry = value
            result[t] = value
        if flip:
            leaving[...] = carry
        info[index : index + 1, :] = exponent(carry)
    total = reach[-1]
    high = total.astype(BF16).astype(F32)
    rest = (total - high) * 256.0
    middle = rest.astype(BF16).astype(F32)
    low = ((rest - middle) * 256.0).astype(BF16).astype(F32)
    info[2:3, :] = high
    info[3:4, :] = middle
    info[4:5, :] = low
    info[5:, :] = jnp.zeros((info.shape[0] - 5, 2 * ch), F32)


def drive_call(parity, frames, cotangent, first, second, w_in, w_out, log_decay):
    times, rows, cols, ch = frames.shape
    half = rows // 2
    field = jax.ShapeDtypeStruct((times, half * cols, 2 * ch), F32)
    taps = jax.ShapeDtypeStruct((3, times, (half + 1) * cols, 2 * ch), BF16)
    return pl.pallas_call(
        drive_kernel,
        in_specs=[pl.BlockSpec(memory_space=pltpu.SMEM)]
        + [pl.BlockSpec(memory_space=pltpu.VMEM)] * 7,
        out_shape=(
            field,
            field,
            jax.ShapeDtypeStruct(field.shape[1:], F32),
            taps,
            taps,
            jax.ShapeDtypeStruct((16, 2 * ch), F32),
        ),
        scratch_shapes=[
            pltpu.VMEM((2, times, half + 1, cols, 2 * ch), BF16),
            pltpu.VMEM((2, 3, 2, 2 * ch, 2 * ch), BF16),
        ],
        compiler_params=pltpu.CompilerParams(vmem_limit_bytes=VMEM_LIMIT),
        cost_estimate=pl.CostEstimate(
            flops=times * rows * cols * ch * ch * 48, bytes_accessed=12 << 20, transcendentals=0
        ),
        name="drive",
    )(parity, frames, cotangent, first, second, w_in, w_out, log_decay)


def grads_kernel(
    parity,
    states,
    adjoints,
    state_in,
    adjoint_in,
    log_decay,
    frame_taps,
    cot_taps,
    states_bf,
    inflow_bf,
    first,
    second,
    grads_in,
    grads_out,
    info,
    turned,
):
    times, count, width = states.shape
    ch = width // 2
    cols = frame_taps.shape[2] - count
    odd = parity[0] == 1
    rate, reach, tail = decays(log_decay[...])
    add = state_in[...]
    back = adjoint_in[...]
    for t in range(times):
        value = (states[t] + reach[t] * add).astype(BF16)
        states_bf[t] = value
        turned[0, t] = value.T
        value = ((1.0 - rate[t]) * (adjoints[t] + tail[t] * back)).astype(BF16)
        inflow_bf[t] = value
        turned[1, t] = value.T
        for index, field in enumerate((states_bf, inflow_bf)):
            low = field[t, :cols, :ch].astype(F32)
            high = field[t, count - cols :, ch:].astype(F32)
            first[index, t] = jnp.where(odd, low, high).astype(BF16)
            second[index, t] = jnp.where(odd, high, low).astype(BF16)
    for index, (taps, grads) in enumerate(((cot_taps, grads_out), (frame_taps, grads_in))):
        largest = None
        for j in range(3):
            blocks = []
            for b in range(2):
                total = None
                for t in range(times):
                    part = jnp.dot(
                        turned[index, t],
                        taps[j, t, b * cols : b * cols + count],
                        preferred_element_type=F32,
                    )
                    total = part if total is None else total + part
                blocks.append(total)
            for tap in range(3):
                total = None
                for b in range(2):
                    for c in range(2):
                        a = 2 * b + c - tap
                        if a in (0, 1):
                            part = blocks[b][a * ch : (a + 1) * ch, c * ch : (c + 1) * ch]
                            total = part if total is None else total + part
                if index == 0:
                    place = (2 - tap) * 3 + 2 - j
                else:
                    place = tap * 3 + j
                    total = total.T
                grads[place * ch : (place + 1) * ch, :] = total
                top = jnp.max(jnp.abs(total), axis=0, keepdims=True)
                largest = top if largest is None else jnp.maximum(largest, top)
        info[index * 8 : index * 8 + 8, :] = jnp.broadcast_to(exponent(largest), (8, ch))


def grads_call(parity, states, adjoints, state_in, adjoint_in, log_decay, frame_taps, cot_taps):
    times, count, width = states.shape
    ch = width // 2
    cols = frame_taps.shape[2] - count
    field = jax.ShapeDtypeStruct((times, count, width), BF16)
    edge = jax.ShapeDtypeStruct((2, times, cols, ch), BF16)
    grads = jax.ShapeDtypeStruct((9 * ch, ch), F32)
    return pl.pallas_call(
        grads_kernel,
        in_specs=[pl.BlockSpec(memory_space=pltpu.SMEM)]
        + [pl.BlockSpec(memory_space=pltpu.VMEM)] * 7,
        out_shape=(field, field, edge, edge, grads, grads, jax.ShapeDtypeStruct((16, ch), F32)),
        scratch_shapes=[pltpu.VMEM((2, times, width, count), BF16)],
        compiler_params=pltpu.CompilerParams(vmem_limit_bytes=VMEM_LIMIT),
        cost_estimate=pl.CostEstimate(
            flops=times * count * ch * ch * 96, bytes_accessed=12 << 20, transcendentals=0
        ),
        name="grads",
    )(parity, states, adjoints, state_in, adjoint_in, log_decay, frame_taps, cot_taps)


def output_kernel(parity, field, first, second, weight, skip, direct, out, pairs, blocks, *, flip):
    times, half, cols, width = field.shape
    ch = width // 2
    fill_weights(blocks, weight, flip)
    top, bottom = pick_halos(first, second, int(flip), parity[0] == 1, times)
    fill_pairs_from_pairs(pairs, field, top, bottom)
    gain = skip[...]
    for t in range(times):
        taps = column_taps(pairs[t].reshape((half + 1) * cols, width), cols)
        value = conv_pairs(taps, blocks, half * cols, cols, flip).reshape(half, cols, width)
        for i in range(half):
            for c in range(2):
                base = gain * direct[t, 2 * i + c].astype(F32)
                out[t, 2 * i + c] = (value[i, :, c * ch : (c + 1) * ch] + base).astype(BF16)


def output_call(parity, field, first, second, weight, skip, direct, flip):
    times, half, cols, width = field.shape
    ch = width // 2
    return pl.pallas_call(
        functools.partial(output_kernel, flip=flip),
        in_specs=[pl.BlockSpec(memory_space=pltpu.SMEM)]
        + [pl.BlockSpec(memory_space=pltpu.VMEM)] * 6,
        out_shape=jax.ShapeDtypeStruct(direct.shape, BF16),
        scratch_shapes=[
            pltpu.VMEM((times, half + 1, cols, width), BF16),
            pltpu.VMEM((3, 2, width, width), BF16),
        ],
        compiler_params=pltpu.CompilerParams(vmem_limit_bytes=VMEM_LIMIT),
        cost_estimate=pl.CostEstimate(
            flops=times * half * cols * ch * ch * 48, bytes_accessed=4 << 20, transcendentals=0
        ),
        name="grad_frames" if flip else "output",
    )(parity, field, first, second, weight, skip, direct)


def swap(value, tm_bits, tile_bits):
    tiles = lax.axis_size("tile")
    mask = tm_bits * tiles + tile_bits
    count = lax.axis_size("tm") * tiles
    return lax.ppermute(value, ("tm", "tile"), [(i, i ^ mask) for i in range(count)])


def swap_across(value):
    count = lax.axis_size("tile")
    pairs = []
    for i in range(1, count - 1, 2):
        pairs += [(i, i + 1), (i + 1, i)]
    return lax.ppermute(value, "tile", pairs)


def packed(value, scale, rows):
    pad = jnp.zeros((16 - rows.shape[0], rows.shape[1]), F32)
    return jnp.concatenate([value * jnp.exp2(-scale), rows, pad], 0).astype(jnp.float16)


def whole_decay(rows):
    return rows[0:1] + rows[1:2] / 256.0 + rows[2:3] / 65536.0


def carry_over(state_end, adjoint_end, info):
    count = lax.axis_size("tm")
    place = lax.axis_index("tm")
    odd = place % 2 == 1
    pair_place = place // 2
    half = state_end.shape[0] // 2

    def both(low, high, scale_low, scale_high, rows):
        pad = jnp.zeros((16 - rows.shape[0], rows.shape[1]), F32)
        return jnp.concatenate(
            [low * jnp.exp2(-scale_low), high * jnp.exp2(-scale_high), rows, pad], 0
        ).astype(jnp.float16)

    def give(value, mine):
        return jnp.where(odd == mine, value[half:], value[:half])

    got = swap(
        both(give(state_end, False), give(adjoint_end, False), info[0:1], info[1:2], info[:5]), 1, 0
    ).astype(F32)
    their_info = got[2 * half : 2 * half + 5]
    total, their_total = whole_decay(info[2:5]), whole_decay(their_info[2:5])
    even_total = jnp.where(odd, their_total, total)
    odd_total = jnp.where(odd, total, their_total)
    state_mine, adjoint_mine = give(state_end, True), give(adjoint_end, True)
    state_theirs = got[:half] * jnp.exp2(their_info[0:1])
    adjoint_theirs = got[half : 2 * half] * jnp.exp2(their_info[1:2])
    state_even = jnp.where(odd, state_theirs, state_mine)
    state_odd = jnp.where(odd, state_mine, state_theirs)
    adjoint_even = jnp.where(odd, adjoint_theirs, adjoint_mine)
    adjoint_odd = jnp.where(odd, adjoint_mine, adjoint_theirs)
    state_pair = odd_total * state_even + state_odd
    adjoint_pair = adjoint_even + even_total * adjoint_odd
    state_scale = jnp.maximum(info[0:1], their_info[0:1])
    adjoint_scale = jnp.maximum(info[1:2], their_info[1:2])

    messages = []
    bit = 1
    while bit < count // 2:
        later = (pair_place // bit) % 2 == 1
        scale = jnp.where(later, adjoint_scale, state_scale)
        rows = jnp.concatenate([scale, info[2:5], their_info[2:5]], 0)
        messages.append(packed(jnp.where(later, adjoint_pair, state_pair), scale, rows))
        bit *= 2
    received = {}
    for d in range(1, count // 2):
        received[d] = swap(messages[d.bit_length() - 1], 2 * d, 0).astype(F32)
    totals, values = {}, {}
    top_scale = jnp.maximum(state_scale, adjoint_scale)
    for d, got in received.items():
        rows = got[half : half + 7]
        totals[d] = whole_decay(rows[1:4]) * whole_decay(rows[4:7])
        values[d] = got[:half] * jnp.exp2(rows[0:1])
        top_scale = jnp.maximum(top_scale, rows[0:1])
    state_before = jnp.zeros_like(state_pair)
    adjoint_after = jnp.zeros_like(adjoint_pair)
    for d in received:
        other = pair_place ^ d
        through = jnp.ones_like(top_scale)
        for e in received:
            between = pair_place ^ e
            inside = ((other < between) & (between < pair_place)) | (
                (pair_place < between) & (between < other)
            )
            through = through * jnp.where(inside, totals[e], 1.0)
        term = through * values[d]
        state_before = state_before + jnp.where(other < pair_place, term, 0.0)
        adjoint_after = adjoint_after + jnp.where(other > pair_place, term, 0.0)

    state_inner = state_even + even_total * state_before
    adjoint_inner = adjoint_odd + odd_total * adjoint_after
    state_keep = jnp.where(odd, state_inner, state_before)
    state_send = jnp.where(odd, state_before, state_inner)
    adjoint_keep = jnp.where(odd, adjoint_after, adjoint_inner)
    adjoint_send = jnp.where(odd, adjoint_inner, adjoint_after)
    got = swap(both(state_send, adjoint_send, top_scale, top_scale, top_scale), 1, 0).astype(F32)
    scale = jnp.exp2(got[2 * half : 2 * half + 1])

    def joined(keep, other):
        return jnp.concatenate([jnp.where(odd, other, keep), jnp.where(odd, keep, other)], 0)

    return (
        joined(state_keep, got[:half] * scale),
        joined(adjoint_keep, got[half : 2 * half] * scale),
    )


def unpacked(got):
    rows = got.shape[-2] - 16
    wide = got.astype(F32)
    scale = wide[..., rows : rows + 1, :]
    return wide[..., :rows, :] * jnp.exp2(scale), scale


def bit_set(tm_bits, tile_bits):
    place = lax.axis_index("tm") // tm_bits if tm_bits else lax.axis_index("tile") // tile_bits
    return place % 2 == 1


def shards(frames, cotangent, w_in, w_out, skip, log_decay):
    times, rows, cols, ch = frames.shape
    half = rows // 2
    tile = lax.axis_index("tile")
    odd = tile % 2 == 1
    parity = (tile % 2).reshape(1).astype(jnp.int32)
    gain = skip[None, :]

    low = jnp.stack([frames[:, 0], cotangent[:, 0]])
    high = jnp.stack([frames[:, -1], cotangent[:, -1]])
    second = swap_across(jnp.where(odd, high, low))
    first = swap(jnp.where(odd, low, high), 0, 1)

    states, adjoints, leaving, frame_taps, cot_taps, info = drive_call(
        parity, frames, cotangent, first, second, w_in, w_out, log_decay
    )
    state_in, adjoint_in = carry_over(states[-1], leaving, info)
    states_bf, inflow_bf, first, second, in_part, out_part, info = grads_call(
        parity, states, adjoints, state_in, adjoint_in, log_decay, frame_taps, cot_taps
    )

    in_scale, out_scale = info[8:9], info[0:1]
    scale = jnp.where(odd, in_scale, out_scale)
    message = packed(jnp.where(odd, in_part, out_part), scale, scale)
    message, first, second = lax.optimization_barrier((message, first, second))
    got, got_scale = unpacked(swap(message, 0, 1))
    value = jnp.where(odd, out_part, in_part) + got
    scale = jnp.maximum(jnp.where(odd, out_scale, in_scale), got_scale)
    second = swap_across(second)
    first = swap(first, 0, 1)

    bits = [(1, 0), (0, 2)] if lax.axis_size("tile") > 2 else [(1, 0)]
    parts = 2 ** len(bits)
    place = sum(bit_set(*bit).astype(jnp.int32) * 2**n for n, bit in enumerate(bits))
    pieces = value.reshape(parts, -1, ch)

    def mask(d):
        chosen = [bit for n, bit in enumerate(bits) if d >> n & 1]
        return sum(b[0] for b in chosen), sum(b[1] for b in chosen)

    messages = [
        packed(lax.dynamic_index_in_dim(pieces, place ^ d, 0, False), scale, scale)
        for d in range(1, parts)
    ]
    value = lax.dynamic_index_in_dim(pieces, place, 0, False)
    states_bf = states_bf.reshape(times, half, cols, 2 * ch)
    inflow_bf = inflow_bf.reshape(times, half, cols, 2 * ch)
    *messages, states_bf = lax.optimization_barrier((*messages, states_bf))
    received = [swap(m, *mask(d + 1)) for d, m in enumerate(messages)]
    output = output_call(parity, states_bf, first, second, w_out, gain, frames, False)
    for got in received:
        got, got_scale = unpacked(got)
        value = value + got
        scale = jnp.maximum(scale, got_scale)

    left = []
    bit = 2
    while bit < lax.axis_size("tm"):
        left.append((bit, 0))
        bit *= 2
    bit = 4
    while bit < lax.axis_size("tile"):
        left.append((0, bit))
        bit *= 2
    waiting = inflow_bf
    for n in range(0, len(left), 2):
        group = left[n : n + 2]
        message = packed(value, scale, scale)
        message, output, waiting = lax.optimization_barrier((message, output, waiting))
        terms = [message]
        for d in range(1, 2 ** len(group)):
            chosen = [b for k, b in enumerate(group) if d >> k & 1]
            terms.append(swap(message, sum(b[0] for b in chosen), sum(b[1] for b in chosen)))
        terms = [unpacked(term) for term in terms]
        while len(terms) > 1:
            terms = [
                (a[0] + b[0], jnp.maximum(a[1], b[1])) for a, b in zip(terms[::2], terms[1::2])
            ]
        value, scale = terms[0]
    grad_frames = output_call(parity, waiting, first, second, w_in, gain, cotangent, True)

    message = packed(value, scale, scale)
    message, grad_frames = lax.optimization_barrier((message, grad_frames))
    gathered = [message] + [swap(message, *mask(d)) for d in range(1, parts)]
    for bit in bits:
        high = bit_set(*bit)
        gathered = [
            (jnp.where(high, b, a), jnp.where(high, a, b))
            for a, b in zip(gathered[::2], gathered[1::2])
        ]
        gathered = [jnp.concatenate(pair, 0) for pair in gathered]
    (mine,) = gathered
    mine = lax.optimization_barrier(mine)
    theirs = swap(mine, 0, 1)
    factor = 1.0 / math.sqrt(
        times * lax.axis_size("tm") * rows * lax.axis_size("tile") * cols
    )
    results = []
    for chosen in (jnp.where(odd, theirs, mine), jnp.where(odd, mine, theirs)):
        whole, _ = unpacked(chosen.reshape(parts, -1, ch))
        results.append((whole * factor).reshape(3, 3, ch, ch))
    return (output, grad_frames, results[0], results[1])


def solution(mesh):
    placed = (
        P("tm", "tile", None, None),
        P("tm", "tile", None, None),
        P(),
        P(),
        P(),
        P("tm", None),
    )
    return jax.shard_map(
        shards,
        mesh=mesh,
        in_specs=placed,
        out_specs=(P("tm", "tile", None, None), P("tm", "tile", None, None), P(), P()),
        check_vma=False,
    )
```

time: 171 us -> 95.1 us (0.56); the launches traced: 169 us -> 94.7 us
  waiting for transfers between devices: 71.1 us -> 26.6 us
  starting transfers between devices: 48 us -> 30.7 us
  other arithmetic: 18 us -> 4.36 us
  Pallas kernels: 15.3 us -> 17.9 us
    ppermute x26 -> x20, waiting for transfers between devices: 71.1 us -> 26.6 us  [the longest x18 26.6 us: swap(): lax.ppermute(value, ('tm', 'tile'), [(i, i ^ mask) for i in range(count)])]
    ppermute x26 -> x20, starting transfers between devices: 48 us -> 30.7 us  [the longest x18 29 us: swap(): lax.ppermute(value, ('tm', 'tile'), [(i, i ^ mask) for i in range(count)])]
    add x9 -> x1, other arithmetic: 5.99 us -> 0.09 us  [shards(): value = jnp.where(odd, out_part, in_part) + got]
    select_n x14 -> x8, other arithmetic: 5.96 us -> 0.54 us  [the longest x3 0.19 us: shards(): jnp.where(high, b, a)]
    pallas_call x6 -> x4, Pallas kernels: 15.3 us -> 17.9 us  [the longest x2 6.11 us: output_call(): pl.pallas_call(functools.partial(output_kernel, flip=flip), in_specs=[pl....]
    slice x4 -> x0, local copies, waits for them, and re-layouts: 2.47 us -> none  [the longest x1 1.54 us: shards(): frames[:, :1]]
    unnamed x58 -> x38, local copies, waits for them, and re-layouts: 11.9 us -> 12 us
  transfers between devices with their start and end apart: 26 -> 20, of which waited for: 16 -> 13; matrix products, arithmetic and copies ran while one was open for 6% -> 1% of each run, Pallas kernels for 5% -> 6%
where the time goes in v2:
time: 95.1 us; the launch traced here: 94.7 us
  starting transfers between devices  30.7 us (32%)
  waiting for transfers between devices  26.6 us (28%)
  Pallas kernels  17.9 us (19%)
  local copies, waits for them, and re-layouts  13.9 us (15%)
  other arithmetic  4.36 us (5%)
  between operations  1.28 us (1%)
    ppermute x18, starting transfers between devices, swap(): lax.ppermute(value, ('tm', 'tile'), [(i, i ^ mask) for i in range(count)])  29 us
    ppermute x18, waiting for transfers between devices, swap(): lax.ppermute(value, ('tm', 'tile'), [(i, i ^ mask) for i in range(count)])  26.6 us
    unnamed x38, local copies, waits for them, and re-layouts  12 us
    pallas_call x2, Pallas kernels, output_call(): pl.pallas_call(functools.partial(output_kernel, flip=flip), in_specs=[pl....  6.11 us
    pallas_call x1, Pallas kernels, drive_call(): pl.pallas_call(drive_kernel, in_specs=[pl.BlockSpec(memory_space=pltpu.SM...  6.11 us
    pallas_call x1, Pallas kernels, grads_call(): pl.pallas_call(grads_kernel, in_specs=[pl.BlockSpec(memory_space=pltpu.SM...  5.66 us
  transfers between devices with their start and end apart: 20, of which 13 were waited for; matrix products, arithmetic and copies ran while one was open for 1% of the time, Pallas kernels for 6%

profile of v2, /device:TPU:0, one launch (start us, length us, event | category | flops | bytes accessed | tf_op | source)
XLA Modules:
  0.0 94.7 jit_solution(2795004735614607906)
XLA Ops:
  0.6 1.0 %slice_bitcast_fusion.2 = (bf16[1,4,64,128]{3,2,1,0:T(8,128)(2,1)S(1)}, bf16[1,4,64,128]{3,2,1,0:T(8,128)(2,1)S(1)}, bf16[1,4,64,128]{3,2,1,0:T(8,128)(2,1)S(1)}, bf16[1,4,64,128]{3,2,1,0:T(8,128)(2,1)S(1)}) fusion(bf16[4,16,64,128]{3,2,1,0:T(8,128)(2,1)} %direct.3, bf16[4,16,64,128]{3,2,1,0:T(8,128)(2,1)} %direct.2), kind=kLoop, calls=%fused_computation.93 | loop fusion | bytes 524288 | tf_op jit(solution)/shard_map/stack;squeeze | solution.py:444
  1.6 0.5 collective-permute-start
  2.2 0.7 collective-permute-start.1
  2.9 0.1 pad.32.clone
  2.9 0.2 collective-permute-done.first
  3.2 1.2 %copy-done.4 = bf16[4,16,64,128]{3,2,1,0:T(8,128)(2,1)S(1)} copy-done((bf16[4,16,64,128]{3,2,1,0:T(8,128)(2,1)S(1)}, bf16[4,16,64,128]{3,2,1,0:T(8,128)(2,1)}, u32[]{:S(2)}) %copy-start.4) | copy-done | bytes 1048600
  4.4 1.2 %copy-done.6 = bf16[4,16,64,128]{3,2,1,0:T(8,128)(2,1)S(1)} copy-done((bf16[4,16,64,128]{3,2,1,0:T(8,128)(2,1)S(1)}, bf16[4,16,64,128]{3,2,1,0:T(8,128)(2,1)}, u32[]{:S(2)}) %copy-start.6) | copy-done | bytes 1048600
  5.6 0.7 copy-done.8
  6.3 1.0 %copy-done.14 = bf16[3,3,128,128]{3,2,1,0:T(8,128)(2,1)S(1)} copy-done((bf16[3,3,128,128]{3,2,1,0:T(8,128)(2,1)S(1)}, bf16[3,3,128,128]{3,2,1,0:T(8,128)(2,1)}, u32[]{:S(2)}) %copy-start.14) | copy-done | bytes 294936
  7.3 1.0 %copy-done.16 = bf16[3,3,128,128]{3,2,1,0:T(8,128)(2,1)S(1)} copy-done((bf16[3,3,128,128]{3,2,1,0:T(8,128)(2,1)S(1)}, bf16[3,3,128,128]{3,2,1,0:T(8,128)(2,1)}, u32[]{:S(2)}) %copy-start.16) | copy-done | bytes 294936
  8.2 6.1 %drive.1 = (f32[4,512,256]{2,1,0:T(8,128)S(1)}, f32[4,512,256]{2,1,0:T(8,128)S(1)}, f32[512,256]{1,0:T(8,128)S(1)}, bf16[3,4,576,256]{3,2,1,0:T(8,128)(2,1)S(1)}...) custom-call(s32[1]{0:T(128)} %bitcast.parity, bf16[4,16,64,128]{3,2,1,0:T(8,128)(2,1)S(1)} %copy-done.4, ...), custom_call_target="tpu_custom_call" | custom-call | flops 3221225472 | bytes 12582912 | tf_op jit(solution)/shard_map/drive/pallas_call | solution.py:163
  14.3 1.8 %copy-done = bf16[3,4,576,256]{3,2,1,0:T(8,128)(2,1)} copy-done((bf16[3,4,576,256]{3,2,1,0:T(8,128)(2,1)}, bf16[3,4,576,256]{3,2,1,0:T(8,128)(2,1)S(1)}, u32[]{:S(2)}) %copy-start) | copy-done | bytes 3538968
  16.1 1.4 %copy-done.2 = f32[4,512,256]{2,1,0:T(8,128)} copy-done((f32[4,512,256]{2,1,0:T(8,128)}, f32[4,512,256]{2,1,0:T(8,128)S(1)}, u32[]{:S(2)}) %copy-start.2) | copy-done | bytes 2097176
  17.6 0.1 maximum_maximum_fusion
  17.7 2.9 %collective-permute-start.2 = (f16[528,256]{1,0:T(8,128)(2,1)S(1)}, f16[528,256]{1,0:T(8,128)(2,1)S(1)}, u32[]{:S(2)}, u32[]{:S(2)}) collective-permute-start(f16[528,256]{1,0:T(8,128)(2,1)S(1)} %maximum_maximum_fusion), channel_id=1, source_target_pairs={{0,4},{1,5},{2,6},{3,7},{4,0},{5,1},{6,2},{7,3},{8,12},{9,13},{10,... | collective-permute-start | bytes 811016 | tf_op jit(solution)/shard_map/ppermute | solution.py:318
  20.7 4.4 %collective-permute-done.2 = f16[528,256]{1,0:T(8,128)(2,1)S(1)} collective-permute-done((f16[528,256]{1,0:T(8,128)(2,1)S(1)}, f16[528,256]{1,0:T(8,128)(2,1)S(1)}, u32[]{:S(2)}, u32[]{:S(2)}) %collective-permute-start.2) | collective-permute-done | bytes 270368 | tf_op jit(solution)/shard_map/ppermute | solution.py:318
  25.2 0.1 multiply_convert_fusion.3
  25.4 0.2 concatenate.56
  25.6 3.2 %collective-permute-start.3 = (f16[272,256]{1,0:T(8,128)(2,1)S(1)}, f16[272,256]{1,0:T(8,128)(2,1)S(1)}, u32[]{:S(2)}, u32[]{:S(2)}) collective-permute-start(f16[272,256]{1,0:T(8,128)(2,1)S(1)} %concatenate.56), channel_id=1, source_target_pairs={{0,16},{1,17},{2,18},{3,19},{4,20},{5,21},{6,22},{7,23},{8,24},{9,... | collective-permute-start | bytes 417800 | tf_op jit(solution)/shard_map/ppermute | solution.py:318
  28.8 0.1 pad.28.clone
  28.9 1.4 %collective-permute-start.4 = (f16[272,256]{1,0:T(8,128)(2,1)S(1)}, f16[272,256]{1,0:T(8,128)(2,1)S(1)}, u32[]{:S(2)}, u32[]{:S(2)}) collective-permute-start(f16[272,256]{1,0:T(8,128)(2,1)S(1)} %concatenate.56), channel_id=1, source_target_pairs={{0,24},{1,25},{2,26},{3,27},{4,28},{5,29},{6,30},{7,31},{8,16},{9,... | collective-permute-start | bytes 417800 | tf_op jit(solution)/shard_map/ppermute | solution.py:318
  30.3 0.2 concatenate.57
  30.5 0.3 collective-permute-start.5
  30.8 2.5 %collective-permute-done.3 = f16[272,256]{1,0:T(8,128)(2,1)S(1)} collective-permute-done((f16[272,256]{1,0:T(8,128)(2,1)S(1)}, f16[272,256]{1,0:T(8,128)(2,1)S(1)}, u32[]{:S(2)}, u32[]{:S(2)}) %collective-permute-start.3) | collective-permute-done | bytes 139296 | tf_op jit(solution)/shard_map/ppermute | solution.py:318
  33.4 3.3 %collective-permute-done.4 = f16[272,256]{1,0:T(8,128)(2,1)S(1)} collective-permute-done((f16[272,256]{1,0:T(8,128)(2,1)S(1)}, f16[272,256]{1,0:T(8,128)(2,1)S(1)}, u32[]{:S(2)}, u32[]{:S(2)}) %collective-permute-start.4) | collective-permute-done | bytes 139296 | tf_op jit(solution)/shard_map/ppermute | solution.py:318
  36.8 1.1 %collective-permute-done.5 = f16[272,256]{1,0:T(8,128)(2,1)S(1)} collective-permute-done((f16[272,256]{1,0:T(8,128)(2,1)S(1)}, f16[272,256]{1,0:T(8,128)(2,1)S(1)}, u32[]{:S(2)}, u32[]{:S(2)}) %collective-permute-start.5) | collective-permute-done | bytes 139296 | tf_op jit(solution)/shard_map/ppermute | solution.py:318
  37.9 0.2 multiply_convert_fusion.2
  38.1 0.2 multiply_convert_fusion.1
  38.3 0.1 maximum_maximum_fusion.1
  38.4 1.6 %collective-permute-start.6 = (f16[528,256]{1,0:T(8,128)(2,1)S(1)}, f16[528,256]{1,0:T(8,128)(2,1)S(1)}, u32[]{:S(2)}, u32[]{:S(2)}) collective-permute-start(f16[528,256]{1,0:T(8,128)(2,1)S(1)} %maximum_maximum_fusion.1), channel_id=1, source_target_pairs={{0,4},{1,5},{2,6},{3,7},{4,0},{5,1},{6,2},{7,3},{8,12},{9,13},{10,... | collective-permute-start | bytes 811016 | tf_op jit(solution)/shard_map/ppermute | solution.py:318
  40.0 5.3 %collective-permute-done.6 = f16[528,256]{1,0:T(8,128)(2,1)S(1)} collective-permute-done((f16[528,256]{1,0:T(8,128)(2,1)S(1)}, f16[528,256]{1,0:T(8,128)(2,1)S(1)}, u32[]{:S(2)}, u32[]{:S(2)}) %collective-permute-start.6) | collective-permute-done | bytes 270368 | tf_op jit(solution)/shard_map/ppermute | solution.py:318
  45.3 0.1 fusion.14
  45.6 1.7 %copy-done.1 = bf16[3,4,576,256]{3,2,1,0:T(8,128)(2,1)S(1)} copy-done((bf16[3,4,576,256]{3,2,1,0:T(8,128)(2,1)S(1)}, bf16[3,4,576,256]{3,2,1,0:T(8,128)(2,1)}, u32[]{:S(2)}) %copy-start.1) | copy-done | bytes 3538968
  47.3 5.7 %grads.1 = (bf16[4,512,256]{2,1,0:T(8,128)(2,1)S(1)}, bf16[4,512,256]{2,1,0:T(8,128)(2,1)S(1)}, bf16[2,4,64,128]{3,2,1,0:T(8,128)(2,1)S(1)}, bf16[2,4,64,128]{3,...) custom-call(s32[1]{0:T(128)} %bitcast.parity, ...), custom_call_target="tpu_custom_call" | custom-call | flops 3221225472 | bytes 12582912 | tf_op jit(solution)/shard_map/grads/pallas_call | solution.py:264
  53.0 1.0 %copy-done.10 = bf16[4,512,256]{2,1,0:T(8,128)(2,1)} copy-done((bf16[4,512,256]{2,1,0:T(8,128)(2,1)}, bf16[4,512,256]{2,1,0:T(8,128)(2,1)S(1)}, u32[]{:S(2)}) %copy-start.10) | copy-done | bytes 1048600
  54.0 1.0 %copy-done.12 = bf16[4,512,256]{2,1,0:T(8,128)(2,1)} copy-done((bf16[4,512,256]{2,1,0:T(8,128)(2,1)}, bf16[4,512,256]{2,1,0:T(8,128)(2,1)S(1)}, u32[]{:S(2)}) %copy-start.12) | copy-done | bytes 1048600
  55.0 0.1 multiply_convert_fusion
  55.1 0.3 concatenate.61
  55.4 2.4 %collective-permute-start.7 = (f16[1168,128]{1,0:T(8,128)(2,1)S(1)}, f16[1168,128]{1,0:T(8,128)(2,1)S(1)}, u32[]{:S(2)}, u32[]{:S(2)}) collective-permute-start(f16[1168,128]{1,0:T(8,128)(2,1)S(1)} %concatenate.61), channel_id=1, source_target_pairs={{0,1},{1,0},{2,3},{3,2},{4,5},{5,4},{6,7},{7,6},{8,9},{9,8},{10,11... | collective-permute-start | bytes 897032 | tf_op jit(solution)/shard_map/ppermute | solution.py:318
  57.9 0.2 collective-permute-start.11
  58.1 1.0 %collective-permute-start.12 = (bf16[2,4,64,128]{3,2,1,0:T(8,128)(2,1)S(1)}, bf16[2,4,64,128]{3,2,1,0:T(8,128)(2,1)S(1)}, u32[]{:S(2)}, u32[]{:S(2)}) collective-permute-start(bf16[2,4,64,128]{3,2,1,0:T(8,128)(2,1)S(1)} %get-tuple-element.47), channel_id=1, source_target_pairs={{1,2},{2,1},{5,6},{6,5},{9,10},{10,9},{13,14},{14,13},{17,18},{18,... | collective-permute-start | bytes 393224 | tf_op jit(solution)/shard_map/ppermute | solution.py:326
  59.2 0.1 fusion.2
  59.3 0.1 pad_maximum_fusion.5
  59.4 1.6 %collective-permute-start.8 = (f16[304,128]{1,0:T(8,128)(2,1)S(1)}, f16[304,128]{1,0:T(8,128)(2,1)S(1)}, u32[]{:S(2)}, u32[]{:S(2)}) collective-permute-start(f16[304,128]{1,0:T(8,128)(2,1)S(1)} %get-tuple-element.42), channel_id=1, source_target_pairs={{0,4},{1,5},{2,6},{3,7},{4,0},{5,1},{6,2},{7,3},{8,12},{9,13},{10,... | collective-permute-start | bytes 233480 | tf_op jit(solution)/shard_map/ppermute | solution.py:318
  61.0 4.7 %collective-permute-start.9 = (f16[304,128]{1,0:T(8,128)(2,1)S(1)}, f16[304,128]{1,0:T(8,128)(2,1)S(1)}, u32[]{:S(2)}, u32[]{:S(2)}) collective-permute-start(f16[304,128]{1,0:T(8,128)(2,1)S(1)} %get-tuple-element.43), channel_id=1, source_target_pairs={{0,2},{1,3},{2,0},{3,1},{4,6},{5,7},{6,4},{7,5},{8,10},{9,11},{10,... | collective-permute-start | bytes 233480 | tf_op jit(solution)/shard_map/ppermute | solution.py:318
  65.7 3.1 %output.1 = bf16[4,16,64,128]{3,2,1,0:T(8,128)(2,1)} custom-call(s32[1]{0:T(128)} %bitcast.parity, bf16[4,8,64,256]{3,2,1,0:T(8,128)(2,1)S(1)} %bitcast.95, bf16[2,4,64,128]{3,2,1,0:T(8,128)(2,1)S(1)} %collective-permute-done.11.first, bf16[2,4,64,128]{3,2,1,0:T(8,128)(2,1)S(1)} %collective-permute-done.12.second, bf16[3,3,128,128]{3,2,1,0:T(8,128)(2,1)S(1)} %copy-done.15, ...), custom_call_target="tpu_custom_call" | custom-call | flops 1610612736 | bytes 4194304 | tf_op jit(solution)/shard_map/output/pallas_call | solution.py:297
  68.9 2.1 %collective-permute-done.10 = f16[304,128]{1,0:T(8,128)(2,1)S(1)} collective-permute-done((f16[304,128]{1,0:T(8,128)(2,1)S(1)}, f16[304,128]{1,0:T(8,128)(2,1)S(1)}, u32[]{:S(2)}, u32[]{:S(2)}) %collective-permute-start.10) | collective-permute-done | bytes 77856 | tf_op jit(solution)/shard_map/ppermute | solution.py:318
  71.1 3.6 %collective-permute-start.13 = (f16[304,128]{1,0:T(8,128)(2,1)S(1)}, f16[304,128]{1,0:T(8,128)(2,1)S(1)}, u32[]{:S(2)}, u32[]{:S(2)}) collective-permute-start(f16[304,128]{1,0:T(8,128)(2,1)S(1)} %pad_maximum_fusion.4), channel_id=1, source_target_pairs={{0,8},{1,9},{2,10},{3,11},{4,12},{5,13},{6,14},{7,15},{8,0},{9,1},... | collective-permute-start | bytes 233480 | tf_op jit(solution)/shard_map/ppermute | solution.py:318
  74.7 1.7 %collective-permute-start.14 = (f16[304,128]{1,0:T(8,128)(2,1)S(1)}, f16[304,128]{1,0:T(8,128)(2,1)S(1)}, u32[]{:S(2)}, u32[]{:S(2)}) collective-permute-start(f16[304,128]{1,0:T(8,128)(2,1)S(1)} %pad_maximum_fusion.4), channel_id=1, source_target_pairs={{0,16},{1,17},{2,18},{3,19},{4,20},{5,21},{6,22},{7,23},{8,24},{9,... | collective-permute-start | bytes 233480 | tf_op jit(solution)/shard_map/ppermute | solution.py:318
  76.4 1.4 %collective-permute-start.15 = (f16[304,128]{1,0:T(8,128)(2,1)S(1)}, f16[304,128]{1,0:T(8,128)(2,1)S(1)}, u32[]{:S(2)}, u32[]{:S(2)}) collective-permute-start(f16[304,128]{1,0:T(8,128)(2,1)S(1)} %pad_maximum_fusion.4), channel_id=1, source_target_pairs={{0,24},{1,25},{2,26},{3,27},{4,28},{5,29},{6,30},{7,31},{8,16},{9,... | collective-permute-start | bytes 233480 | tf_op jit(solution)/shard_map/ppermute | solution.py:318
  77.8 3.0 %grad_frames.1 = bf16[4,16,64,128]{3,2,1,0:T(8,128)(2,1)} custom-call(s32[1]{0:T(128)} %bitcast.parity, bf16[4,8,64,256]{3,2,1,0:T(8,128)(2,1)S(1)} %bitcast.94, bf16[2,4,64,128]{3,2,1,0:T(8,128)(2,1)S(1)} %collective-permute-done.11.first, bf16[2,4,64,128]{3,2,1,0:T(8,128)(2,1)S(1)} %collective-permute-done.12.second, ...), custom_call_target="tpu_custom_call" | custom-call | flops 1610612736 | bytes 4194304 | tf_op jit(solution)/shard_map/grad_frames/pallas_call | solution.py:297
  80.9 2.0 %collective-permute-done.14 = f16[304,128]{1,0:T(8,128)(2,1)S(1)} collective-permute-done((f16[304,128]{1,0:T(8,128)(2,1)S(1)}, f16[304,128]{1,0:T(8,128)(2,1)S(1)}, u32[]{:S(2)}, u32[]{:S(2)}) %collective-permute-start.14) | collective-permute-done | bytes 77856 | tf_op jit(solution)/shard_map/ppermute | solution.py:318
  83.1 1.9 %collective-permute-start.18 = (f16[304,128]{1,0:T(8,128)(2,1)S(1)}, f16[304,128]{1,0:T(8,128)(2,1)S(1)}, u32[]{:S(2)}, u32[]{:S(2)}) collective-permute-start(f16[304,128]{1,0:T(8,128)(2,1)S(1)} %pad_maximum_fusion.3), channel_id=1, source_target_pairs={{0,4},{1,5},{2,6},{3,7},{4,0},{5,1},{6,2},{7,3},{8,12},{9,13},{10,... | collective-permute-start | bytes 233480 | tf_op jit(solution)/shard_map/ppermute | solution.py:318
  85.0 1.6 %collective-permute-start.17 = (f16[304,128]{1,0:T(8,128)(2,1)S(1)}, f16[304,128]{1,0:T(8,128)(2,1)S(1)}, u32[]{:S(2)}, u32[]{:S(2)}) collective-permute-start(f16[304,128]{1,0:T(8,128)(2,1)S(1)} %pad_maximum_fusion.3), channel_id=1, source_target_pairs={{0,2},{1,3},{2,0},{3,1},{4,6},{5,7},{6,4},{7,5},{8,10},{9,11},{10,... | collective-permute-start | bytes 233480 | tf_op jit(solution)/shard_map/ppermute | solution.py:318
  86.6 1.7 %collective-permute-done.18 = f16[304,128]{1,0:T(8,128)(2,1)S(1)} collective-permute-done((f16[304,128]{1,0:T(8,128)(2,1)S(1)}, f16[304,128]{1,0:T(8,128)(2,1)S(1)}, u32[]{:S(2)}, u32[]{:S(2)}) %collective-permute-start.18) | collective-permute-done | bytes 77856 | tf_op jit(solution)/shard_map/ppermute | solution.py:318
  88.4 2.0 %collective-permute-done.16 = f16[304,128]{1,0:T(8,128)(2,1)S(1)} collective-permute-done((f16[304,128]{1,0:T(8,128)(2,1)S(1)}, f16[304,128]{1,0:T(8,128)(2,1)S(1)}, u32[]{:S(2)}, u32[]{:S(2)}) %collective-permute-start.16) | collective-permute-done | bytes 77856 | tf_op jit(solution)/shard_map/ppermute | solution.py:318
  90.3 0.4 collective-permute-done.17
  90.8 0.1 broadcast_select_fusion.3
  90.9 0.1 pad_maximum_fusion.2
  91.0 0.1 collective-permute-start.19
  91.1 1.6 %collective-permute-done.19 = f16[1216,128]{1,0:T(8,128)(2,1)S(1)} collective-permute-done((f16[1216,128]{1,0:T(8,128)(2,1)S(1)}, f16[1216,128]{1,0:T(8,128)(2,1)S(1)}, u32[]{:S(2)}, u32[]{:S(2)}) %collective-permute-start.19) | collective-permute-done | bytes 311328 | tf_op jit(solution)/shard_map/ppermute | solution.py:318
  92.7 0.2 broadcast_select_fusion
  92.9 0.9 fusion
  93.8 0.9 fusion.1
  (94 shorter events, 1.3 us)
Async XLA Ops:
  1.6 1.5 %collective-permute-start = (bf16[2,4,64,128]{3,2,1,0:T(8,128)(2,1)S(1)}, bf16[2,4,64,128]{3,2,1,0:T(8,128)(2,1)S(1)}, u32[]{:S(2)}, u32[]{:S(2)}) collective-permute-start(bf16[2,4,64,128]{3,2,1,0:T(8,128)(2,1)S(1)} %get-tuple-element.111), channel_id=1, source_target_pairs={{0,1},{1,0},{2,3},{3,2},{4,5},{5,4},{6,7},{7,6},{8,9},{9,8},{10,11... | collective-permute-start | bytes 393224 | tf_op jit(solution)/shard_map/ppermute | solution.py:318
  2.2 1.0 %collective-permute-start.1 = (bf16[2,4,64,128]{3,2,1,0:T(8,128)(2,1)S(1)}, bf16[2,4,64,128]{3,2,1,0:T(8,128)(2,1)S(1)}, u32[]{:S(2)}, u32[]{:S(2)}) collective-permute-start(bf16[2,4,64,128]{3,2,1,0:T(8,128)(2,1)S(1)} %get-tuple-element.110), channel_id=1, source_target_pairs={{1,2},{2,1},{5,6},{6,5},{9,10},{10,9},{13,14},{14,13},{17,18},{18,... | collective-permute-start | bytes 393224 | tf_op jit(solution)/shard_map/ppermute | solution.py:326
  3.2 1.2 %copy-start.4 = (bf16[4,16,64,128]{3,2,1,0:T(8,128)(2,1)S(1)}, bf16[4,16,64,128]{3,2,1,0:T(8,128)(2,1)}, u32[]{:S(2)}) copy-start(bf16[4,16,64,128]{3,2,1,0:T(8,128)(2,1)} %direct.2) | copy-start | bytes 3145732
  4.4 1.2 %copy-start.6 = (bf16[4,16,64,128]{3,2,1,0:T(8,128)(2,1)S(1)}, bf16[4,16,64,128]{3,2,1,0:T(8,128)(2,1)}, u32[]{:S(2)}) copy-start(bf16[4,16,64,128]{3,2,1,0:T(8,128)(2,1)} %direct.3) | copy-start | bytes 3145732
  5.6 0.7 copy-start.8
  6.3 1.0 %copy-start.14 = (bf16[3,3,128,128]{3,2,1,0:T(8,128)(2,1)S(1)}, bf16[3,3,128,128]{3,2,1,0:T(8,128)(2,1)}, u32[]{:S(2)}) copy-start(bf16[3,3,128,128]{3,2,1,0:T(8,128)(2,1)} %weight.2) | copy-start | bytes 884740
  7.3 1.0 %copy-start.16 = (bf16[3,3,128,128]{3,2,1,0:T(8,128)(2,1)S(1)}, bf16[3,3,128,128]{3,2,1,0:T(8,128)(2,1)}, u32[]{:S(2)}) copy-start(bf16[3,3,128,128]{3,2,1,0:T(8,128)(2,1)} %weight.3) | copy-start | bytes 884740
  14.3 1.8 %copy-start = (bf16[3,4,576,256]{3,2,1,0:T(8,128)(2,1)}, bf16[3,4,576,256]{3,2,1,0:T(8,128)(2,1)S(1)}, u32[]{:S(2)}) copy-start(bf16[3,4,576,256]{3,2,1,0:T(8,128)(2,1)S(1)} %get-tuple-element.33.frame_taps) | copy-start | bytes 10616836
  16.1 1.4 %copy-start.2 = (f32[4,512,256]{2,1,0:T(8,128)}, f32[4,512,256]{2,1,0:T(8,128)S(1)}, u32[]{:S(2)}) copy-start(f32[4,512,256]{2,1,0:T(8,128)S(1)} %get-tuple-element.30.adjoints) | copy-start | bytes 6291460
  17.7 7.4 %collective-permute-start.2 = (f16[528,256]{1,0:T(8,128)(2,1)S(1)}, f16[528,256]{1,0:T(8,128)(2,1)S(1)}, u32[]{:S(2)}, u32[]{:S(2)}) collective-permute-start(f16[528,256]{1,0:T(8,128)(2,1)S(1)} %maximum_maximum_fusion), channel_id=1, source_target_pairs={{0,4},{1,5},{2,6},{3,7},{4,0},{5,1},{6,2},{7,3},{8,12},{9,13},{10,... | collective-permute-start | bytes 811016 | tf_op jit(solution)/shard_map/ppermute | solution.py:318
  25.6 7.7 %collective-permute-start.3 = (f16[272,256]{1,0:T(8,128)(2,1)S(1)}, f16[272,256]{1,0:T(8,128)(2,1)S(1)}, u32[]{:S(2)}, u32[]{:S(2)}) collective-permute-start(f16[272,256]{1,0:T(8,128)(2,1)S(1)} %concatenate.56), channel_id=1, source_target_pairs={{0,16},{1,17},{2,18},{3,19},{4,20},{5,21},{6,22},{7,23},{8,24},{9,... | collective-permute-start | bytes 417800 | tf_op jit(solution)/shard_map/ppermute | solution.py:318
  28.9 7.8 %collective-permute-start.4 = (f16[272,256]{1,0:T(8,128)(2,1)S(1)}, f16[272,256]{1,0:T(8,128)(2,1)S(1)}, u32[]{:S(2)}, u32[]{:S(2)}) collective-permute-start(f16[272,256]{1,0:T(8,128)(2,1)S(1)} %concatenate.56), channel_id=1, source_target_pairs={{0,24},{1,25},{2,26},{3,27},{4,28},{5,29},{6,30},{7,31},{8,16},{9,... | collective-permute-start | bytes 417800 | tf_op jit(solution)/shard_map/ppermute | solution.py:318
  30.5 7.3 %collective-permute-start.5 = (f16[272,256]{1,0:T(8,128)(2,1)S(1)}, f16[272,256]{1,0:T(8,128)(2,1)S(1)}, u32[]{:S(2)}, u32[]{:S(2)}) collective-permute-start(f16[272,256]{1,0:T(8,128)(2,1)S(1)} %concatenate.57), channel_id=1, source_target_pairs={{0,8},{1,9},{2,10},{3,11},{4,12},{5,13},{6,14},{7,15},{8,0},{9,1},... | collective-permute-start | bytes 417800 | tf_op jit(solution)/shard_map/ppermute | solution.py:318
  38.2 7.3 %copy-start.3 = (f32[4,512,256]{2,1,0:T(8,128)S(1)}, f32[4,512,256]{2,1,0:T(8,128)}, u32[]{:S(2)}) copy-start(f32[4,512,256]{2,1,0:T(8,128)} %copy-done.2) | copy-start | bytes 6291460
  38.4 6.8 %collective-permute-start.6 = (f16[528,256]{1,0:T(8,128)(2,1)S(1)}, f16[528,256]{1,0:T(8,128)(2,1)S(1)}, u32[]{:S(2)}, u32[]{:S(2)}) collective-permute-start(f16[528,256]{1,0:T(8,128)(2,1)S(1)} %maximum_maximum_fusion.1), channel_id=1, source_target_pairs={{0,4},{1,5},{2,6},{3,7},{4,0},{5,1},{6,2},{7,3},{8,12},{9,13},{10,... | collective-permute-start | bytes 811016 | tf_op jit(solution)/shard_map/ppermute | solution.py:318
  45.3 2.0 %copy-start.1 = (bf16[3,4,576,256]{3,2,1,0:T(8,128)(2,1)S(1)}, bf16[3,4,576,256]{3,2,1,0:T(8,128)(2,1)}, u32[]{:S(2)}) copy-start(bf16[3,4,576,256]{3,2,1,0:T(8,128)(2,1)} %copy-done) | copy-start | bytes 10616836
  45.3 2.0 %copy-start.9 = (f32[4,128]{1,0:T(4,128)S(1)}, f32[4,128]{1,0:T(4,128)}, u32[]{:S(2)}) copy-start(f32[4,128]{1,0:T(4,128)} %log_decay.3) | copy-start | bytes 6148
  53.0 1.0 %copy-start.10 = (bf16[4,512,256]{2,1,0:T(8,128)(2,1)}, bf16[4,512,256]{2,1,0:T(8,128)(2,1)S(1)}, u32[]{:S(2)}) copy-start(bf16[4,512,256]{2,1,0:T(8,128)(2,1)S(1)} %get-tuple-element.48) | copy-start | bytes 3145732
  54.0 1.0 %copy-start.12 = (bf16[4,512,256]{2,1,0:T(8,128)(2,1)}, bf16[4,512,256]{2,1,0:T(8,128)(2,1)S(1)}, u32[]{:S(2)}) copy-start(bf16[4,512,256]{2,1,0:T(8,128)(2,1)S(1)} %get-tuple-element.41) | copy-start | bytes 3145732
  55.4 3.7 %collective-permute-start.7 = (f16[1168,128]{1,0:T(8,128)(2,1)S(1)}, f16[1168,128]{1,0:T(8,128)(2,1)S(1)}, u32[]{:S(2)}, u32[]{:S(2)}) collective-permute-start(f16[1168,128]{1,0:T(8,128)(2,1)S(1)} %concatenate.61), channel_id=1, source_target_pairs={{0,1},{1,0},{2,3},{3,2},{4,5},{5,4},{6,7},{7,6},{8,9},{9,8},{10,11... | collective-permute-start | bytes 897032 | tf_op jit(solution)/shard_map/ppermute | solution.py:318
  57.9 7.8 %copy-start.5 = (bf16[4,16,64,128]{3,2,1,0:T(8,128)(2,1)S(1)}, bf16[4,16,64,128]{3,2,1,0:T(8,128)(2,1)}, u32[]{:S(2)}) copy-start(bf16[4,16,64,128]{3,2,1,0:T(8,128)(2,1)} %direct.2) | copy-start | bytes 3145732
  57.9 7.8 %copy-start.13 = (bf16[4,512,256]{2,1,0:T(8,128)(2,1)S(1)}, bf16[4,512,256]{2,1,0:T(8,128)(2,1)}, u32[]{:S(2)}) copy-start(bf16[4,512,256]{2,1,0:T(8,128)(2,1)} %copy-done.12) | copy-start | bytes 3145732
  57.9 7.8 %copy-start.15 = (bf16[3,3,128,128]{3,2,1,0:T(8,128)(2,1)S(1)}, bf16[3,3,128,128]{3,2,1,0:T(8,128)(2,1)}, u32[]{:S(2)}) copy-start(bf16[3,3,128,128]{3,2,1,0:T(8,128)(2,1)} %weight.2) | copy-start | bytes 884740
  57.9 7.8 %copy-start.18 = (f32[128]{0:T(128)S(1)}, f32[128]{0:T(128)}, u32[]{:S(2)}) copy-start(f32[128]{0:T(128)} %param.10) | copy-start | bytes 1540
  57.9 7.8 %collective-permute-start.11 = (bf16[2,4,64,128]{3,2,1,0:T(8,128)(2,1)S(1)}, bf16[2,4,64,128]{3,2,1,0:T(8,128)(2,1)S(1)}, u32[]{:S(2)}, u32[]{:S(2)}) collective-permute-start(bf16[2,4,64,128]{3,2,1,0:T(8,128)(2,1)S(1)} %get-tuple-element.46), channel_id=1, source_target_pairs={{0,1},{1,0},{2,3},{3,2},{4,5},{5,4},{6,7},{7,6},{8,9},{9,8},{10,11... | collective-permute-start | bytes 393224 | tf_op jit(solution)/shard_map/ppermute | solution.py:318
  58.1 7.6 %collective-permute-start.12 = (bf16[2,4,64,128]{3,2,1,0:T(8,128)(2,1)S(1)}, bf16[2,4,64,128]{3,2,1,0:T(8,128)(2,1)S(1)}, u32[]{:S(2)}, u32[]{:S(2)}) collective-permute-start(bf16[2,4,64,128]{3,2,1,0:T(8,128)(2,1)S(1)} %get-tuple-element.47), channel_id=1, source_target_pairs={{1,2},{2,1},{5,6},{6,5},{9,10},{10,9},{13,14},{14,13},{17,18},{18,... | collective-permute-start | bytes 393224 | tf_op jit(solution)/shard_map/ppermute | solution.py:326
  59.4 9.4 %collective-permute-start.8 = (f16[304,128]{1,0:T(8,128)(2,1)S(1)}, f16[304,128]{1,0:T(8,128)(2,1)S(1)}, u32[]{:S(2)}, u32[]{:S(2)}) collective-permute-start(f16[304,128]{1,0:T(8,128)(2,1)S(1)} %get-tuple-element.42), channel_id=1, source_target_pairs={{0,4},{1,5},{2,6},{3,7},{4,0},{5,1},{6,2},{7,3},{8,12},{9,13},{10,... | collective-permute-start | bytes 233480 | tf_op jit(solution)/shard_map/ppermute | solution.py:318
  61.0 7.8 %collective-permute-start.9 = (f16[304,128]{1,0:T(8,128)(2,1)S(1)}, f16[304,128]{1,0:T(8,128)(2,1)S(1)}, u32[]{:S(2)}, u32[]{:S(2)}) collective-permute-start(f16[304,128]{1,0:T(8,128)(2,1)S(1)} %get-tuple-element.43), channel_id=1, source_target_pairs={{0,2},{1,3},{2,0},{3,1},{4,6},{5,7},{6,4},{7,5},{8,10},{9,11},{10,... | collective-permute-start | bytes 233480 | tf_op jit(solution)/shard_map/ppermute | solution.py:318
  65.7 5.3 %collective-permute-start.10 = (f16[304,128]{1,0:T(8,128)(2,1)S(1)}, f16[304,128]{1,0:T(8,128)(2,1)S(1)}, u32[]{:S(2)}, u32[]{:S(2)}) collective-permute-start(f16[304,128]{1,0:T(8,128)(2,1)S(1)} %get-tuple-element.44), channel_id=1, source_target_pairs={{0,6},{1,7},{2,4},{3,5},{4,2},{5,3},{6,0},{7,1},{8,14},{9,15},{10,... | collective-permute-start | bytes 233480 | tf_op jit(solution)/shard_map/ppermute | solution.py:318
  65.7 12.1 %copy-start.7 = (bf16[4,16,64,128]{3,2,1,0:T(8,128)(2,1)S(1)}, bf16[4,16,64,128]{3,2,1,0:T(8,128)(2,1)}, u32[]{:S(2)}) copy-start(bf16[4,16,64,128]{3,2,1,0:T(8,128)(2,1)} %direct.3) | copy-start | bytes 3145732
  65.7 12.1 %copy-start.11 = (bf16[4,512,256]{2,1,0:T(8,128)(2,1)S(1)}, bf16[4,512,256]{2,1,0:T(8,128)(2,1)}, u32[]{:S(2)}) copy-start(bf16[4,512,256]{2,1,0:T(8,128)(2,1)} %copy-done.10) | copy-start | bytes 3145732
  65.7 12.1 %copy-start.17 = (bf16[3,3,128,128]{3,2,1,0:T(8,128)(2,1)S(1)}, bf16[3,3,128,128]{3,2,1,0:T(8,128)(2,1)}, u32[]{:S(2)}) copy-start(bf16[3,3,128,128]{3,2,1,0:T(8,128)(2,1)} %weight.3) | copy-start | bytes 884740
  71.1 9.8 %collective-permute-start.13 = (f16[304,128]{1,0:T(8,128)(2,1)S(1)}, f16[304,128]{1,0:T(8,128)(2,1)S(1)}, u32[]{:S(2)}, u32[]{:S(2)}) collective-permute-start(f16[304,128]{1,0:T(8,128)(2,1)S(1)} %pad_maximum_fusion.4), channel_id=1, source_target_pairs={{0,8},{1,9},{2,10},{3,11},{4,12},{5,13},{6,14},{7,15},{8,0},{9,1},... | collective-permute-start | bytes 233480 | tf_op jit(solution)/shard_map/ppermute | solution.py:318
  74.7 8.2 %collective-permute-start.14 = (f16[304,128]{1,0:T(8,128)(2,1)S(1)}, f16[304,128]{1,0:T(8,128)(2,1)S(1)}, u32[]{:S(2)}, u32[]{:S(2)}) collective-permute-start(f16[304,128]{1,0:T(8,128)(2,1)S(1)} %pad_maximum_fusion.4), channel_id=1, source_target_pairs={{0,16},{1,17},{2,18},{3,19},{4,20},{5,21},{6,22},{7,23},{8,24},{9,... | collective-permute-start | bytes 233480 | tf_op jit(solution)/shard_map/ppermute | solution.py:318
  76.4 6.5 %collective-permute-start.15 = (f16[304,128]{1,0:T(8,128)(2,1)S(1)}, f16[304,128]{1,0:T(8,128)(2,1)S(1)}, u32[]{:S(2)}, u32[]{:S(2)}) collective-permute-start(f16[304,128]{1,0:T(8,128)(2,1)S(1)} %pad_maximum_fusion.4), channel_id=1, source_target_pairs={{0,24},{1,25},{2,26},{3,27},{4,28},{5,29},{6,30},{7,31},{8,16},{9,... | collective-permute-start | bytes 233480 | tf_op jit(solution)/shard_map/ppermute | solution.py:318
  83.1 5.3 %collective-permute-start.18 = (f16[304,128]{1,0:T(8,128)(2,1)S(1)}, f16[304,128]{1,0:T(8,128)(2,1)S(1)}, u32[]{:S(2)}, u32[]{:S(2)}) collective-permute-start(f16[304,128]{1,0:T(8,128)(2,1)S(1)} %pad_maximum_fusion.3), channel_id=1, source_target_pairs={{0,4},{1,5},{2,6},{3,7},{4,0},{5,1},{6,2},{7,3},{8,12},{9,13},{10,... | collective-permute-start | bytes 233480 | tf_op jit(solution)/shard_map/ppermute | solution.py:318
  85.0 5.4 %collective-permute-start.16 = (f16[304,128]{1,0:T(8,128)(2,1)S(1)}, f16[304,128]{1,0:T(8,128)(2,1)S(1)}, u32[]{:S(2)}, u32[]{:S(2)}) collective-permute-start(f16[304,128]{1,0:T(8,128)(2,1)S(1)} %pad_maximum_fusion.3), channel_id=1, source_target_pairs={{0,6},{1,7},{2,4},{3,5},{4,2},{5,3},{6,0},{7,1},{8,14},{9,15},{10,... | collective-permute-start | bytes 233480 | tf_op jit(solution)/shard_map/ppermute | solution.py:318
  85.0 5.7 %collective-permute-start.17 = (f16[304,128]{1,0:T(8,128)(2,1)S(1)}, f16[304,128]{1,0:T(8,128)(2,1)S(1)}, u32[]{:S(2)}, u32[]{:S(2)}) collective-permute-start(f16[304,128]{1,0:T(8,128)(2,1)S(1)} %pad_maximum_fusion.3), channel_id=1, source_target_pairs={{0,2},{1,3},{2,0},{3,1},{4,6},{5,7},{6,4},{7,5},{8,10},{9,11},{10,... | collective-permute-start | bytes 233480 | tf_op jit(solution)/shard_map/ppermute | solution.py:318
  91.0 1.7 %collective-permute-start.19 = (f16[1216,128]{1,0:T(8,128)(2,1)S(1)}, f16[1216,128]{1,0:T(8,128)(2,1)S(1)}, u32[]{:S(2)}, u32[]{:S(2)}) collective-permute-start(f16[1216,128]{1,0:T(8,128)(2,1)S(1)} %pad_maximum_fusion.2), channel_id=1, source_target_pairs={{0,1},{1,0},{2,3},{3,2},{4,5},{5,4},{6,7},{7,6},{8,9},{9,8},{10,11... | collective-permute-start | bytes 933896 | tf_op jit(solution)/shard_map/ppermute | solution.py:318

commit v3 on v2

--- a/solution.py
+++ b/solution.py
@@ -10,7 +10,7 @@
 
 F32 = jnp.float32
 BF16 = jnp.bfloat16
-VMEM_LIMIT = 40 * 1024 * 1024
+VMEM_LIMIT = 24 * 1024 * 1024
 
 
 def fill_pairs(pairs, field, top, bottom):
@@ -98,14 +98,29 @@
     return rate, reach, tail
 
 
+def blocks_kernel(frames, cotangent, w_in, w_out, log_decay, blocks):
+    fill_weights(blocks.at[0], w_in, False)
+    fill_weights(blocks.at[1], w_out, True)
+
+
+def blocks_call(frames, cotangent, w_in, w_out, log_decay):
+    ch = w_in.shape[2]
+    return pl.pallas_call(
+        blocks_kernel,
+        out_shape=jax.ShapeDtypeStruct((2, 3, 2, 2 * ch, 2 * ch), BF16),
+        compiler_params=pltpu.CompilerParams(vmem_limit_bytes=VMEM_LIMIT),
+        cost_estimate=pl.CostEstimate(flops=0, bytes_accessed=10 << 20, transcendentals=0),
+        name="blocks",
+    )(frames, cotangent, w_in, w_out, log_decay)
+
+
 def drive_kernel(
-    parity,
+    place,
     frames,
     cotangent,
     first,
     second,
-    w_in,
-    w_out,
+    blocks,
     log_decay,
     states,
     adjoints,
@@ -114,17 +129,15 @@
     cot_taps,
     info,
     pairs,
-    blocks,
 ):
     times, rows, cols, ch = frames.shape
     half = rows // 2
-    odd = parity[0] == 1
+    odd = lax.rem(place[0], 2) == 1
     rate, reach, _ = decays(log_decay[...])
-    fields = ((frames, w_in, states, frame_taps), (cotangent, w_out, adjoints, cot_taps))
-    for index, (field, weight, result, taps_out) in enumerate(fields):
+    fields = ((frames, states, frame_taps), (cotangent, adjoints, cot_taps))
+    for index, (field, result, taps_out) in enumerate(fields):
         flip = index == 1
         top, bottom = pick_halos(first, second, index, odd, times)
-        fill_weights(blocks.at[index], weight, flip)
         fill_pairs(pairs.at[index], field, top, bottom)
         carry = None
         for step in range(times):
@@ -152,40 +165,43 @@
     info[2:3, :] = high
     info[3:4, :] = middle
     info[4:5, :] = low
-    info[5:, :] = jnp.zeros((info.shape[0] - 5, 2 * ch), F32)
-
-
-def drive_call(parity, frames, cotangent, first, second, w_in, w_out, log_decay):
+    row = jnp.zeros((1, 2 * ch), F32)
+    info[5:6, :] = row + lax.rem(place[1], 2).astype(F32)
+    for d in range(info.shape[0] - 6):
+        info[6 + d : 7 + d, :] = row + (lax.div(place[1], 2) ^ d).astype(F32)
+
+
+def drive_call(place, frames, cotangent, first, second, blocks, log_decay):
     times, rows, cols, ch = frames.shape
     half = rows // 2
     field = jax.ShapeDtypeStruct((times, half * cols, 2 * ch), F32)
+    rows_info = (6 + lax.axis_size("tm") // 2 + 15) // 16 * 16
     taps = jax.ShapeDtypeStruct((3, times, (half + 1) * cols, 2 * ch), BF16)
     return pl.pallas_call(
         drive_kernel,
         in_specs=[pl.BlockSpec(memory_space=pltpu.SMEM)]
-        + [pl.BlockSpec(memory_space=pltpu.VMEM)] * 7,
+        + [pl.BlockSpec(memory_space=pltpu.VMEM)] * 6,
         out_shape=(
             field,
             field,
             jax.ShapeDtypeStruct(field.shape[1:], F32),
             taps,
             taps,
-            jax.ShapeDtypeStruct((16, 2 * ch), F32),
+            jax.ShapeDtypeStruct((rows_info, 2 * ch), F32),
         ),
         scratch_shapes=[
             pltpu.VMEM((2, times, half + 1, cols, 2 * ch), BF16),
-            pltpu.VMEM((2, 3, 2, 2 * ch, 2 * ch), BF16),
         ],
         compiler_params=pltpu.CompilerParams(vmem_limit_bytes=VMEM_LIMIT),
         cost_estimate=pl.CostEstimate(
             flops=times * rows * cols * ch * ch * 48, bytes_accessed=12 << 20, transcendentals=0
         ),
         name="drive",
-    )(parity, frames, cotangent, first, second, w_in, w_out, log_decay)
+    )(place, frames, cotangent, first, second, blocks, log_decay)
 
 
 def grads_kernel(
-    parity,
+    place,
     states,
     adjoints,
     state_in,
@@ -205,7 +221,7 @@
     times, count, width = states.shape
     ch = width // 2
     cols = frame_taps.shape[2] - count
-    odd = parity[0] == 1
+    odd = lax.rem(place[0], 2) == 1
     rate, reach, tail = decays(log_decay[...])
     add = state_in[...]
     back = adjoint_in[...]
@@ -244,17 +260,22 @@
                             part = blocks[b][a * ch : (a + 1) * ch, c * ch : (c + 1) * ch]
                             total = part if total is None else total + part
                 if index == 0:
-                    place = (2 - tap) * 3 + 2 - j
+                    spot = (2 - tap) * 3 + 2 - j
                 else:
-                    place = tap * 3 + j
+                    spot = tap * 3 + j
                     total = total.T
-                grads[place * ch : (place + 1) * ch, :] = total
+                grads[spot * ch : (spot + 1) * ch, :] = total
                 top = jnp.max(jnp.abs(total), axis=0, keepdims=True)
                 largest = top if largest is None else jnp.maximum(largest, top)
-        info[index * 8 : index * 8 + 8, :] = jnp.broadcast_to(exponent(largest), (8, ch))
-
-
-def grads_call(parity, states, adjoints, state_in, adjoint_in, log_decay, frame_taps, cot_taps):
+        info[index : index + 1, :] = exponent(largest)
+    row = jnp.zeros((1, ch), F32)
+    info[2:3, :] = row + lax.rem(place[0], 2).astype(F32)
+    info[3:4, :] = row + lax.rem(place[1], 2).astype(F32)
+    info[4:5, :] = row + lax.rem(lax.div(place[0], 2), 2).astype(F32)
+    info[5:, :] = jnp.zeros((info.shape[0] - 5, ch), F32)
+
+
+def grads_call(place, states, adjoints, state_in, adjoint_in, log_decay, frame_taps, cot_taps):
     times, count, width = states.shape
     ch = width // 2
     cols = frame_taps.shape[2] - count
@@ -272,14 +293,14 @@
             flops=times * count * ch * ch * 96, bytes_accessed=12 << 20, transcendentals=0
         ),
         name="grads",
-    )(parity, states, adjoints, state_in, adjoint_in, log_decay, frame_taps, cot_taps)
-
-
-def output_kernel(parity, field, first, second, weight, skip, direct, out, pairs, blocks, *, flip):
+    )(place, states, adjoints, state_in, adjoint_in, log_decay, frame_taps, cot_taps)
+
+
+def output_kernel(place, field, first, second, weight, skip, direct, out, pairs, blocks, *, flip):
     times, half, cols, width = field.shape
     ch = width // 2
     fill_weights(blocks, weight, flip)
-    top, bottom = pick_halos(first, second, int(flip), parity[0] == 1, times)
+    top, bottom = pick_halos(first, second, int(flip), lax.rem(place[0], 2) == 1, times)
     fill_pairs_from_pairs(pairs, field, top, bottom)
     gain = skip[...]
     for t in range(times):
@@ -291,7 +312,7 @@
                 out[t, 2 * i + c] = (value[i, :, c * ch : (c + 1) * ch] + base).astype(BF16)
 
 
-def output_call(parity, field, first, second, weight, skip, direct, flip):
+def output_call(place, field, first, second, weight, skip, direct, flip):
     times, half, cols, width = field.shape
     ch = width // 2
     return pl.pallas_call(
@@ -308,7 +329,7 @@
             flops=times * half * cols * ch * ch * 48, bytes_accessed=4 << 20, transcendentals=0
         ),
         name="grad_frames" if flip else "output",
-    )(parity, field, first, second, weight, skip, direct)
+    )(place, field, first, second, weight, skip, direct)
 
 
 def swap(value, tm_bits, tile_bits):
@@ -326,9 +347,19 @@
     return lax.ppermute(value, "tile", pairs)
 
 
-def packed(value, scale, rows):
-    pad = jnp.zeros((16 - rows.shape[0], rows.shape[1]), F32)
-    return jnp.concatenate([value * jnp.exp2(-scale), rows, pad], 0).astype(jnp.float16)
+def laid(parts, count):
+    total, start = None, 0
+    for part in parts:
+        end = count - start - part.shape[0]
+        wide = jnp.pad(part, ((start, end), (0, 0)))
+        total = wide if total is None else total + wide
+        start += part.shape[0]
+    return total
+
+
+def packed(value, scale, *rows):
+    parts = [value * jnp.exp2(-scale), *rows]
+    return laid(parts, value.shape[0] + 16).astype(jnp.float16)
 
 
 def whole_decay(rows):
@@ -337,19 +368,17 @@
 
 def carry_over(state_end, adjoint_end, info):
     count = lax.axis_size("tm")
-    place = lax.axis_index("tm")
-    odd = place % 2 == 1
-    pair_place = place // 2
+    odd = info[5:6] > 0.5
+    places = [info[6 + d : 7 + d] for d in range(count // 2)]
     half = state_end.shape[0] // 2
 
     def both(low, high, scale_low, scale_high, rows):
-        pad = jnp.zeros((16 - rows.shape[0], rows.shape[1]), F32)
-        return jnp.concatenate(
-            [low * jnp.exp2(-scale_low), high * jnp.exp2(-scale_high), rows, pad], 0
-        ).astype(jnp.float16)
+        parts = [low * jnp.exp2(-scale_low), high * jnp.exp2(-scale_high), rows]
+        return laid(parts, 2 * half + 16).astype(jnp.float16)
 
     def give(value, mine):
-        return jnp.where(odd == mine, value[half:], value[:half])
+        low, high = value[:half], value[half:]
+        return jnp.where(odd, high, low) if mine else jnp.where(odd, low, high)
 
     got = swap(
         both(give(state_end, False), give(adjoint_end, False), info[0:1], info[1:2], info[:5]), 1, 0
@@ -373,10 +402,10 @@
     messages = []
     bit = 1
     while bit < count // 2:
-        later = (pair_place // bit) % 2 == 1
+        later = places[bit] < places[0]
         scale = jnp.where(later, adjoint_scale, state_scale)
-        rows = jnp.concatenate([scale, info[2:5], their_info[2:5]], 0)
-        messages.append(packed(jnp.where(later, adjoint_pair, state_pair), scale, rows))
+        value = jnp.where(later, adjoint_pair, state_pair)
+        messages.append(packed(value, scale, scale, info[2:5], their_info[2:5]))
         bit *= 2
     received = {}
     for d in range(1, count // 2):
@@ -391,17 +420,15 @@
     state_before = jnp.zeros_like(state_pair)
     adjoint_after = jnp.zeros_like(adjoint_pair)
     for d in received:
-        other = pair_place ^ d
         through = jnp.ones_like(top_scale)
         for e in received:
-            between = pair_place ^ e
-            inside = ((other < between) & (between < pair_place)) | (
-                (pair_place < between) & (between < other)
-            )
+            low = jnp.minimum(places[0], places[d])
+            high = jnp.maximum(places[0], places[d])
+            inside = (low < places[e]) & (places[e] < high)
             through = through * jnp.where(inside, totals[e], 1.0)
         term = through * values[d]
-        state_before = state_before + jnp.where(other < pair_place, term, 0.0)
-        adjoint_after = adjoint_after + jnp.where(other > pair_place, term, 0.0)
+        state_before = state_before + jnp.where(places[d] < places[0], term, 0.0)
+        adjoint_after = adjoint_after + jnp.where(places[d] > places[0], term, 0.0)
 
     state_inner = state_even + even_total * state_before
     adjoint_inner = adjoint_odd + odd_total * adjoint_after
@@ -428,17 +455,12 @@
     return wide[..., :rows, :] * jnp.exp2(scale), scale
 
 
-def bit_set(tm_bits, tile_bits):
-    place = lax.axis_index("tm") // tm_bits if tm_bits else lax.axis_index("tile") // tile_bits
-    return place % 2 == 1
-
-
 def shards(frames, cotangent, w_in, w_out, skip, log_decay):
     times, rows, cols, ch = frames.shape
     half = rows // 2
-    tile = lax.axis_index("tile")
-    odd = tile % 2 == 1
-    parity = (tile % 2).reshape(1).astype(jnp.int32)
+    place = jnp.stack([lax.axis_index("tile"), lax.axis_index("tm")]).astype(jnp.int32)
+    place = lax.optimization_barrier(place)
+    odd = place[0] % 2 == 1
     gain = skip[None, :]
 
     low = jnp.stack([frames[:, 0], cotangent[:, 0]])
@@ -446,15 +468,17 @@
     second = swap_across(jnp.where(odd, high, low))
     first = swap(jnp.where(odd, low, high), 0, 1)
 
+    blocks = blocks_call(frames, cotangent, w_in, w_out, log_decay)
     states, adjoints, leaving, frame_taps, cot_taps, info = drive_call(
-        parity, frames, cotangent, first, second, w_in, w_out, log_decay
+        place, frames, cotangent, first, second, blocks, log_decay
     )
     state_in, adjoint_in = carry_over(states[-1], leaving, info)
     states_bf, inflow_bf, first, second, in_part, out_part, info = grads_call(
-        parity, states, adjoints, state_in, adjoint_in, log_decay, frame_taps, cot_taps
+        place, states, adjoints, state_in, adjoint_in, log_decay, frame_taps, cot_taps
     )
 
-    in_scale, out_scale = info[8:9], info[0:1]
+    out_scale, in_scale = info[0:1], info[1:2]
+    odd, odd_tm, high_tile = (info[n : n + 1] > 0.5 for n in (2, 3, 4))
     scale = jnp.where(odd, in_scale, out_scale)
     message = packed(jnp.where(odd, in_part, out_part), scale, scale)
     message, first, second = lax.optimization_barrier((message, first, second))
@@ -464,25 +488,26 @@
     second = swap_across(second)
     first = swap(first, 0, 1)
 
-    bits = [(1, 0), (0, 2)] if lax.axis_size("tile") > 2 else [(1, 0)]
+    bits = [((1, 0), odd_tm), ((0, 2), high_tile)] if lax.axis_size("tile") > 2 else [((1, 0), odd_tm)]
     parts = 2 ** len(bits)
-    place = sum(bit_set(*bit).astype(jnp.int32) * 2**n for n, bit in enumerate(bits))
-    pieces = value.reshape(parts, -1, ch)
+    pieces = list(value.reshape(parts, -1, ch))
+    for n, (_, high) in enumerate(bits):
+        for d in range(parts):
+            if not d >> n & 1:
+                a, b = pieces[d], pieces[d + 2**n]
+                pieces[d], pieces[d + 2**n] = jnp.where(high, b, a), jnp.where(high, a, b)
 
     def mask(d):
-        chosen = [bit for n, bit in enumerate(bits) if d >> n & 1]
+        chosen = [bit for n, (bit, _) in enumerate(bits) if d >> n & 1]
         return sum(b[0] for b in chosen), sum(b[1] for b in chosen)
 
-    messages = [
-        packed(lax.dynamic_index_in_dim(pieces, place ^ d, 0, False), scale, scale)
-        for d in range(1, parts)
-    ]
-    value = lax.dynamic_index_in_dim(pieces, place, 0, False)
+    messages = [packed(pieces[d], scale, scale) for d in range(1, parts)]
+    value = pieces[0]
     states_bf = states_bf.reshape(times, half, cols, 2 * ch)
     inflow_bf = inflow_bf.reshape(times, half, cols, 2 * ch)
     *messages, states_bf = lax.optimization_barrier((*messages, states_bf))
     received = [swap(m, *mask(d + 1)) for d, m in enumerate(messages)]
-    output = output_call(parity, states_bf, first, second, w_out, gain, frames, False)
+    output = output_call(place, states_bf, first, second, w_out, gain, frames, False)
     for got in received:
         got, got_scale = unpacked(got)
         value = value + got
@@ -512,13 +537,12 @@
                 (a[0] + b[0], jnp.maximum(a[1], b[1])) for a, b in zip(terms[::2], terms[1::2])
             ]
         value, scale = terms[0]
-    grad_frames = output_call(parity, waiting, first, second, w_in, gain, cotangent, True)
+    grad_frames = output_call(place, waiting, first, second, w_in, gain, cotangent, True)
 
     message = packed(value, scale, scale)
     message, grad_frames = lax.optimization_barrier((message, grad_frames))
     gathered = [message] + [swap(message, *mask(d)) for d in range(1, parts)]
-    for bit in bits:
-        high = bit_set(*bit)
+    for _, high in bits:
         gathered = [
             (jnp.where(high, b, a), jnp.where(high, a, b))
             for a, b in zip(gathered[::2], gathered[1::2])

time: 95.1 us -> 87.2 us (0.917)
  local copies, waits for them, and re-layouts: 13.9 us -> 6.05 us
  waiting for transfers between devices: 26.6 us -> 32.2 us
  starting transfers between devices: 30.7 us -> 26.2 us
  Pallas kernels: 17.9 us -> 16.8 us
    unnamed x38 -> x20, local copies, waits for them, and re-layouts: 12 us -> 5.08 us
    ppermute x18, waiting for transfers between devices: 26.6 us -> 32.2 us  [swap(): lax.ppermute(value, ('tm', 'tile'), [(i, i ^ mask) for i in range(count)])]
    ppermute x18, starting transfers between devices: 29 us -> 24.7 us  [swap(): lax.ppermute(value, ('tm', 'tile'), [(i, i ^ mask) for i in range(count)])]
    pallas_call x1, Pallas kernels: 5.66 us -> 4.35 us  [grads_call(): pl.pallas_call(grads_kernel, in_specs=[pl.BlockSpec(memory_space=pltpu.SM...]
    pallas_call x2, Pallas kernels: 6.11 us -> 7.21 us  [output_call(): pl.pallas_call(functools.partial(output_kernel, flip=flip), in_specs=[pl....]
    pallas_call x1, Pallas kernels: 6.11 us -> 5.03 us  [drive_call(): pl.pallas_call(drive_kernel, in_specs=[pl.BlockSpec(memory_space=pltpu.SM...]
  transfers between devices with their start and end apart: 20 -> 20, of which waited for: 13 -> 12; matrix products, arithmetic and copies ran while one was open for 1% -> 0% of each run, Pallas kernels for 6% -> 9%
where the time goes in v3:
time: 87.2 us; the launch traced here: 86.8 us
  waiting for transfers between devices  32.2 us (37%)
  starting transfers between devices  26.2 us (30%)
  Pallas kernels  16.8 us (19%)
  local copies, waits for them, and re-layouts  6.05 us (7%)
  other arithmetic  4.31 us (5%)
  between operations  1.26 us (1%)
    ppermute x18, waiting for transfers between devices, swap(): lax.ppermute(value, ('tm', 'tile'), [(i, i ^ mask) for i in range(count)])  32.2 us
    ppermute x18, starting transfers between devices, swap(): lax.ppermute(value, ('tm', 'tile'), [(i, i ^ mask) for i in range(count)])  24.7 us
    pallas_call x2, Pallas kernels, output_call(): pl.pallas_call(functools.partial(output_kernel, flip=flip), in_specs=[pl....  7.21 us
    unnamed x20, local copies, waits for them, and re-layouts  5.08 us
    pallas_call x1, Pallas kernels, drive_call(): pl.pallas_call(drive_kernel, in_specs=[pl.BlockSpec(memory_space=pltpu.SM...  5.03 us
    pallas_call x1, Pallas kernels, grads_call(): pl.pallas_call(grads_kernel, in_specs=[pl.BlockSpec(memory_space=pltpu.SM...  4.35 us
  transfers between devices with their start and end apart: 20, of which 12 were waited for; matrix products, arithmetic and copies ran while one was open for 0% of the time, Pallas kernels for 9%

profile of v3, /device:TPU:0, one launch (start us, length us, event | category | flops | bytes accessed | tf_op | source)
XLA Modules:
  0.0 86.8 jit_solution(14127226955511665582)
XLA Ops:
  0.6 0.1 pad_add_fusion.7.place
  0.8 1.0 %slice_bitcast_fusion.2 = (bf16[1,4,64,128]{3,2,1,0:T(8,128)(2,1)S(1)}, bf16[1,4,64,128]{3,2,1,0:T(8,128)(2,1)S(1)}, bf16[1,4,64,128]{3,2,1,0:T(8,128)(2,1)S(1)}, bf16[1,4,64,128]{3,2,1,0:T(8,128)(2,1)S(1)}) fusion(bf16[4,16,64,128]{3,2,1,0:T(8,128)(2,1)} %direct.3, bf16[4,16,64,128]{3,2,1,0:T(8,128)(2,1)} %direct.2), kind=kLoop, calls=%fused_computation.98 | loop fusion | bytes 524288 | tf_op jit(solution)/shard_map/stack;squeeze | solution.py:466
  1.8 0.7 collective-permute-start.1
  2.5 4.4 %collective-permute-start = (bf16[2,4,64,128]{3,2,1,0:T(8,128)(2,1)S(1)}, bf16[2,4,64,128]{3,2,1,0:T(8,128)(2,1)S(1)}, u32[]{:S(2)}, u32[]{:S(2)}) collective-permute-start(bf16[2,4,64,128]{3,2,1,0:T(8,128)(2,1)S(1)} %get-tuple-element.119), channel_id=1, source_target_pairs={{0,1},{1,0},{2,3},{3,2},{4,5},{5,4},{6,7},{7,6},{8,9},{9,8},{10,11... | collective-permute-start | bytes 393224 | tf_op jit(solution)/shard_map/ppermute | solution.py:339
  6.9 1.2 %copy-done = bf16[4,16,64,128]{3,2,1,0:T(8,128)(2,1)S(1)} copy-done((bf16[4,16,64,128]{3,2,1,0:T(8,128)(2,1)S(1)}, bf16[4,16,64,128]{3,2,1,0:T(8,128)(2,1)}, u32[]{:S(2)}) %copy-start) | copy-done | bytes 1048600
  8.1 1.2 %copy-done.2 = bf16[4,16,64,128]{3,2,1,0:T(8,128)(2,1)S(1)} copy-done((bf16[4,16,64,128]{3,2,1,0:T(8,128)(2,1)S(1)}, bf16[4,16,64,128]{3,2,1,0:T(8,128)(2,1)}, u32[]{:S(2)}) %copy-start.2) | copy-done | bytes 1048600
  9.4 1.0 %copy-done.4 = bf16[3,3,128,128]{3,2,1,0:T(8,128)(2,1)S(1)} copy-done((bf16[3,3,128,128]{3,2,1,0:T(8,128)(2,1)S(1)}, bf16[3,3,128,128]{3,2,1,0:T(8,128)(2,1)}, u32[]{:S(2)}) %copy-start.4) | copy-done | bytes 294936
  10.3 1.0 %copy-done.6 = bf16[3,3,128,128]{3,2,1,0:T(8,128)(2,1)S(1)} copy-done((bf16[3,3,128,128]{3,2,1,0:T(8,128)(2,1)S(1)}, bf16[3,3,128,128]{3,2,1,0:T(8,128)(2,1)}, u32[]{:S(2)}) %copy-start.6) | copy-done | bytes 294936
  11.3 0.7 copy-done.8
  12.0 0.2 blocks.1
  12.2 5.0 %drive.1 = (f32[4,512,256]{2,1,0:T(8,128)S(1)}, f32[4,512,256]{2,1,0:T(8,128)S(1)}, f32[512,256]{1,0:T(8,128)S(1)}, bf16[3,4,576,256]{3,2,1,0:T(8,128)(2,1)S(1)}...) custom-call(s32[2]{0:T(128)S(1)} %pad_add_fusion.7.place, bf16[4,16,64,128]{3,2,1,0:T(8,128)(2,1)S(1)} %copy-done, ...), custom_call_target="tpu_custom_call" | custom-call | flops 3221225472 | bytes 12582912 | tf_op jit(solution)/shard_map/drive/pallas_call | solution.py:180
  17.3 0.1 fusion.8
  17.5 1.6 %collective-permute-start.2 = (f16[528,256]{1,0:T(8,128)(2,1)S(1)}, f16[528,256]{1,0:T(8,128)(2,1)S(1)}, u32[]{:S(2)}, u32[]{:S(2)}) collective-permute-start(f16[528,256]{1,0:T(8,128)(2,1)S(1)} %add_convert_fusion.2), channel_id=1, source_target_pairs={{0,4},{1,5},{2,6},{3,7},{4,0},{5,1},{6,2},{7,3},{8,12},{9,13},{10,... | collective-permute-start | bytes 811016 | tf_op jit(solution)/shard_map/ppermute | solution.py:339
  19.0 6.9 %collective-permute-done.2 = f16[528,256]{1,0:T(8,128)(2,1)S(1)} collective-permute-done((f16[528,256]{1,0:T(8,128)(2,1)S(1)}, f16[528,256]{1,0:T(8,128)(2,1)S(1)}, u32[]{:S(2)}, u32[]{:S(2)}) %collective-permute-start.2) | collective-permute-done | bytes 270368 | tf_op jit(solution)/shard_map/ppermute | solution.py:339
  26.0 0.2 select_multiply_fusion.4
  26.3 1.6 %collective-permute-start.3 = (f16[272,256]{1,0:T(8,128)(2,1)S(1)}, f16[272,256]{1,0:T(8,128)(2,1)S(1)}, u32[]{:S(2)}, u32[]{:S(2)}) collective-permute-start(f16[272,256]{1,0:T(8,128)(2,1)S(1)} %get-tuple-element.138), channel_id=1, source_target_pairs={{0,8},{1,9},{2,10},{3,11},{4,12},{5,13},{6,14},{7,15},{8,0},{9,1},... | collective-permute-start | bytes 417800 | tf_op jit(solution)/shard_map/ppermute | solution.py:339
  28.0 2.5 %collective-permute-start.5 = (f16[272,256]{1,0:T(8,128)(2,1)S(1)}, f16[272,256]{1,0:T(8,128)(2,1)S(1)}, u32[]{:S(2)}, u32[]{:S(2)}) collective-permute-start(f16[272,256]{1,0:T(8,128)(2,1)S(1)} %get-tuple-element.139), channel_id=1, source_target_pairs={{0,24},{1,25},{2,26},{3,27},{4,28},{5,29},{6,30},{7,31},{8,16},{9,... | collective-permute-start | bytes 417800 | tf_op jit(solution)/shard_map/ppermute | solution.py:339
  30.5 0.1 collective-permute-start.4
  30.6 1.2 %collective-permute-done.3 = f16[272,256]{1,0:T(8,128)(2,1)S(1)} collective-permute-done((f16[272,256]{1,0:T(8,128)(2,1)S(1)}, f16[272,256]{1,0:T(8,128)(2,1)S(1)}, u32[]{:S(2)}, u32[]{:S(2)}) %collective-permute-start.3) | collective-permute-done | bytes 139296 | tf_op jit(solution)/shard_map/ppermute | solution.py:339
  31.8 5.9 %collective-permute-done.5 = f16[272,256]{1,0:T(8,128)(2,1)S(1)} collective-permute-done((f16[272,256]{1,0:T(8,128)(2,1)S(1)}, f16[272,256]{1,0:T(8,128)(2,1)S(1)}, u32[]{:S(2)}, u32[]{:S(2)}) %collective-permute-start.5) | collective-permute-done | bytes 139296 | tf_op jit(solution)/shard_map/ppermute | solution.py:339
  37.7 4.6 %collective-permute-done.4 = f16[272,256]{1,0:T(8,128)(2,1)S(1)} collective-permute-done((f16[272,256]{1,0:T(8,128)(2,1)S(1)}, f16[272,256]{1,0:T(8,128)(2,1)S(1)}, u32[]{:S(2)}, u32[]{:S(2)}) %collective-permute-start.4) | collective-permute-done | bytes 139296 | tf_op jit(solution)/shard_map/ppermute | solution.py:339
  42.3 0.1 select_multiply_fusion.2
  42.5 0.1 select_multiply_fusion.1
  42.7 1.6 %collective-permute-start.6 = (f16[528,256]{1,0:T(8,128)(2,1)S(1)}, f16[528,256]{1,0:T(8,128)(2,1)S(1)}, u32[]{:S(2)}, u32[]{:S(2)}) collective-permute-start(f16[528,256]{1,0:T(8,128)(2,1)S(1)} %add_convert_fusion.1), channel_id=1, source_target_pairs={{0,4},{1,5},{2,6},{3,7},{4,0},{5,1},{6,2},{7,3},{8,12},{9,13},{10,... | collective-permute-start | bytes 811016 | tf_op jit(solution)/shard_map/ppermute | solution.py:339
  44.3 5.6 %collective-permute-done.6 = f16[528,256]{1,0:T(8,128)(2,1)S(1)} collective-permute-done((f16[528,256]{1,0:T(8,128)(2,1)S(1)}, f16[528,256]{1,0:T(8,128)(2,1)S(1)}, u32[]{:S(2)}, u32[]{:S(2)}) %collective-permute-start.6) | collective-permute-done | bytes 270368 | tf_op jit(solution)/shard_map/ppermute | solution.py:339
  50.0 0.1 fusion.16
  50.2 4.3 %grads.1 = (bf16[4,512,256]{2,1,0:T(8,128)(2,1)S(1)}, bf16[4,512,256]{2,1,0:T(8,128)(2,1)S(1)}, bf16[2,4,64,128]{3,2,1,0:T(8,128)(2,1)S(1)}, bf16[2,4,64,128]{3,...) custom-call(s32[2]{0:T(128)S(1)} %pad_add_fusion.7.place, ...), custom_call_target="tpu_custom_call" | custom-call | flops 3221225472 | bytes 12582912 | tf_op jit(solution)/shard_map/grads/pallas_call | solution.py:285
  54.6 0.1 select_multiply_fusion
  54.7 0.1 collective-permute-start.7
  54.8 0.5 collective-permute-start.11
  55.3 0.8 collective-permute-start.12
  56.1 0.2 collective-permute-done.7
  56.4 0.0 copy-start.1
  56.4 0.0 copy-start.5
  56.4 0.0 copy-start.9
  56.4 0.1 fusion.2
  56.5 0.1 select_multiply_fusion.6
  56.6 1.6 %collective-permute-start.8 = (f16[304,128]{1,0:T(8,128)(2,1)S(1)}, f16[304,128]{1,0:T(8,128)(2,1)S(1)}, u32[]{:S(2)}, u32[]{:S(2)}) collective-permute-start(f16[304,128]{1,0:T(8,128)(2,1)S(1)} %get-tuple-element.42), channel_id=1, source_target_pairs={{0,4},{1,5},{2,6},{3,7},{4,0},{5,1},{6,2},{7,3},{8,12},{9,13},{10,... | collective-permute-start | bytes 233480 | tf_op jit(solution)/shard_map/ppermute | solution.py:339
  58.2 2.7 %collective-permute-start.9 = (f16[304,128]{1,0:T(8,128)(2,1)S(1)}, f16[304,128]{1,0:T(8,128)(2,1)S(1)}, u32[]{:S(2)}, u32[]{:S(2)}) collective-permute-start(f16[304,128]{1,0:T(8,128)(2,1)S(1)} %get-tuple-element.43), channel_id=1, source_target_pairs={{0,2},{1,3},{2,0},{3,1},{4,6},{5,7},{6,4},{7,5},{8,10},{9,11},{10,... | collective-permute-start | bytes 233480 | tf_op jit(solution)/shard_map/ppermute | solution.py:339
  61.0 0.0 collective-permute-start.10
  61.0 0.0 collective-permute-done.11.first
  61.0 0.0 collective-permute-done.12.second
  61.0 3.6 %output.1 = bf16[4,16,64,128]{3,2,1,0:T(8,128)(2,1)} custom-call(s32[2]{0:T(128)S(1)} %pad_add_fusion.7.place, bf16[4,8,64,256]{3,2,1,0:T(8,128)(2,1)S(1)} %bitcast.101, bf16[2,4,64,128]{3,2,1,0:T(8,128)(2,1)S(1)} %collective-permute-done.11.first, bf16[2,4,64,128]{3,2,1,0:T(8,128)(2,1)S(1)} %collective-permute-done.12.second, ...), custom_call_target="tpu_custom_call" | custom-call | flops 1610612736 | bytes 4194304 | tf_op jit(solution)/shard_map/output/pallas_call | solution.py:318
  64.7 1.6 %collective-permute-done.10 = f16[304,128]{1,0:T(8,128)(2,1)S(1)} collective-permute-done((f16[304,128]{1,0:T(8,128)(2,1)S(1)}, f16[304,128]{1,0:T(8,128)(2,1)S(1)}, u32[]{:S(2)}, u32[]{:S(2)}) %collective-permute-start.10) | collective-permute-done | bytes 77856 | tf_op jit(solution)/shard_map/ppermute | solution.py:339
  66.3 0.1 fusion.25
  66.4 2.6 %collective-permute-start.15 = (f16[304,128]{1,0:T(8,128)(2,1)S(1)}, f16[304,128]{1,0:T(8,128)(2,1)S(1)}, u32[]{:S(2)}, u32[]{:S(2)}) collective-permute-start(f16[304,128]{1,0:T(8,128)(2,1)S(1)} %add_convert_fusion.4), channel_id=1, source_target_pairs={{0,24},{1,25},{2,26},{3,27},{4,28},{5,29},{6,30},{7,31},{8,16},{9,... | collective-permute-start | bytes 233480 | tf_op jit(solution)/shard_map/ppermute | solution.py:339
  69.0 1.8 %collective-permute-start.13 = (f16[304,128]{1,0:T(8,128)(2,1)S(1)}, f16[304,128]{1,0:T(8,128)(2,1)S(1)}, u32[]{:S(2)}, u32[]{:S(2)}) collective-permute-start(f16[304,128]{1,0:T(8,128)(2,1)S(1)} %add_convert_fusion.4), channel_id=1, source_target_pairs={{0,8},{1,9},{2,10},{3,11},{4,12},{5,13},{6,14},{7,15},{8,0},{9,1},... | collective-permute-start | bytes 233480 | tf_op jit(solution)/shard_map/ppermute | solution.py:339
  70.9 3.6 %grad_frames.1 = bf16[4,16,64,128]{3,2,1,0:T(8,128)(2,1)} custom-call(s32[2]{0:T(128)S(1)} %pad_add_fusion.7.place, bf16[4,8,64,256]{3,2,1,0:T(8,128)(2,1)S(1)} %bitcast.100, bf16[2,4,64,128]{3,2,1,0:T(8,128)(2,1)S(1)} %collective-permute-done.11.first, bf16[2,4,64,128]{3,2,1,0:T(8,128)(2,1)S(1)} %collective-permute-done.12.second, ...), custom_call_target="tpu_custom_call" | custom-call | flops 1610612736 | bytes 4194304 | tf_op jit(solution)/shard_map/grad_frames/pallas_call | solution.py:318
  74.5 0.6 collective-permute-done.14
  75.1 0.1 fusion.22
  75.2 1.6 %collective-permute-start.18 = (f16[304,128]{1,0:T(8,128)(2,1)S(1)}, f16[304,128]{1,0:T(8,128)(2,1)S(1)}, u32[]{:S(2)}, u32[]{:S(2)}) collective-permute-start(f16[304,128]{1,0:T(8,128)(2,1)S(1)} %add_convert_fusion.3), channel_id=1, source_target_pairs={{0,4},{1,5},{2,6},{3,7},{4,0},{5,1},{6,2},{7,3},{8,12},{9,13},{10,... | collective-permute-start | bytes 233480 | tf_op jit(solution)/shard_map/ppermute | solution.py:339
  76.8 0.7 collective-permute-start.17
  77.5 1.3 %collective-permute-start.16 = (f16[304,128]{1,0:T(8,128)(2,1)S(1)}, f16[304,128]{1,0:T(8,128)(2,1)S(1)}, u32[]{:S(2)}, u32[]{:S(2)}) collective-permute-start(f16[304,128]{1,0:T(8,128)(2,1)S(1)} %add_convert_fusion.3), channel_id=1, source_target_pairs={{0,6},{1,7},{2,4},{3,5},{4,2},{5,3},{6,0},{7,1},{8,14},{9,15},{10,... | collective-permute-start | bytes 233480 | tf_op jit(solution)/shard_map/ppermute | solution.py:339
  78.8 0.9 %collective-permute-done.18 = f16[304,128]{1,0:T(8,128)(2,1)S(1)} collective-permute-done((f16[304,128]{1,0:T(8,128)(2,1)S(1)}, f16[304,128]{1,0:T(8,128)(2,1)S(1)}, u32[]{:S(2)}, u32[]{:S(2)}) %collective-permute-start.18) | collective-permute-done | bytes 77856 | tf_op jit(solution)/shard_map/ppermute | solution.py:339
  79.7 2.3 %collective-permute-done.17 = f16[304,128]{1,0:T(8,128)(2,1)S(1)} collective-permute-done((f16[304,128]{1,0:T(8,128)(2,1)S(1)}, f16[304,128]{1,0:T(8,128)(2,1)S(1)}, u32[]{:S(2)}, u32[]{:S(2)}) %collective-permute-start.17) | collective-permute-done | bytes 77856 | tf_op jit(solution)/shard_map/ppermute | solution.py:339
  82.0 0.8 collective-permute-done.16
  82.8 0.1 broadcast_select_fusion.9
  82.9 0.1 broadcast_select_fusion.3
  83.0 0.1 pad_maximum_fusion.2
  83.1 0.1 collective-permute-start.19
  83.2 1.6 %collective-permute-done.19 = f16[1216,128]{1,0:T(8,128)(2,1)S(1)} collective-permute-done((f16[1216,128]{1,0:T(8,128)(2,1)S(1)}, f16[1216,128]{1,0:T(8,128)(2,1)S(1)}, u32[]{:S(2)}, u32[]{:S(2)}) %collective-permute-start.19) | collective-permute-done | bytes 311328 | tf_op jit(solution)/shard_map/ppermute | solution.py:339
  84.8 0.2 broadcast_select_fusion
  85.0 0.9 %fusion.1 = f32[4,288,128]{2,1,0:T(8,128)} fusion(f32[4,304,128]{2,1,0:T(8,128)S(1)} %convert.2, f32[4,128]{1,0:T(4,128)S(1)} %bitcast.128), kind=kLoop, calls=%fused_computation.4 | loop fusion | flops 294912 | bytes 1181696 | tf_op jit(solution)/shard_map/mul | solution.py:560
  85.9 0.9 %fusion = f32[4,288,128]{2,1,0:T(8,128)} fusion(f32[4,304,128]{2,1,0:T(8,128)S(1)} %convert.3, f32[4,128]{1,0:T(4,128)S(1)} %bitcast.129), kind=kLoop, calls=%fused_computation.2 | loop fusion | flops 294912 | bytes 1181696 | tf_op jit(solution)/shard_map/mul | solution.py:560
  (64 shorter events, 1.0 us)
Async XLA Ops:
  1.8 10.3 %collective-permute-start.1 = (bf16[2,4,64,128]{3,2,1,0:T(8,128)(2,1)S(1)}, bf16[2,4,64,128]{3,2,1,0:T(8,128)(2,1)S(1)}, u32[]{:S(2)}, u32[]{:S(2)}) collective-permute-start(bf16[2,4,64,128]{3,2,1,0:T(8,128)(2,1)S(1)} %get-tuple-element.118), channel_id=1, source_target_pairs={{1,2},{2,1},{5,6},{6,5},{9,10},{10,9},{13,14},{14,13},{17,18},{18,... | collective-permute-start | bytes 393224 | tf_op jit(solution)/shard_map/ppermute | solution.py:347
  2.5 9.7 %collective-permute-start = (bf16[2,4,64,128]{3,2,1,0:T(8,128)(2,1)S(1)}, bf16[2,4,64,128]{3,2,1,0:T(8,128)(2,1)S(1)}, u32[]{:S(2)}, u32[]{:S(2)}) collective-permute-start(bf16[2,4,64,128]{3,2,1,0:T(8,128)(2,1)S(1)} %get-tuple-element.119), channel_id=1, source_target_pairs={{0,1},{1,0},{2,3},{3,2},{4,5},{5,4},{6,7},{7,6},{8,9},{9,8},{10,11... | collective-permute-start | bytes 393224 | tf_op jit(solution)/shard_map/ppermute | solution.py:339
  6.9 1.2 %copy-start = (bf16[4,16,64,128]{3,2,1,0:T(8,128)(2,1)S(1)}, bf16[4,16,64,128]{3,2,1,0:T(8,128)(2,1)}, u32[]{:S(2)}) copy-start(bf16[4,16,64,128]{3,2,1,0:T(8,128)(2,1)} %direct.2) | copy-start | bytes 3145732
  8.1 1.2 %copy-start.2 = (bf16[4,16,64,128]{3,2,1,0:T(8,128)(2,1)S(1)}, bf16[4,16,64,128]{3,2,1,0:T(8,128)(2,1)}, u32[]{:S(2)}) copy-start(bf16[4,16,64,128]{3,2,1,0:T(8,128)(2,1)} %direct.3) | copy-start | bytes 3145732
  9.4 1.0 %copy-start.4 = (bf16[3,3,128,128]{3,2,1,0:T(8,128)(2,1)S(1)}, bf16[3,3,128,128]{3,2,1,0:T(8,128)(2,1)}, u32[]{:S(2)}) copy-start(bf16[3,3,128,128]{3,2,1,0:T(8,128)(2,1)} %weight.2) | copy-start | bytes 884740
  10.3 1.0 %copy-start.6 = (bf16[3,3,128,128]{3,2,1,0:T(8,128)(2,1)S(1)}, bf16[3,3,128,128]{3,2,1,0:T(8,128)(2,1)}, u32[]{:S(2)}) copy-start(bf16[3,3,128,128]{3,2,1,0:T(8,128)(2,1)} %weight.3) | copy-start | bytes 884740
  11.3 0.7 copy-start.8
  17.5 8.5 %collective-permute-start.2 = (f16[528,256]{1,0:T(8,128)(2,1)S(1)}, f16[528,256]{1,0:T(8,128)(2,1)S(1)}, u32[]{:S(2)}, u32[]{:S(2)}) collective-permute-start(f16[528,256]{1,0:T(8,128)(2,1)S(1)} %add_convert_fusion.2), channel_id=1, source_target_pairs={{0,4},{1,5},{2,6},{3,7},{4,0},{5,1},{6,2},{7,3},{8,12},{9,13},{10,... | collective-permute-start | bytes 811016 | tf_op jit(solution)/shard_map/ppermute | solution.py:339
  26.3 5.4 %collective-permute-start.3 = (f16[272,256]{1,0:T(8,128)(2,1)S(1)}, f16[272,256]{1,0:T(8,128)(2,1)S(1)}, u32[]{:S(2)}, u32[]{:S(2)}) collective-permute-start(f16[272,256]{1,0:T(8,128)(2,1)S(1)} %get-tuple-element.138), channel_id=1, source_target_pairs={{0,8},{1,9},{2,10},{3,11},{4,12},{5,13},{6,14},{7,15},{8,0},{9,1},... | collective-permute-start | bytes 417800 | tf_op jit(solution)/shard_map/ppermute | solution.py:339
  28.0 9.7 %collective-permute-start.5 = (f16[272,256]{1,0:T(8,128)(2,1)S(1)}, f16[272,256]{1,0:T(8,128)(2,1)S(1)}, u32[]{:S(2)}, u32[]{:S(2)}) collective-permute-start(f16[272,256]{1,0:T(8,128)(2,1)S(1)} %get-tuple-element.139), channel_id=1, source_target_pairs={{0,24},{1,25},{2,26},{3,27},{4,28},{5,29},{6,30},{7,31},{8,16},{9,... | collective-permute-start | bytes 417800 | tf_op jit(solution)/shard_map/ppermute | solution.py:339
  30.5 11.8 %collective-permute-start.4 = (f16[272,256]{1,0:T(8,128)(2,1)S(1)}, f16[272,256]{1,0:T(8,128)(2,1)S(1)}, u32[]{:S(2)}, u32[]{:S(2)}) collective-permute-start(f16[272,256]{1,0:T(8,128)(2,1)S(1)} %get-tuple-element.139), channel_id=1, source_target_pairs={{0,16},{1,17},{2,18},{3,19},{4,20},{5,21},{6,22},{7,23},{8,24},{9,... | collective-permute-start | bytes 417800 | tf_op jit(solution)/shard_map/ppermute | solution.py:339
  42.7 7.2 %collective-permute-start.6 = (f16[528,256]{1,0:T(8,128)(2,1)S(1)}, f16[528,256]{1,0:T(8,128)(2,1)S(1)}, u32[]{:S(2)}, u32[]{:S(2)}) collective-permute-start(f16[528,256]{1,0:T(8,128)(2,1)S(1)} %add_convert_fusion.1), channel_id=1, source_target_pairs={{0,4},{1,5},{2,6},{3,7},{4,0},{5,1},{6,2},{7,3},{8,12},{9,13},{10,... | collective-permute-start | bytes 811016 | tf_op jit(solution)/shard_map/ppermute | solution.py:339
  54.7 1.7 %collective-permute-start.7 = (f16[1168,128]{1,0:T(8,128)(2,1)S(1)}, f16[1168,128]{1,0:T(8,128)(2,1)S(1)}, u32[]{:S(2)}, u32[]{:S(2)}) collective-permute-start(f16[1168,128]{1,0:T(8,128)(2,1)S(1)} %add_convert_fusion), channel_id=1, source_target_pairs={{0,1},{1,0},{2,3},{3,2},{4,5},{5,4},{6,7},{7,6},{8,9},{9,8},{10,11... | collective-permute-start | bytes 897032 | tf_op jit(solution)/shard_map/ppermute | solution.py:339
  54.8 6.2 %collective-permute-start.11 = (bf16[2,4,64,128]{3,2,1,0:T(8,128)(2,1)S(1)}, bf16[2,4,64,128]{3,2,1,0:T(8,128)(2,1)S(1)}, u32[]{:S(2)}, u32[]{:S(2)}) collective-permute-start(bf16[2,4,64,128]{3,2,1,0:T(8,128)(2,1)S(1)} %get-tuple-element.46), channel_id=1, source_target_pairs={{0,1},{1,0},{2,3},{3,2},{4,5},{5,4},{6,7},{7,6},{8,9},{9,8},{10,11... | collective-permute-start | bytes 393224 | tf_op jit(solution)/shard_map/ppermute | solution.py:339
  55.3 5.7 %collective-permute-start.12 = (bf16[2,4,64,128]{3,2,1,0:T(8,128)(2,1)S(1)}, bf16[2,4,64,128]{3,2,1,0:T(8,128)(2,1)S(1)}, u32[]{:S(2)}, u32[]{:S(2)}) collective-permute-start(bf16[2,4,64,128]{3,2,1,0:T(8,128)(2,1)S(1)} %get-tuple-element.47), channel_id=1, source_target_pairs={{1,2},{2,1},{5,6},{6,5},{9,10},{10,9},{13,14},{14,13},{17,18},{18,... | collective-permute-start | bytes 393224 | tf_op jit(solution)/shard_map/ppermute | solution.py:347
  56.4 4.6 %copy-start.1 = (bf16[4,16,64,128]{3,2,1,0:T(8,128)(2,1)S(1)}, bf16[4,16,64,128]{3,2,1,0:T(8,128)(2,1)}, u32[]{:S(2)}) copy-start(bf16[4,16,64,128]{3,2,1,0:T(8,128)(2,1)} %direct.2) | copy-start | bytes 3145732
  56.4 4.6 %copy-start.5 = (bf16[3,3,128,128]{3,2,1,0:T(8,128)(2,1)S(1)}, bf16[3,3,128,128]{3,2,1,0:T(8,128)(2,1)}, u32[]{:S(2)}) copy-start(bf16[3,3,128,128]{3,2,1,0:T(8,128)(2,1)} %weight.2) | copy-start | bytes 884740
  56.4 4.6 %copy-start.9 = (f32[128]{0:T(128)S(1)}, f32[128]{0:T(128)}, u32[]{:S(2)}) copy-start(f32[128]{0:T(128)} %param.10) | copy-start | bytes 1540
  56.6 8.0 %collective-permute-start.8 = (f16[304,128]{1,0:T(8,128)(2,1)S(1)}, f16[304,128]{1,0:T(8,128)(2,1)S(1)}, u32[]{:S(2)}, u32[]{:S(2)}) collective-permute-start(f16[304,128]{1,0:T(8,128)(2,1)S(1)} %get-tuple-element.42), channel_id=1, source_target_pairs={{0,4},{1,5},{2,6},{3,7},{4,0},{5,1},{6,2},{7,3},{8,12},{9,13},{10,... | collective-permute-start | bytes 233480 | tf_op jit(solution)/shard_map/ppermute | solution.py:339
  58.2 6.4 %collective-permute-start.9 = (f16[304,128]{1,0:T(8,128)(2,1)S(1)}, f16[304,128]{1,0:T(8,128)(2,1)S(1)}, u32[]{:S(2)}, u32[]{:S(2)}) collective-permute-start(f16[304,128]{1,0:T(8,128)(2,1)S(1)} %get-tuple-element.43), channel_id=1, source_target_pairs={{0,2},{1,3},{2,0},{3,1},{4,6},{5,7},{6,4},{7,5},{8,10},{9,11},{10,... | collective-permute-start | bytes 233480 | tf_op jit(solution)/shard_map/ppermute | solution.py:339
  61.0 5.3 %collective-permute-start.10 = (f16[304,128]{1,0:T(8,128)(2,1)S(1)}, f16[304,128]{1,0:T(8,128)(2,1)S(1)}, u32[]{:S(2)}, u32[]{:S(2)}) collective-permute-start(f16[304,128]{1,0:T(8,128)(2,1)S(1)} %get-tuple-element.44), channel_id=1, source_target_pairs={{0,6},{1,7},{2,4},{3,5},{4,2},{5,3},{6,0},{7,1},{8,14},{9,15},{10,... | collective-permute-start | bytes 233480 | tf_op jit(solution)/shard_map/ppermute | solution.py:339
  64.6 6.2 %copy-start.3 = (bf16[4,16,64,128]{3,2,1,0:T(8,128)(2,1)S(1)}, bf16[4,16,64,128]{3,2,1,0:T(8,128)(2,1)}, u32[]{:S(2)}) copy-start(bf16[4,16,64,128]{3,2,1,0:T(8,128)(2,1)} %direct.3) | copy-start | bytes 3145732
  64.6 6.3 %copy-start.7 = (bf16[3,3,128,128]{3,2,1,0:T(8,128)(2,1)S(1)}, bf16[3,3,128,128]{3,2,1,0:T(8,128)(2,1)}, u32[]{:S(2)}) copy-start(bf16[3,3,128,128]{3,2,1,0:T(8,128)(2,1)} %weight.3) | copy-start | bytes 884740
  66.4 8.1 %collective-permute-start.15 = (f16[304,128]{1,0:T(8,128)(2,1)S(1)}, f16[304,128]{1,0:T(8,128)(2,1)S(1)}, u32[]{:S(2)}, u32[]{:S(2)}) collective-permute-start(f16[304,128]{1,0:T(8,128)(2,1)S(1)} %add_convert_fusion.4), channel_id=1, source_target_pairs={{0,24},{1,25},{2,26},{3,27},{4,28},{5,29},{6,30},{7,31},{8,16},{9,... | collective-permute-start | bytes 233480 | tf_op jit(solution)/shard_map/ppermute | solution.py:339
  69.0 6.1 %collective-permute-start.14 = (f16[304,128]{1,0:T(8,128)(2,1)S(1)}, f16[304,128]{1,0:T(8,128)(2,1)S(1)}, u32[]{:S(2)}, u32[]{:S(2)}) collective-permute-start(f16[304,128]{1,0:T(8,128)(2,1)S(1)} %add_convert_fusion.4), channel_id=1, source_target_pairs={{0,16},{1,17},{2,18},{3,19},{4,20},{5,21},{6,22},{7,23},{8,24},{9,... | collective-permute-start | bytes 233480 | tf_op jit(solution)/shard_map/ppermute | solution.py:339
  69.0 6.1 %collective-permute-start.13 = (f16[304,128]{1,0:T(8,128)(2,1)S(1)}, f16[304,128]{1,0:T(8,128)(2,1)S(1)}, u32[]{:S(2)}, u32[]{:S(2)}) collective-permute-start(f16[304,128]{1,0:T(8,128)(2,1)S(1)} %add_convert_fusion.4), channel_id=1, source_target_pairs={{0,8},{1,9},{2,10},{3,11},{4,12},{5,13},{6,14},{7,15},{8,0},{9,1},... | collective-permute-start | bytes 233480 | tf_op jit(solution)/shard_map/ppermute | solution.py:339
  75.2 4.5 %collective-permute-start.18 = (f16[304,128]{1,0:T(8,128)(2,1)S(1)}, f16[304,128]{1,0:T(8,128)(2,1)S(1)}, u32[]{:S(2)}, u32[]{:S(2)}) collective-permute-start(f16[304,128]{1,0:T(8,128)(2,1)S(1)} %add_convert_fusion.3), channel_id=1, source_target_pairs={{0,4},{1,5},{2,6},{3,7},{4,0},{5,1},{6,2},{7,3},{8,12},{9,13},{10,... | collective-permute-start | bytes 233480 | tf_op jit(solution)/shard_map/ppermute | solution.py:339
  76.8 5.2 %collective-permute-start.17 = (f16[304,128]{1,0:T(8,128)(2,1)S(1)}, f16[304,128]{1,0:T(8,128)(2,1)S(1)}, u32[]{:S(2)}, u32[]{:S(2)}) collective-permute-start(f16[304,128]{1,0:T(8,128)(2,1)S(1)} %add_convert_fusion.3), channel_id=1, source_target_pairs={{0,2},{1,3},{2,0},{3,1},{4,6},{5,7},{6,4},{7,5},{8,10},{9,11},{10,... | collective-permute-start | bytes 233480 | tf_op jit(solution)/shard_map/ppermute | solution.py:339
  77.5 5.3 %collective-permute-start.16 = (f16[304,128]{1,0:T(8,128)(2,1)S(1)}, f16[304,128]{1,0:T(8,128)(2,1)S(1)}, u32[]{:S(2)}, u32[]{:S(2)}) collective-permute-start(f16[304,128]{1,0:T(8,128)(2,1)S(1)} %add_convert_fusion.3), channel_id=1, source_target_pairs={{0,6},{1,7},{2,4},{3,5},{4,2},{5,3},{6,0},{7,1},{8,14},{9,15},{10,... | collective-permute-start | bytes 233480 | tf_op jit(solution)/shard_map/ppermute | solution.py:339
  83.1 1.7 %collective-permute-start.19 = (f16[1216,128]{1,0:T(8,128)(2,1)S(1)}, f16[1216,128]{1,0:T(8,128)(2,1)S(1)}, u32[]{:S(2)}, u32[]{:S(2)}) collective-permute-start(f16[1216,128]{1,0:T(8,128)(2,1)S(1)} %pad_maximum_fusion.2), channel_id=1, source_target_pairs={{0,1},{1,0},{2,3},{3,2},{4,5},{5,4},{6,7},{7,6},{8,9},{9,8},{10,11... | collective-permute-start | bytes 933896 | tf_op jit(solution)/shard_map/ppermute | solution.py:339

commit v4 on v3

--- a/solution.py
+++ b/solution.py
@@ -167,15 +167,16 @@
     info[4:5, :] = low
     row = jnp.zeros((1, 2 * ch), F32)
     info[5:6, :] = row + lax.rem(place[1], 2).astype(F32)
-    for d in range(info.shape[0] - 6):
-        info[6 + d : 7 + d, :] = row + (lax.div(place[1], 2) ^ d).astype(F32)
+    info[6:7, :] = row + lax.rem(lax.div(place[1], 2), 2).astype(F32)
+    for d in range(info.shape[0] - 7):
+        info[7 + d : 8 + d, :] = row + (lax.div(place[1], 4) ^ d).astype(F32)
 
 
 def drive_call(place, frames, cotangent, first, second, blocks, log_decay):
     times, rows, cols, ch = frames.shape
     half = rows // 2
     field = jax.ShapeDtypeStruct((times, half * cols, 2 * ch), F32)
-    rows_info = (6 + lax.axis_size("tm") // 2 + 15) // 16 * 16
+    rows_info = (7 + lax.axis_size("tm") // 4 + 15) // 16 * 16
     taps = jax.ShapeDtypeStruct((3, times, (half + 1) * cols, 2 * ch), BF16)
     return pl.pallas_call(
         drive_kernel,
@@ -366,85 +367,99 @@
     return rows[0:1] + rows[1:2] / 256.0 + rows[2:3] / 65536.0
 
 
+def by_place(values, flags):
+    values = list(values)
+    for n, flag in enumerate(flags):
+        for d in range(len(values)):
+            if not d >> n & 1:
+                a, b = values[d], values[d + 2**n]
+                values[d], values[d + 2**n] = jnp.where(flag, b, a), jnp.where(flag, a, b)
+    return values
+
+
 def carry_over(state_end, adjoint_end, info):
-    count = lax.axis_size("tm")
-    odd = info[5:6] > 0.5
-    places = [info[6 + d : 7 + d] for d in range(count // 2)]
-    half = state_end.shape[0] // 2
+    squares = lax.axis_size("tm") // 4
+    flags = [info[5:6] > 0.5, info[6:7] > 0.5]
+    places = [info[7 + d : 8 + d] for d in range(squares)]
+    part = state_end.shape[0] // 4
+    width = state_end.shape[1]
 
     def both(low, high, scale_low, scale_high, rows):
         parts = [low * jnp.exp2(-scale_low), high * jnp.exp2(-scale_high), rows]
-        return laid(parts, 2 * half + 16).astype(jnp.float16)
-
-    def give(value, mine):
-        low, high = value[:half], value[half:]
-        return jnp.where(odd, high, low) if mine else jnp.where(odd, low, high)
-
-    got = swap(
-        both(give(state_end, False), give(adjoint_end, False), info[0:1], info[1:2], info[:5]), 1, 0
-    ).astype(F32)
-    their_info = got[2 * half : 2 * half + 5]
-    total, their_total = whole_decay(info[2:5]), whole_decay(their_info[2:5])
-    even_total = jnp.where(odd, their_total, total)
-    odd_total = jnp.where(odd, total, their_total)
-    state_mine, adjoint_mine = give(state_end, True), give(adjoint_end, True)
-    state_theirs = got[:half] * jnp.exp2(their_info[0:1])
-    adjoint_theirs = got[half : 2 * half] * jnp.exp2(their_info[1:2])
-    state_even = jnp.where(odd, state_theirs, state_mine)
-    state_odd = jnp.where(odd, state_mine, state_theirs)
-    adjoint_even = jnp.where(odd, adjoint_theirs, adjoint_mine)
-    adjoint_odd = jnp.where(odd, adjoint_mine, adjoint_theirs)
-    state_pair = odd_total * state_even + state_odd
-    adjoint_pair = adjoint_even + even_total * adjoint_odd
-    state_scale = jnp.maximum(info[0:1], their_info[0:1])
-    adjoint_scale = jnp.maximum(info[1:2], their_info[1:2])
+        return laid(parts, 2 * part + 16).astype(jnp.float16)
+
+    def quarters(value):
+        return by_place([value[n * part : (n + 1) * part] for n in range(4)], flags)
+
+    states, adjoints = quarters(state_end), quarters(adjoint_end)
+    messages = [both(states[d], adjoints[d], info[0:1], info[1:2], info[:5]) for d in (1, 2, 3)]
+    received = [swap(m, d + 1, 0).astype(F32) for d, m in enumerate(messages)]
+    rows = [info[:5]] + [got[2 * part : 2 * part + 5] for got in received]
+    state_scale = functools.reduce(jnp.maximum, [row[0:1] for row in rows])
+    adjoint_scale = functools.reduce(jnp.maximum, [row[1:2] for row in rows])
+    states = [states[0]] + [
+        got[:part] * jnp.exp2(row[0:1]) for got, row in zip(received, rows[1:])
+    ]
+    adjoints = [adjoints[0]] + [
+        got[part : 2 * part] * jnp.exp2(row[1:2]) for got, row in zip(received, rows[1:])
+    ]
+    states, adjoints = by_place(states, flags), by_place(adjoints, flags)
+    decay_rows = by_place([row[2:5] for row in rows], flags)
+    totals = [whole_decay(row) for row in decay_rows]
+
+    one = jnp.ones((1, width), F32)
+    zero = jnp.zeros((part, width), F32)
+    before, reach = [zero], [one]
+    for n in range(4):
+        before.append(totals[n] * before[-1] + states[n])
+        reach.append(reach[-1] * totals[n])
+    after, back = [zero], [one]
+    for n in (3, 2, 1, 0):
+        after.insert(0, adjoints[n] + totals[n] * after[0])
+        back.insert(0, back[0] * totals[n])
+    state_square, adjoint_square = before.pop(), after.pop(0)
+    back.pop(0)
 
     messages = []
     bit = 1
-    while bit < count // 2:
+    while bit < squares:
         later = places[bit] < places[0]
         scale = jnp.where(later, adjoint_scale, state_scale)
-        value = jnp.where(later, adjoint_pair, state_pair)
-        messages.append(packed(value, scale, scale, info[2:5], their_info[2:5]))
+        value = jnp.where(later, adjoint_square, state_square)
+        messages.append(packed(value, scale, scale, *decay_rows))
         bit *= 2
-    received = {}
-    for d in range(1, count // 2):
-        received[d] = swap(messages[d.bit_length() - 1], 2 * d, 0).astype(F32)
-    totals, values = {}, {}
+    through_square, values = {}, {}
     top_scale = jnp.maximum(state_scale, adjoint_scale)
-    for d, got in received.items():
-        rows = got[half : half + 7]
-        totals[d] = whole_decay(rows[1:4]) * whole_decay(rows[4:7])
-        values[d] = got[:half] * jnp.exp2(rows[0:1])
-        top_scale = jnp.maximum(top_scale, rows[0:1])
-    state_before = jnp.zeros_like(state_pair)
-    adjoint_after = jnp.zeros_like(adjoint_pair)
-    for d in received:
-        through = jnp.ones_like(top_scale)
-        for e in received:
-            low = jnp.minimum(places[0], places[d])
-            high = jnp.maximum(places[0], places[d])
-            inside = (low < places[e]) & (places[e] < high)
-            through = through * jnp.where(inside, totals[e], 1.0)
-        term = through * values[d]
+    for d in range(1, squares):
+        got = swap(messages[d.bit_length() - 1], 4 * d, 0).astype(F32)
+        there = [got[part + 1 + 3 * n : part + 4 + 3 * n] for n in range(4)]
+        through_square[d] = functools.reduce(jnp.multiply, [whole_decay(row) for row in there])
+        values[d] = got[:part] * jnp.exp2(got[part : part + 1])
+        top_scale = jnp.maximum(top_scale, got[part : part + 1])
+    state_before, adjoint_after = zero, zero
+    for d in values:
+        term = values[d]
+        if squares > 2:
+            through = one
+            for e in values:
+                low = jnp.minimum(places[0], places[d])
+                high = jnp.maximum(places[0], places[d])
+                inside = (low < places[e]) & (places[e] < high)
+                through = through * jnp.where(inside, through_square[e], 1.0)
+            term = through * term
         state_before = state_before + jnp.where(places[d] < places[0], term, 0.0)
         adjoint_after = adjoint_after + jnp.where(places[d] > places[0], term, 0.0)
 
-    state_inner = state_even + even_total * state_before
-    adjoint_inner = adjoint_odd + odd_total * adjoint_after
-    state_keep = jnp.where(odd, state_inner, state_before)
-    state_send = jnp.where(odd, state_before, state_inner)
-    adjoint_keep = jnp.where(odd, adjoint_after, adjoint_inner)
-    adjoint_send = jnp.where(odd, adjoint_inner, adjoint_after)
-    got = swap(both(state_send, adjoint_send, top_scale, top_scale, top_scale), 1, 0).astype(F32)
-    scale = jnp.exp2(got[2 * half : 2 * half + 1])
-
-    def joined(keep, other):
-        return jnp.concatenate([jnp.where(odd, other, keep), jnp.where(odd, keep, other)], 0)
-
+    states = by_place([before[n] + reach[n] * state_before for n in range(4)], flags)
+    adjoints = by_place([after[n] + back[n] * adjoint_after for n in range(4)], flags)
+    messages = [both(states[d], adjoints[d], top_scale, top_scale, top_scale) for d in (1, 2, 3)]
+    received = [swap(m, d + 1, 0).astype(F32) for d, m in enumerate(messages)]
+    scales = [jnp.exp2(got[2 * part : 2 * part + 1]) for got in received]
+    states = [states[0]] + [got[:part] * s for got, s in zip(received, scales)]
+    adjoints = [adjoints[0]] + [got[part : 2 * part] * s for got, s in zip(received, scales)]
     return (
-        joined(state_keep, got[:half] * scale),
-        joined(adjoint_keep, got[half : 2 * half] * scale),
+        jnp.concatenate(by_place(states, flags), 0),
+        jnp.concatenate(by_place(adjoints, flags), 0),
     )
 
 

time: 87.2 us -> 80.5 us (0.923)
  waiting for transfers between devices: 32.2 us -> 22.6 us
  starting transfers between devices: 26.2 us -> 29 us
    ppermute x18 -> x20, waiting for transfers between devices: 32.2 us -> 22.6 us  [swap(): lax.ppermute(value, ('tm', 'tile'), [(i, i ^ mask) for i in range(count)])]
    ppermute x18 -> x20, starting transfers between devices: 24.7 us -> 27.5 us  [swap(): lax.ppermute(value, ('tm', 'tile'), [(i, i ^ mask) for i in range(count)])]
  transfers between devices with their start and end apart: 20 -> 22, of which waited for: 12 -> 13; matrix products, arithmetic and copies ran while one was open for 0% -> 0% of each run, Pallas kernels for 9% -> 9%
where the time goes in v4:
time: 80.5 us; the launch traced here: 80.2 us
  starting transfers between devices  29 us (36%)
  waiting for transfers between devices  22.6 us (28%)
  Pallas kernels  16.8 us (21%)
  local copies, waits for them, and re-layouts  6.04 us (8%)
  other arithmetic  4.44 us (6%)
  between operations  1.31 us (2%)
    ppermute x20, starting transfers between devices, swap(): lax.ppermute(value, ('tm', 'tile'), [(i, i ^ mask) for i in range(count)])  27.5 us
    ppermute x20, waiting for transfers between devices, swap(): lax.ppermute(value, ('tm', 'tile'), [(i, i ^ mask) for i in range(count)])  22.6 us
    pallas_call x2, Pallas kernels, output_call(): pl.pallas_call(functools.partial(output_kernel, flip=flip), in_specs=[pl....  7.21 us
    unnamed x20, local copies, waits for them, and re-layouts  5.08 us
    pallas_call x1, Pallas kernels, drive_call(): pl.pallas_call(drive_kernel, in_specs=[pl.BlockSpec(memory_space=pltpu.SM...  5.03 us
    pallas_call x1, Pallas kernels, grads_call(): pl.pallas_call(grads_kernel, in_specs=[pl.BlockSpec(memory_space=pltpu.SM...  4.36 us
    mul x2, other arithmetic, shards(): results.append((whole * factor).reshape(3, 3, ch, ch))  1.74 us
  transfers between devices with their start and end apart: 22, of which 13 were waited for; matrix products, arithmetic and copies ran while one was open for 0% of the time, Pallas kernels for 9%

profile of v4, /device:TPU:0, one launch (start us, length us, event | category | flops | bytes accessed | tf_op | source)
XLA Modules:
  0.0 80.2 jit_solution(18121379151999791083)
XLA Ops:
  0.6 0.1 pad_add_fusion.9.place
  0.8 1.0 %slice_bitcast_fusion.2 = (bf16[1,4,64,128]{3,2,1,0:T(8,128)(2,1)S(1)}, bf16[1,4,64,128]{3,2,1,0:T(8,128)(2,1)S(1)}, bf16[1,4,64,128]{3,2,1,0:T(8,128)(2,1)S(1)}, bf16[1,4,64,128]{3,2,1,0:T(8,128)(2,1)S(1)}) fusion(bf16[4,16,64,128]{3,2,1,0:T(8,128)(2,1)} %direct.3, bf16[4,16,64,128]{3,2,1,0:T(8,128)(2,1)} %direct.2), kind=kLoop, calls=%fused_computation.138 | loop fusion | bytes 524288 | tf_op jit(solution)/shard_map/stack;squeeze | solution.py:481
  1.8 0.7 collective-permute-start.1
  2.5 4.4 %collective-permute-start = (bf16[2,4,64,128]{3,2,1,0:T(8,128)(2,1)S(1)}, bf16[2,4,64,128]{3,2,1,0:T(8,128)(2,1)S(1)}, u32[]{:S(2)}, u32[]{:S(2)}) collective-permute-start(bf16[2,4,64,128]{3,2,1,0:T(8,128)(2,1)S(1)} %get-tuple-element.146), channel_id=1, source_target_pairs={{0,1},{1,0},{2,3},{3,2},{4,5},{5,4},{6,7},{7,6},{8,9},{9,8},{10,11... | collective-permute-start | bytes 393224 | tf_op jit(solution)/shard_map/ppermute | solution.py:340
  6.9 1.2 %copy-done = bf16[4,16,64,128]{3,2,1,0:T(8,128)(2,1)S(1)} copy-done((bf16[4,16,64,128]{3,2,1,0:T(8,128)(2,1)S(1)}, bf16[4,16,64,128]{3,2,1,0:T(8,128)(2,1)}, u32[]{:S(2)}) %copy-start) | copy-done | bytes 1048600
  8.1 1.2 %copy-done.2 = bf16[4,16,64,128]{3,2,1,0:T(8,128)(2,1)S(1)} copy-done((bf16[4,16,64,128]{3,2,1,0:T(8,128)(2,1)S(1)}, bf16[4,16,64,128]{3,2,1,0:T(8,128)(2,1)}, u32[]{:S(2)}) %copy-start.2) | copy-done | bytes 1048600
  9.4 1.0 %copy-done.4 = bf16[3,3,128,128]{3,2,1,0:T(8,128)(2,1)S(1)} copy-done((bf16[3,3,128,128]{3,2,1,0:T(8,128)(2,1)S(1)}, bf16[3,3,128,128]{3,2,1,0:T(8,128)(2,1)}, u32[]{:S(2)}) %copy-start.4) | copy-done | bytes 294936
  10.3 1.0 %copy-done.6 = bf16[3,3,128,128]{3,2,1,0:T(8,128)(2,1)S(1)} copy-done((bf16[3,3,128,128]{3,2,1,0:T(8,128)(2,1)S(1)}, bf16[3,3,128,128]{3,2,1,0:T(8,128)(2,1)}, u32[]{:S(2)}) %copy-start.6) | copy-done | bytes 294936
  11.3 0.7 copy-done.8
  12.0 0.2 blocks.1
  12.2 5.0 %drive.1 = (f32[4,512,256]{2,1,0:T(8,128)S(1)}, f32[4,512,256]{2,1,0:T(8,128)S(1)}, f32[512,256]{1,0:T(8,128)S(1)}, bf16[3,4,576,256]{3,2,1,0:T(8,128)(2,1)S(1)}...) custom-call(s32[2]{0:T(128)S(1)} %pad_add_fusion.9.place, bf16[4,16,64,128]{3,2,1,0:T(8,128)(2,1)S(1)} %copy-done, ...), custom_call_target="tpu_custom_call" | custom-call | flops 3221225472 | bytes 12582912 | tf_op jit(solution)/shard_map/drive/pallas_call | solution.py:181
  17.4 0.1 fusion.5
  17.5 1.6 %collective-permute-start.4 = (f16[272,256]{1,0:T(8,128)(2,1)S(1)}, f16[272,256]{1,0:T(8,128)(2,1)S(1)}, u32[]{:S(2)}, u32[]{:S(2)}) collective-permute-start(f16[272,256]{1,0:T(8,128)(2,1)S(1)} %get-tuple-element.166), channel_id=1, source_target_pairs={{0,4},{1,5},{2,6},{3,7},{4,0},{5,1},{6,2},{7,3},{8,12},{9,13},{10,... | collective-permute-start | bytes 417800 | tf_op jit(solution)/shard_map/ppermute | solution.py:340
  19.0 1.6 %collective-permute-start.3 = (f16[272,256]{1,0:T(8,128)(2,1)S(1)}, f16[272,256]{1,0:T(8,128)(2,1)S(1)}, u32[]{:S(2)}, u32[]{:S(2)}) collective-permute-start(f16[272,256]{1,0:T(8,128)(2,1)S(1)} %get-tuple-element.167), channel_id=1, source_target_pairs={{0,8},{1,9},{2,10},{3,11},{4,12},{5,13},{6,14},{7,15},{8,0},{9,1},... | collective-permute-start | bytes 417800 | tf_op jit(solution)/shard_map/ppermute | solution.py:340
  20.6 0.4 collective-permute-start.2
  21.0 2.1 %collective-permute-done.4 = f16[272,256]{1,0:T(8,128)(2,1)S(1)} collective-permute-done((f16[272,256]{1,0:T(8,128)(2,1)S(1)}, f16[272,256]{1,0:T(8,128)(2,1)S(1)}, u32[]{:S(2)}, u32[]{:S(2)}) %collective-permute-start.4) | collective-permute-done | bytes 139296 | tf_op jit(solution)/shard_map/ppermute | solution.py:340
  23.2 2.4 %collective-permute-done.3 = f16[272,256]{1,0:T(8,128)(2,1)S(1)} collective-permute-done((f16[272,256]{1,0:T(8,128)(2,1)S(1)}, f16[272,256]{1,0:T(8,128)(2,1)S(1)}, u32[]{:S(2)}, u32[]{:S(2)}) %collective-permute-start.3) | collective-permute-done | bytes 139296 | tf_op jit(solution)/shard_map/ppermute | solution.py:340
  25.6 1.7 %collective-permute-done.2 = f16[272,256]{1,0:T(8,128)(2,1)S(1)} collective-permute-done((f16[272,256]{1,0:T(8,128)(2,1)S(1)}, f16[272,256]{1,0:T(8,128)(2,1)S(1)}, u32[]{:S(2)}, u32[]{:S(2)}) %collective-permute-start.2) | collective-permute-done | bytes 139296 | tf_op jit(solution)/shard_map/ppermute | solution.py:340
  27.4 0.3 select_multiply_fusion.10
  27.7 2.7 %collective-permute-start.5 = (f16[144,256]{1,0:T(8,128)(2,1)S(1)}, f16[144,256]{1,0:T(8,128)(2,1)S(1)}, u32[]{:S(2)}, u32[]{:S(2)}) collective-permute-start(f16[144,256]{1,0:T(8,128)(2,1)S(1)} %add_convert_fusion.3), channel_id=1, source_target_pairs={{0,16},{1,17},{2,18},{3,19},{4,20},{5,21},{6,22},{7,23},{8,24},{9,... | collective-permute-start | bytes 221192 | tf_op jit(solution)/shard_map/ppermute | solution.py:340
  30.4 2.7 %collective-permute-done.5 = f16[144,256]{1,0:T(8,128)(2,1)S(1)} collective-permute-done((f16[144,256]{1,0:T(8,128)(2,1)S(1)}, f16[144,256]{1,0:T(8,128)(2,1)S(1)}, u32[]{:S(2)}, u32[]{:S(2)}) %collective-permute-start.5) | collective-permute-done | bytes 73760 | tf_op jit(solution)/shard_map/ppermute | solution.py:340
  33.1 0.1 select_multiply_fusion.7
  33.2 0.1 select_multiply_fusion.6
  33.3 0.1 select_multiply_fusion.4
  33.4 0.1 fusion.8
  33.5 1.6 %collective-permute-start.8 = (f16[272,256]{1,0:T(8,128)(2,1)S(1)}, f16[272,256]{1,0:T(8,128)(2,1)S(1)}, u32[]{:S(2)}, u32[]{:S(2)}) collective-permute-start(f16[272,256]{1,0:T(8,128)(2,1)S(1)} %get-tuple-element.169), channel_id=1, source_target_pairs={{0,4},{1,5},{2,6},{3,7},{4,0},{5,1},{6,2},{7,3},{8,12},{9,13},{10,... | collective-permute-start | bytes 417800 | tf_op jit(solution)/shard_map/ppermute | solution.py:340
  35.1 1.5 %collective-permute-start.6 = (f16[272,256]{1,0:T(8,128)(2,1)S(1)}, f16[272,256]{1,0:T(8,128)(2,1)S(1)}, u32[]{:S(2)}, u32[]{:S(2)}) collective-permute-start(f16[272,256]{1,0:T(8,128)(2,1)S(1)} %get-tuple-element.170), channel_id=1, source_target_pairs={{0,12},{1,13},{2,14},{3,15},{4,8},{5,9},{6,10},{7,11},{8,4},{9,5},... | collective-permute-start | bytes 417800 | tf_op jit(solution)/shard_map/ppermute | solution.py:340
  36.6 0.4 collective-permute-start.7
  37.1 2.6 %collective-permute-done.8 = f16[272,256]{1,0:T(8,128)(2,1)S(1)} collective-permute-done((f16[272,256]{1,0:T(8,128)(2,1)S(1)}, f16[272,256]{1,0:T(8,128)(2,1)S(1)}, u32[]{:S(2)}, u32[]{:S(2)}) %collective-permute-start.8) | collective-permute-done | bytes 139296 | tf_op jit(solution)/shard_map/ppermute | solution.py:340
  39.7 1.4 %collective-permute-done.6 = f16[272,256]{1,0:T(8,128)(2,1)S(1)} collective-permute-done((f16[272,256]{1,0:T(8,128)(2,1)S(1)}, f16[272,256]{1,0:T(8,128)(2,1)S(1)}, u32[]{:S(2)}, u32[]{:S(2)}) %collective-permute-start.6) | collective-permute-done | bytes 139296 | tf_op jit(solution)/shard_map/ppermute | solution.py:340
  41.2 1.1 %collective-permute-done.7 = f16[272,256]{1,0:T(8,128)(2,1)S(1)} collective-permute-done((f16[272,256]{1,0:T(8,128)(2,1)S(1)}, f16[272,256]{1,0:T(8,128)(2,1)S(1)}, u32[]{:S(2)}, u32[]{:S(2)}) %collective-permute-start.7) | collective-permute-done | bytes 139296 | tf_op jit(solution)/shard_map/ppermute | solution.py:340
  42.3 0.1 broadcast_select_fusion.16
  42.4 0.1 broadcast_select_fusion.21
  42.5 0.1 broadcast_select_fusion.14
  42.7 4.4 %grads.1 = (bf16[4,512,256]{2,1,0:T(8,128)(2,1)S(1)}, bf16[4,512,256]{2,1,0:T(8,128)(2,1)S(1)}, bf16[2,4,64,128]{3,2,1,0:T(8,128)(2,1)S(1)}, bf16[2,4,64,128]{3,...) custom-call(s32[2]{0:T(128)S(1)} %pad_add_fusion.9.place, ...), custom_call_target="tpu_custom_call" | custom-call | flops 3221225472 | bytes 12582912 | tf_op jit(solution)/shard_map/grads/pallas_call | solution.py:286
  47.1 0.1 select_multiply_fusion
  47.2 0.1 collective-permute-start.9
  47.3 0.5 collective-permute-start.13
  47.8 0.8 %collective-permute-start.14 = (bf16[2,4,64,128]{3,2,1,0:T(8,128)(2,1)S(1)}, bf16[2,4,64,128]{3,2,1,0:T(8,128)(2,1)S(1)}, u32[]{:S(2)}, u32[]{:S(2)}) collective-permute-start(bf16[2,4,64,128]{3,2,1,0:T(8,128)(2,1)S(1)} %get-tuple-element.47), channel_id=1, source_target_pairs={{1,2},{2,1},{5,6},{6,5},{9,10},{10,9},{13,14},{14,13},{17,18},{18,... | collective-permute-start | bytes 393224 | tf_op jit(solution)/shard_map/ppermute | solution.py:348
  48.6 0.2 collective-permute-done.9
  48.9 0.1 fusion.2
  49.1 0.9 %collective-permute-start.10 = (f16[304,128]{1,0:T(8,128)(2,1)S(1)}, f16[304,128]{1,0:T(8,128)(2,1)S(1)}, u32[]{:S(2)}, u32[]{:S(2)}) collective-permute-start(f16[304,128]{1,0:T(8,128)(2,1)S(1)} %get-tuple-element.42), channel_id=1, source_target_pairs={{0,4},{1,5},{2,6},{3,7},{4,0},{5,1},{6,2},{7,3},{8,12},{9,13},{10,... | collective-permute-start | bytes 233480 | tf_op jit(solution)/shard_map/ppermute | solution.py:340
  50.0 2.7 %collective-permute-start.11 = (f16[304,128]{1,0:T(8,128)(2,1)S(1)}, f16[304,128]{1,0:T(8,128)(2,1)S(1)}, u32[]{:S(2)}, u32[]{:S(2)}) collective-permute-start(f16[304,128]{1,0:T(8,128)(2,1)S(1)} %get-tuple-element.43), channel_id=1, source_target_pairs={{0,2},{1,3},{2,0},{3,1},{4,6},{5,7},{6,4},{7,5},{8,10},{9,11},{10,... | collective-permute-start | bytes 233480 | tf_op jit(solution)/shard_map/ppermute | solution.py:340
  52.8 0.6 collective-permute-start.12
  53.4 3.6 %output.1 = bf16[4,16,64,128]{3,2,1,0:T(8,128)(2,1)} custom-call(s32[2]{0:T(128)S(1)} %pad_add_fusion.9.place, bf16[4,8,64,256]{3,2,1,0:T(8,128)(2,1)S(1)} %bitcast.147, bf16[2,4,64,128]{3,2,1,0:T(8,128)(2,1)S(1)} %collective-permute-done.13.first, bf16[2,4,64,128]{3,2,1,0:T(8,128)(2,1)S(1)} %collective-permute-done.14.second, ...), custom_call_target="tpu_custom_call" | custom-call | flops 1610612736 | bytes 4194304 | tf_op jit(solution)/shard_map/output/pallas_call | solution.py:319
  57.1 1.0 %collective-permute-done.12 = f16[304,128]{1,0:T(8,128)(2,1)S(1)} collective-permute-done((f16[304,128]{1,0:T(8,128)(2,1)S(1)}, f16[304,128]{1,0:T(8,128)(2,1)S(1)}, u32[]{:S(2)}, u32[]{:S(2)}) %collective-permute-start.12) | collective-permute-done | bytes 77856 | tf_op jit(solution)/shard_map/ppermute | solution.py:340
  58.1 0.1 fusion.17
  58.2 4.2 %collective-permute-start.17 = (f16[304,128]{1,0:T(8,128)(2,1)S(1)}, f16[304,128]{1,0:T(8,128)(2,1)S(1)}, u32[]{:S(2)}, u32[]{:S(2)}) collective-permute-start(f16[304,128]{1,0:T(8,128)(2,1)S(1)} %add_convert_fusion.2), channel_id=1, source_target_pairs={{0,24},{1,25},{2,26},{3,27},{4,28},{5,29},{6,30},{7,31},{8,16},{9,... | collective-permute-start | bytes 233480 | tf_op jit(solution)/shard_map/ppermute | solution.py:340
  62.5 0.6 collective-permute-start.15
  63.1 3.6 %grad_frames.1 = bf16[4,16,64,128]{3,2,1,0:T(8,128)(2,1)} custom-call(s32[2]{0:T(128)S(1)} %pad_add_fusion.9.place, bf16[4,8,64,256]{3,2,1,0:T(8,128)(2,1)S(1)} %bitcast.146, bf16[2,4,64,128]{3,2,1,0:T(8,128)(2,1)S(1)} %collective-permute-done.13.first, bf16[2,4,64,128]{3,2,1,0:T(8,128)(2,1)S(1)} %collective-permute-done.14.second, ...), custom_call_target="tpu_custom_call" | custom-call | flops 1610612736 | bytes 4194304 | tf_op jit(solution)/shard_map/grad_frames/pallas_call | solution.py:319
  66.8 1.8 %collective-permute-done.16 = f16[304,128]{1,0:T(8,128)(2,1)S(1)} collective-permute-done((f16[304,128]{1,0:T(8,128)(2,1)S(1)}, f16[304,128]{1,0:T(8,128)(2,1)S(1)}, u32[]{:S(2)}, u32[]{:S(2)}) %collective-permute-start.16) | collective-permute-done | bytes 77856 | tf_op jit(solution)/shard_map/ppermute | solution.py:340
  68.6 0.1 fusion.14
  68.7 1.5 %collective-permute-start.20 = (f16[304,128]{1,0:T(8,128)(2,1)S(1)}, f16[304,128]{1,0:T(8,128)(2,1)S(1)}, u32[]{:S(2)}, u32[]{:S(2)}) collective-permute-start(f16[304,128]{1,0:T(8,128)(2,1)S(1)} %add_convert_fusion.1), channel_id=1, source_target_pairs={{0,4},{1,5},{2,6},{3,7},{4,0},{5,1},{6,2},{7,3},{8,12},{9,13},{10,... | collective-permute-start | bytes 233480 | tf_op jit(solution)/shard_map/ppermute | solution.py:340
  70.2 2.0 %collective-permute-start.18 = (f16[304,128]{1,0:T(8,128)(2,1)S(1)}, f16[304,128]{1,0:T(8,128)(2,1)S(1)}, u32[]{:S(2)}, u32[]{:S(2)}) collective-permute-start(f16[304,128]{1,0:T(8,128)(2,1)S(1)} %add_convert_fusion.1), channel_id=1, source_target_pairs={{0,6},{1,7},{2,4},{3,5},{4,2},{5,3},{6,0},{7,1},{8,14},{9,15},{10,... | collective-permute-start | bytes 233480 | tf_op jit(solution)/shard_map/ppermute | solution.py:340
  72.2 0.9 %collective-permute-done.20 = f16[304,128]{1,0:T(8,128)(2,1)S(1)} collective-permute-done((f16[304,128]{1,0:T(8,128)(2,1)S(1)}, f16[304,128]{1,0:T(8,128)(2,1)S(1)}, u32[]{:S(2)}, u32[]{:S(2)}) %collective-permute-start.20) | collective-permute-done | bytes 77856 | tf_op jit(solution)/shard_map/ppermute | solution.py:340
  73.2 3.0 %collective-permute-done.19 = f16[304,128]{1,0:T(8,128)(2,1)S(1)} collective-permute-done((f16[304,128]{1,0:T(8,128)(2,1)S(1)}, f16[304,128]{1,0:T(8,128)(2,1)S(1)}, u32[]{:S(2)}, u32[]{:S(2)}) %collective-permute-start.19) | collective-permute-done | bytes 77856 | tf_op jit(solution)/shard_map/ppermute | solution.py:340
  76.2 0.1 broadcast_select_fusion.9
  76.3 0.1 broadcast_select_fusion.3
  76.4 0.1 pad_maximum_fusion.2
  76.5 0.1 collective-permute-start.21
  76.6 1.6 %collective-permute-done.21 = f16[1216,128]{1,0:T(8,128)(2,1)S(1)} collective-permute-done((f16[1216,128]{1,0:T(8,128)(2,1)S(1)}, f16[1216,128]{1,0:T(8,128)(2,1)S(1)}, u32[]{:S(2)}, u32[]{:S(2)}) %collective-permute-start.21) | collective-permute-done | bytes 311328 | tf_op jit(solution)/shard_map/ppermute | solution.py:340
  78.1 0.2 broadcast_select_fusion
  78.4 0.9 %fusion.1 = f32[4,288,128]{2,1,0:T(8,128)} fusion(f32[4,304,128]{2,1,0:T(8,128)S(1)} %convert.2, f32[4,128]{1,0:T(4,128)S(1)} %bitcast.182), kind=kLoop, calls=%fused_computation.4 | loop fusion | flops 294912 | bytes 1181696 | tf_op jit(solution)/shard_map/mul | solution.py:575
  79.3 0.9 %fusion = f32[4,288,128]{2,1,0:T(8,128)} fusion(f32[4,304,128]{2,1,0:T(8,128)S(1)} %convert.3, f32[4,128]{1,0:T(4,128)S(1)} %bitcast.183), kind=kLoop, calls=%fused_computation.2 | loop fusion | flops 294912 | bytes 1181696 | tf_op jit(solution)/shard_map/mul | solution.py:575
  (75 shorter events, 1.1 us)
Async XLA Ops:
  1.8 10.3 %collective-permute-start.1 = (bf16[2,4,64,128]{3,2,1,0:T(8,128)(2,1)S(1)}, bf16[2,4,64,128]{3,2,1,0:T(8,128)(2,1)S(1)}, u32[]{:S(2)}, u32[]{:S(2)}) collective-permute-start(bf16[2,4,64,128]{3,2,1,0:T(8,128)(2,1)S(1)} %get-tuple-element.145), channel_id=1, source_target_pairs={{1,2},{2,1},{5,6},{6,5},{9,10},{10,9},{13,14},{14,13},{17,18},{18,... | collective-permute-start | bytes 393224 | tf_op jit(solution)/shard_map/ppermute | solution.py:348
  2.5 9.7 %collective-permute-start = (bf16[2,4,64,128]{3,2,1,0:T(8,128)(2,1)S(1)}, bf16[2,4,64,128]{3,2,1,0:T(8,128)(2,1)S(1)}, u32[]{:S(2)}, u32[]{:S(2)}) collective-permute-start(bf16[2,4,64,128]{3,2,1,0:T(8,128)(2,1)S(1)} %get-tuple-element.146), channel_id=1, source_target_pairs={{0,1},{1,0},{2,3},{3,2},{4,5},{5,4},{6,7},{7,6},{8,9},{9,8},{10,11... | collective-permute-start | bytes 393224 | tf_op jit(solution)/shard_map/ppermute | solution.py:340
  6.9 1.2 %copy-start = (bf16[4,16,64,128]{3,2,1,0:T(8,128)(2,1)S(1)}, bf16[4,16,64,128]{3,2,1,0:T(8,128)(2,1)}, u32[]{:S(2)}) copy-start(bf16[4,16,64,128]{3,2,1,0:T(8,128)(2,1)} %direct.2) | copy-start | bytes 3145732
  8.1 1.2 %copy-start.2 = (bf16[4,16,64,128]{3,2,1,0:T(8,128)(2,1)S(1)}, bf16[4,16,64,128]{3,2,1,0:T(8,128)(2,1)}, u32[]{:S(2)}) copy-start(bf16[4,16,64,128]{3,2,1,0:T(8,128)(2,1)} %direct.3) | copy-start | bytes 3145732
  9.4 1.0 %copy-start.4 = (bf16[3,3,128,128]{3,2,1,0:T(8,128)(2,1)S(1)}, bf16[3,3,128,128]{3,2,1,0:T(8,128)(2,1)}, u32[]{:S(2)}) copy-start(bf16[3,3,128,128]{3,2,1,0:T(8,128)(2,1)} %weight.2) | copy-start | bytes 884740
  10.3 1.0 %copy-start.6 = (bf16[3,3,128,128]{3,2,1,0:T(8,128)(2,1)S(1)}, bf16[3,3,128,128]{3,2,1,0:T(8,128)(2,1)}, u32[]{:S(2)}) copy-start(bf16[3,3,128,128]{3,2,1,0:T(8,128)(2,1)} %weight.3) | copy-start | bytes 884740
  11.3 0.7 copy-start.8
  17.5 5.7 %collective-permute-start.4 = (f16[272,256]{1,0:T(8,128)(2,1)S(1)}, f16[272,256]{1,0:T(8,128)(2,1)S(1)}, u32[]{:S(2)}, u32[]{:S(2)}) collective-permute-start(f16[272,256]{1,0:T(8,128)(2,1)S(1)} %get-tuple-element.166), channel_id=1, source_target_pairs={{0,4},{1,5},{2,6},{3,7},{4,0},{5,1},{6,2},{7,3},{8,12},{9,13},{10,... | collective-permute-start | bytes 417800 | tf_op jit(solution)/shard_map/ppermute | solution.py:340
  19.0 6.6 %collective-permute-start.3 = (f16[272,256]{1,0:T(8,128)(2,1)S(1)}, f16[272,256]{1,0:T(8,128)(2,1)S(1)}, u32[]{:S(2)}, u32[]{:S(2)}) collective-permute-start(f16[272,256]{1,0:T(8,128)(2,1)S(1)} %get-tuple-element.167), channel_id=1, source_target_pairs={{0,8},{1,9},{2,10},{3,11},{4,12},{5,13},{6,14},{7,15},{8,0},{9,1},... | collective-permute-start | bytes 417800 | tf_op jit(solution)/shard_map/ppermute | solution.py:340
  20.6 6.7 %collective-permute-start.2 = (f16[272,256]{1,0:T(8,128)(2,1)S(1)}, f16[272,256]{1,0:T(8,128)(2,1)S(1)}, u32[]{:S(2)}, u32[]{:S(2)}) collective-permute-start(f16[272,256]{1,0:T(8,128)(2,1)S(1)} %get-tuple-element.168), channel_id=1, source_target_pairs={{0,12},{1,13},{2,14},{3,15},{4,8},{5,9},{6,10},{7,11},{8,4},{9,5},... | collective-permute-start | bytes 417800 | tf_op jit(solution)/shard_map/ppermute | solution.py:340
  27.7 5.3 %collective-permute-start.5 = (f16[144,256]{1,0:T(8,128)(2,1)S(1)}, f16[144,256]{1,0:T(8,128)(2,1)S(1)}, u32[]{:S(2)}, u32[]{:S(2)}) collective-permute-start(f16[144,256]{1,0:T(8,128)(2,1)S(1)} %add_convert_fusion.3), channel_id=1, source_target_pairs={{0,16},{1,17},{2,18},{3,19},{4,20},{5,21},{6,22},{7,23},{8,24},{9,... | collective-permute-start | bytes 221192 | tf_op jit(solution)/shard_map/ppermute | solution.py:340
  33.5 6.1 %collective-permute-start.8 = (f16[272,256]{1,0:T(8,128)(2,1)S(1)}, f16[272,256]{1,0:T(8,128)(2,1)S(1)}, u32[]{:S(2)}, u32[]{:S(2)}) collective-permute-start(f16[272,256]{1,0:T(8,128)(2,1)S(1)} %get-tuple-element.169), channel_id=1, source_target_pairs={{0,4},{1,5},{2,6},{3,7},{4,0},{5,1},{6,2},{7,3},{8,12},{9,13},{10,... | collective-permute-start | bytes 417800 | tf_op jit(solution)/shard_map/ppermute | solution.py:340
  35.1 6.1 %collective-permute-start.6 = (f16[272,256]{1,0:T(8,128)(2,1)S(1)}, f16[272,256]{1,0:T(8,128)(2,1)S(1)}, u32[]{:S(2)}, u32[]{:S(2)}) collective-permute-start(f16[272,256]{1,0:T(8,128)(2,1)S(1)} %get-tuple-element.170), channel_id=1, source_target_pairs={{0,12},{1,13},{2,14},{3,15},{4,8},{5,9},{6,10},{7,11},{8,4},{9,5},... | collective-permute-start | bytes 417800 | tf_op jit(solution)/shard_map/ppermute | solution.py:340
  36.6 5.7 %collective-permute-start.7 = (f16[272,256]{1,0:T(8,128)(2,1)S(1)}, f16[272,256]{1,0:T(8,128)(2,1)S(1)}, u32[]{:S(2)}, u32[]{:S(2)}) collective-permute-start(f16[272,256]{1,0:T(8,128)(2,1)S(1)} %get-tuple-element.171), channel_id=1, source_target_pairs={{0,8},{1,9},{2,10},{3,11},{4,12},{5,13},{6,14},{7,15},{8,0},{9,1},... | collective-permute-start | bytes 417800 | tf_op jit(solution)/shard_map/ppermute | solution.py:340
  47.2 1.7 %collective-permute-start.9 = (f16[1168,128]{1,0:T(8,128)(2,1)S(1)}, f16[1168,128]{1,0:T(8,128)(2,1)S(1)}, u32[]{:S(2)}, u32[]{:S(2)}) collective-permute-start(f16[1168,128]{1,0:T(8,128)(2,1)S(1)} %add_convert_fusion), channel_id=1, source_target_pairs={{0,1},{1,0},{2,3},{3,2},{4,5},{5,4},{6,7},{7,6},{8,9},{9,8},{10,11... | collective-permute-start | bytes 897032 | tf_op jit(solution)/shard_map/ppermute | solution.py:340
  47.3 6.1 %collective-permute-start.13 = (bf16[2,4,64,128]{3,2,1,0:T(8,128)(2,1)S(1)}, bf16[2,4,64,128]{3,2,1,0:T(8,128)(2,1)S(1)}, u32[]{:S(2)}, u32[]{:S(2)}) collective-permute-start(bf16[2,4,64,128]{3,2,1,0:T(8,128)(2,1)S(1)} %get-tuple-element.46), channel_id=1, source_target_pairs={{0,1},{1,0},{2,3},{3,2},{4,5},{5,4},{6,7},{7,6},{8,9},{9,8},{10,11... | collective-permute-start | bytes 393224 | tf_op jit(solution)/shard_map/ppermute | solution.py:340
  47.8 5.7 %collective-permute-start.14 = (bf16[2,4,64,128]{3,2,1,0:T(8,128)(2,1)S(1)}, bf16[2,4,64,128]{3,2,1,0:T(8,128)(2,1)S(1)}, u32[]{:S(2)}, u32[]{:S(2)}) collective-permute-start(bf16[2,4,64,128]{3,2,1,0:T(8,128)(2,1)S(1)} %get-tuple-element.47), channel_id=1, source_target_pairs={{1,2},{2,1},{5,6},{6,5},{9,10},{10,9},{13,14},{14,13},{17,18},{18,... | collective-permute-start | bytes 393224 | tf_op jit(solution)/shard_map/ppermute | solution.py:348
  48.9 4.5 %copy-start.1 = (bf16[4,16,64,128]{3,2,1,0:T(8,128)(2,1)S(1)}, bf16[4,16,64,128]{3,2,1,0:T(8,128)(2,1)}, u32[]{:S(2)}) copy-start(bf16[4,16,64,128]{3,2,1,0:T(8,128)(2,1)} %direct.2) | copy-start | bytes 3145732
  48.9 4.5 %copy-start.5 = (bf16[3,3,128,128]{3,2,1,0:T(8,128)(2,1)S(1)}, bf16[3,3,128,128]{3,2,1,0:T(8,128)(2,1)}, u32[]{:S(2)}) copy-start(bf16[3,3,128,128]{3,2,1,0:T(8,128)(2,1)} %weight.2) | copy-start | bytes 884740
  48.9 4.5 %copy-start.9 = (f32[128]{0:T(128)S(1)}, f32[128]{0:T(128)}, u32[]{:S(2)}) copy-start(f32[128]{0:T(128)} %param.10) | copy-start | bytes 1540
  49.1 7.9 %collective-permute-start.10 = (f16[304,128]{1,0:T(8,128)(2,1)S(1)}, f16[304,128]{1,0:T(8,128)(2,1)S(1)}, u32[]{:S(2)}, u32[]{:S(2)}) collective-permute-start(f16[304,128]{1,0:T(8,128)(2,1)S(1)} %get-tuple-element.42), channel_id=1, source_target_pairs={{0,4},{1,5},{2,6},{3,7},{4,0},{5,1},{6,2},{7,3},{8,12},{9,13},{10,... | collective-permute-start | bytes 233480 | tf_op jit(solution)/shard_map/ppermute | solution.py:340
  50.0 7.0 %collective-permute-start.11 = (f16[304,128]{1,0:T(8,128)(2,1)S(1)}, f16[304,128]{1,0:T(8,128)(2,1)S(1)}, u32[]{:S(2)}, u32[]{:S(2)}) collective-permute-start(f16[304,128]{1,0:T(8,128)(2,1)S(1)} %get-tuple-element.43), channel_id=1, source_target_pairs={{0,2},{1,3},{2,0},{3,1},{4,6},{5,7},{6,4},{7,5},{8,10},{9,11},{10,... | collective-permute-start | bytes 233480 | tf_op jit(solution)/shard_map/ppermute | solution.py:340
  52.8 5.3 %collective-permute-start.12 = (f16[304,128]{1,0:T(8,128)(2,1)S(1)}, f16[304,128]{1,0:T(8,128)(2,1)S(1)}, u32[]{:S(2)}, u32[]{:S(2)}) collective-permute-start(f16[304,128]{1,0:T(8,128)(2,1)S(1)} %get-tuple-element.44), channel_id=1, source_target_pairs={{0,6},{1,7},{2,4},{3,5},{4,2},{5,3},{6,0},{7,1},{8,14},{9,15},{10,... | collective-permute-start | bytes 233480 | tf_op jit(solution)/shard_map/ppermute | solution.py:340
  57.1 6.1 %copy-start.3 = (bf16[4,16,64,128]{3,2,1,0:T(8,128)(2,1)S(1)}, bf16[4,16,64,128]{3,2,1,0:T(8,128)(2,1)}, u32[]{:S(2)}) copy-start(bf16[4,16,64,128]{3,2,1,0:T(8,128)(2,1)} %direct.3) | copy-start | bytes 3145732
  57.1 6.1 %copy-start.7 = (bf16[3,3,128,128]{3,2,1,0:T(8,128)(2,1)S(1)}, bf16[3,3,128,128]{3,2,1,0:T(8,128)(2,1)}, u32[]{:S(2)}) copy-start(bf16[3,3,128,128]{3,2,1,0:T(8,128)(2,1)} %weight.3) | copy-start | bytes 884740
  58.2 8.5 %collective-permute-start.17 = (f16[304,128]{1,0:T(8,128)(2,1)S(1)}, f16[304,128]{1,0:T(8,128)(2,1)S(1)}, u32[]{:S(2)}, u32[]{:S(2)}) collective-permute-start(f16[304,128]{1,0:T(8,128)(2,1)S(1)} %add_convert_fusion.2), channel_id=1, source_target_pairs={{0,24},{1,25},{2,26},{3,27},{4,28},{5,29},{6,30},{7,31},{8,16},{9,... | collective-permute-start | bytes 233480 | tf_op jit(solution)/shard_map/ppermute | solution.py:340
  62.5 6.1 %collective-permute-start.16 = (f16[304,128]{1,0:T(8,128)(2,1)S(1)}, f16[304,128]{1,0:T(8,128)(2,1)S(1)}, u32[]{:S(2)}, u32[]{:S(2)}) collective-permute-start(f16[304,128]{1,0:T(8,128)(2,1)S(1)} %add_convert_fusion.2), channel_id=1, source_target_pairs={{0,16},{1,17},{2,18},{3,19},{4,20},{5,21},{6,22},{7,23},{8,24},{9,... | collective-permute-start | bytes 233480 | tf_op jit(solution)/shard_map/ppermute | solution.py:340
  62.5 6.1 %collective-permute-start.15 = (f16[304,128]{1,0:T(8,128)(2,1)S(1)}, f16[304,128]{1,0:T(8,128)(2,1)S(1)}, u32[]{:S(2)}, u32[]{:S(2)}) collective-permute-start(f16[304,128]{1,0:T(8,128)(2,1)S(1)} %add_convert_fusion.2), channel_id=1, source_target_pairs={{0,8},{1,9},{2,10},{3,11},{4,12},{5,13},{6,14},{7,15},{8,0},{9,1},... | collective-permute-start | bytes 233480 | tf_op jit(solution)/shard_map/ppermute | solution.py:340
  68.7 4.5 %collective-permute-start.20 = (f16[304,128]{1,0:T(8,128)(2,1)S(1)}, f16[304,128]{1,0:T(8,128)(2,1)S(1)}, u32[]{:S(2)}, u32[]{:S(2)}) collective-permute-start(f16[304,128]{1,0:T(8,128)(2,1)S(1)} %add_convert_fusion.1), channel_id=1, source_target_pairs={{0,4},{1,5},{2,6},{3,7},{4,0},{5,1},{6,2},{7,3},{8,12},{9,13},{10,... | collective-permute-start | bytes 233480 | tf_op jit(solution)/shard_map/ppermute | solution.py:340
  70.2 6.0 %collective-permute-start.19 = (f16[304,128]{1,0:T(8,128)(2,1)S(1)}, f16[304,128]{1,0:T(8,128)(2,1)S(1)}, u32[]{:S(2)}, u32[]{:S(2)}) collective-permute-start(f16[304,128]{1,0:T(8,128)(2,1)S(1)} %add_convert_fusion.1), channel_id=1, source_target_pairs={{0,2},{1,3},{2,0},{3,1},{4,6},{5,7},{6,4},{7,5},{8,10},{9,11},{10,... | collective-permute-start | bytes 233480 | tf_op jit(solution)/shard_map/ppermute | solution.py:340
  70.2 6.0 %collective-permute-start.18 = (f16[304,128]{1,0:T(8,128)(2,1)S(1)}, f16[304,128]{1,0:T(8,128)(2,1)S(1)}, u32[]{:S(2)}, u32[]{:S(2)}) collective-permute-start(f16[304,128]{1,0:T(8,128)(2,1)S(1)} %add_convert_fusion.1), channel_id=1, source_target_pairs={{0,6},{1,7},{2,4},{3,5},{4,2},{5,3},{6,0},{7,1},{8,14},{9,15},{10,... | collective-permute-start | bytes 233480 | tf_op jit(solution)/shard_map/ppermute | solution.py:340
  76.5 1.7 %collective-permute-start.21 = (f16[1216,128]{1,0:T(8,128)(2,1)S(1)}, f16[1216,128]{1,0:T(8,128)(2,1)S(1)}, u32[]{:S(2)}, u32[]{:S(2)}) collective-permute-start(f16[1216,128]{1,0:T(8,128)(2,1)S(1)} %pad_maximum_fusion.2), channel_id=1, source_target_pairs={{0,1},{1,0},{2,3},{3,2},{4,5},{5,4},{6,7},{7,6},{8,9},{9,8},{10,11... | collective-permute-start | bytes 933896 | tf_op jit(solution)/shard_map/ppermute | solution.py:340

commit v5 on v4

--- a/solution.py
+++ b/solution.py
@@ -98,26 +98,25 @@
     return rate, reach, tail
 
 
-def blocks_kernel(frames, cotangent, w_in, w_out, log_decay, blocks):
-    fill_weights(blocks.at[0], w_in, False)
-    fill_weights(blocks.at[1], w_out, True)
-
-
-def blocks_call(frames, cotangent, w_in, w_out, log_decay):
-    ch = w_in.shape[2]
+def blocks_kernel(fields, weights, log_decay, blocks):
+    fill_weights(blocks.at[0], weights.at[0], False)
+    fill_weights(blocks.at[1], weights.at[1], True)
+
+
+def blocks_call(fields, weights, log_decay):
+    ch = weights.shape[3]
     return pl.pallas_call(
         blocks_kernel,
         out_shape=jax.ShapeDtypeStruct((2, 3, 2, 2 * ch, 2 * ch), BF16),
         compiler_params=pltpu.CompilerParams(vmem_limit_bytes=VMEM_LIMIT),
         cost_estimate=pl.CostEstimate(flops=0, bytes_accessed=10 << 20, transcendentals=0),
         name="blocks",
-    )(frames, cotangent, w_in, w_out, log_decay)
+    )(fields, weights, log_decay)
 
 
 def drive_kernel(
     place,
-    frames,
-    cotangent,
+    fields,
     first,
     second,
     blocks,
@@ -130,15 +129,15 @@
     info,
     pairs,
 ):
-    times, rows, cols, ch = frames.shape
+    _, times, rows, cols, ch = fields.shape
     half = rows // 2
     odd = lax.rem(place[0], 2) == 1
     rate, reach, _ = decays(log_decay[...])
-    fields = ((frames, states, frame_taps), (cotangent, adjoints, cot_taps))
-    for index, (field, result, taps_out) in enumerate(fields):
+    results = ((states, frame_taps), (adjoints, cot_taps))
+    for index, (result, taps_out) in enumerate(results):
         flip = index == 1
         top, bottom = pick_halos(first, second, index, odd, times)
-        fill_pairs(pairs.at[index], field, top, bottom)
+        fill_pairs(pairs.at[index], fields.at[index], top, bottom)
         carry = None
         for step in range(times):
             t = times - 1 - step if flip else step
@@ -172,8 +171,8 @@
         info[7 + d : 8 + d, :] = row + (lax.div(place[1], 4) ^ d).astype(F32)
 
 
-def drive_call(place, frames, cotangent, first, second, blocks, log_decay):
-    times, rows, cols, ch = frames.shape
+def drive_call(place, fields, first, second, blocks, log_decay):
+    _, times, rows, cols, ch = fields.shape
     half = rows // 2
     field = jax.ShapeDtypeStruct((times, half * cols, 2 * ch), F32)
     rows_info = (7 + lax.axis_size("tm") // 4 + 15) // 16 * 16
@@ -181,7 +180,7 @@
     return pl.pallas_call(
         drive_kernel,
         in_specs=[pl.BlockSpec(memory_space=pltpu.SMEM)]
-        + [pl.BlockSpec(memory_space=pltpu.VMEM)] * 6,
+        + [pl.BlockSpec(memory_space=pltpu.VMEM)] * 5,
         out_shape=(
             field,
             field,
@@ -198,7 +197,7 @@
             flops=times * rows * cols * ch * ch * 48, bytes_accessed=12 << 20, transcendentals=0
         ),
         name="drive",
-    )(place, frames, cotangent, first, second, blocks, log_decay)
+    )(place, fields, first, second, blocks, log_decay)
 
 
 def grads_kernel(
@@ -483,9 +482,10 @@
     second = swap_across(jnp.where(odd, high, low))
     first = swap(jnp.where(odd, low, high), 0, 1)
 
-    blocks = blocks_call(frames, cotangent, w_in, w_out, log_decay)
+    fields = jnp.stack([frames, cotangent])
+    blocks = blocks_call(fields, jnp.stack([w_in, w_out]), log_decay)
     states, adjoints, leaving, frame_taps, cot_taps, info = drive_call(
-        place, frames, cotangent, first, second, blocks, log_decay
+        place, fields, first, second, blocks, log_decay
     )
     state_in, adjoint_in = carry_over(states[-1], leaving, info)
     states_bf, inflow_bf, first, second, in_part, out_part, info = grads_call(

time: 80.5 us -> 77.5 us (0.963)
  local copies, waits for them, and re-layouts: 6.04 us -> 0.99 us
  other arithmetic: 4.44 us -> 6.37 us
    unnamed x20 -> x12, local copies, waits for them, and re-layouts: 5.08 us -> 0.03 us
    another operation x0 -> x2, other arithmetic: none -> 1.85 us  [the longest x1 1.79 us: shards(): fields = jnp.stack([frames, cotangent])]
  transfers between devices with their start and end apart: 22 -> 22, of which waited for: 13 -> 13; matrix products, arithmetic and copies ran while one was open for 0% -> 3% of each run, Pallas kernels for 9% -> 10%
where the time goes in v5:
time: 77.5 us; the launch traced here: 77.3 us
  starting transfers between devices  28.9 us (37%)
  waiting for transfers between devices  22.9 us (30%)
  Pallas kernels  16.8 us (22%)
  other arithmetic  6.37 us (8%)
  between operations  1.32 us (2%)
  local copies, waits for them, and re-layouts  0.99 us (1%)
    ppermute x20, starting transfers between devices, swap(): lax.ppermute(value, ('tm', 'tile'), [(i, i ^ mask) for i in range(count)])  27.4 us
    ppermute x20, waiting for transfers between devices, swap(): lax.ppermute(value, ('tm', 'tile'), [(i, i ^ mask) for i in range(count)])  22.9 us
    pallas_call x2, Pallas kernels, output_call(): pl.pallas_call(functools.partial(output_kernel, flip=flip), in_specs=[pl....  7.23 us
    pallas_call x1, Pallas kernels, drive_call(): pl.pallas_call(drive_kernel, in_specs=[pl.BlockSpec(memory_space=pltpu.SM...  5.06 us
    pallas_call x1, Pallas kernels, grads_call(): pl.pallas_call(grads_kernel, in_specs=[pl.BlockSpec(memory_space=pltpu.SM...  4.33 us
    another operation x1, other arithmetic, shards(): fields = jnp.stack([frames, cotangent])  1.79 us
    mul x2, other arithmetic, shards(): results.append((whole * factor).reshape(3, 3, ch, ch))  1.74 us
  transfers between devices with their start and end apart: 22, of which 13 were waited for; matrix products, arithmetic and copies ran while one was open for 3% of the time, Pallas kernels for 10%

profile of v5, /device:TPU:0, one launch (start us, length us, event | category | flops | bytes accessed | tf_op | source)
XLA Modules:
  0.0 77.3 jit_solution(11354602585518556033)
XLA Ops:
  0.6 0.1 pad_add_fusion.9.place
  0.8 1.0 %slice_bitcast_fusion.2 = (bf16[1,4,64,128]{3,2,1,0:T(8,128)(2,1)S(1)}, bf16[1,4,64,128]{3,2,1,0:T(8,128)(2,1)S(1)}, bf16[1,4,64,128]{3,2,1,0:T(8,128)(2,1)S(1)}, bf16[1,4,64,128]{3,2,1,0:T(8,128)(2,1)S(1)}) fusion(bf16[4,16,64,128]{3,2,1,0:T(8,128)(2,1)} %direct.3, bf16[4,16,64,128]{3,2,1,0:T(8,128)(2,1)} %direct.2), kind=kLoop, calls=%fused_computation.140 | loop fusion | bytes 524288 | tf_op jit(solution)/shard_map/stack;squeeze | solution.py:480
  1.8 0.7 collective-permute-start.1
  2.5 4.4 %collective-permute-start = (bf16[2,4,64,128]{3,2,1,0:T(8,128)(2,1)S(1)}, bf16[2,4,64,128]{3,2,1,0:T(8,128)(2,1)S(1)}, u32[]{:S(2)}, u32[]{:S(2)}) collective-permute-start(bf16[2,4,64,128]{3,2,1,0:T(8,128)(2,1)S(1)} %get-tuple-element.146), channel_id=1, source_target_pairs={{0,1},{1,0},{2,3},{3,2},{4,5},{5,4},{6,7},{7,6},{8,9},{9,8},{10,11... | collective-permute-start | bytes 393224 | tf_op jit(solution)/shard_map/ppermute | solution.py:339
  6.9 1.8 %pad_maximum_fusion.fields = bf16[2,4,16,64,128]{4,3,2,1,0:T(8,128)(2,1)S(1)} fusion(bf16[1,4,16,64,128]{4,3,2,1,0:T(8,128)(2,1)} %bitcast.148, bf16[1,4,16,64,128]{4,3,2,1,0:T(8,128)(2,1)} %bitcast.147), kind=kLoop, calls=%fused_computation | loop fusion | flops 1048576 | bytes 4194304 | tf_op jit(solution)/shard_map/stack | solution.py:485
  8.7 0.1 pad_maximum_fusion.1.weights
  8.8 0.2 blocks.1
  9.0 5.1 %drive.1 = (f32[4,512,256]{2,1,0:T(8,128)S(1)}, f32[4,512,256]{2,1,0:T(8,128)S(1)}, f32[512,256]{1,0:T(8,128)S(1)}, bf16[3,4,576,256]{3,2,1,0:T(8,128)(2,1)S(1)}...) custom-call(s32[2]{0:T(128)S(1)} %pad_add_fusion.9.place, ...), custom_call_target="tpu_custom_call" | custom-call | flops 3221225472 | bytes 12582912 | tf_op jit(solution)/shard_map/drive/pallas_call | solution.py:180
  14.2 0.1 select_multiply_fusion.11
  14.2 0.1 select_multiply_fusion.12
  14.3 0.1 fusion.5
  14.4 1.6 %collective-permute-start.4 = (f16[272,256]{1,0:T(8,128)(2,1)S(1)}, f16[272,256]{1,0:T(8,128)(2,1)S(1)}, u32[]{:S(2)}, u32[]{:S(2)}) collective-permute-start(f16[272,256]{1,0:T(8,128)(2,1)S(1)} %get-tuple-element.166), channel_id=1, source_target_pairs={{0,4},{1,5},{2,6},{3,7},{4,0},{5,1},{6,2},{7,3},{8,12},{9,13},{10,... | collective-permute-start | bytes 417800 | tf_op jit(solution)/shard_map/ppermute | solution.py:339
  15.9 1.6 %collective-permute-start.3 = (f16[272,256]{1,0:T(8,128)(2,1)S(1)}, f16[272,256]{1,0:T(8,128)(2,1)S(1)}, u32[]{:S(2)}, u32[]{:S(2)}) collective-permute-start(f16[272,256]{1,0:T(8,128)(2,1)S(1)} %get-tuple-element.167), channel_id=1, source_target_pairs={{0,8},{1,9},{2,10},{3,11},{4,12},{5,13},{6,14},{7,15},{8,0},{9,1},... | collective-permute-start | bytes 417800 | tf_op jit(solution)/shard_map/ppermute | solution.py:339
  17.5 0.4 collective-permute-start.2
  17.9 2.5 %collective-permute-done.4 = f16[272,256]{1,0:T(8,128)(2,1)S(1)} collective-permute-done((f16[272,256]{1,0:T(8,128)(2,1)S(1)}, f16[272,256]{1,0:T(8,128)(2,1)S(1)}, u32[]{:S(2)}, u32[]{:S(2)}) %collective-permute-start.4) | collective-permute-done | bytes 139296 | tf_op jit(solution)/shard_map/ppermute | solution.py:339
  20.5 2.0 %collective-permute-done.3 = f16[272,256]{1,0:T(8,128)(2,1)S(1)} collective-permute-done((f16[272,256]{1,0:T(8,128)(2,1)S(1)}, f16[272,256]{1,0:T(8,128)(2,1)S(1)}, u32[]{:S(2)}, u32[]{:S(2)}) %collective-permute-start.3) | collective-permute-done | bytes 139296 | tf_op jit(solution)/shard_map/ppermute | solution.py:339
  22.5 2.1 %collective-permute-done.2 = f16[272,256]{1,0:T(8,128)(2,1)S(1)} collective-permute-done((f16[272,256]{1,0:T(8,128)(2,1)S(1)}, f16[272,256]{1,0:T(8,128)(2,1)S(1)}, u32[]{:S(2)}, u32[]{:S(2)}) %collective-permute-start.2) | collective-permute-done | bytes 139296 | tf_op jit(solution)/shard_map/ppermute | solution.py:339
  24.8 0.3 select_multiply_fusion.10
  25.1 2.7 %collective-permute-start.5 = (f16[144,256]{1,0:T(8,128)(2,1)S(1)}, f16[144,256]{1,0:T(8,128)(2,1)S(1)}, u32[]{:S(2)}, u32[]{:S(2)}) collective-permute-start(f16[144,256]{1,0:T(8,128)(2,1)S(1)} %add_convert_fusion.3), channel_id=1, source_target_pairs={{0,16},{1,17},{2,18},{3,19},{4,20},{5,21},{6,22},{7,23},{8,24},{9,... | collective-permute-start | bytes 221192 | tf_op jit(solution)/shard_map/ppermute | solution.py:339
  27.7 2.8 %collective-permute-done.5 = f16[144,256]{1,0:T(8,128)(2,1)S(1)} collective-permute-done((f16[144,256]{1,0:T(8,128)(2,1)S(1)}, f16[144,256]{1,0:T(8,128)(2,1)S(1)}, u32[]{:S(2)}, u32[]{:S(2)}) %collective-permute-start.5) | collective-permute-done | bytes 73760 | tf_op jit(solution)/shard_map/ppermute | solution.py:339
  30.6 0.1 select_multiply_fusion.7
  30.7 0.1 select_multiply_fusion.6
  30.8 0.1 select_multiply_fusion.4
  30.9 0.1 fusion.8
  31.0 1.6 %collective-permute-start.8 = (f16[272,256]{1,0:T(8,128)(2,1)S(1)}, f16[272,256]{1,0:T(8,128)(2,1)S(1)}, u32[]{:S(2)}, u32[]{:S(2)}) collective-permute-start(f16[272,256]{1,0:T(8,128)(2,1)S(1)} %get-tuple-element.169), channel_id=1, source_target_pairs={{0,4},{1,5},{2,6},{3,7},{4,0},{5,1},{6,2},{7,3},{8,12},{9,13},{10,... | collective-permute-start | bytes 417800 | tf_op jit(solution)/shard_map/ppermute | solution.py:339
  32.6 1.4 %collective-permute-start.6 = (f16[272,256]{1,0:T(8,128)(2,1)S(1)}, f16[272,256]{1,0:T(8,128)(2,1)S(1)}, u32[]{:S(2)}, u32[]{:S(2)}) collective-permute-start(f16[272,256]{1,0:T(8,128)(2,1)S(1)} %get-tuple-element.170), channel_id=1, source_target_pairs={{0,12},{1,13},{2,14},{3,15},{4,8},{5,9},{6,10},{7,11},{8,4},{9,5},... | collective-permute-start | bytes 417800 | tf_op jit(solution)/shard_map/ppermute | solution.py:339
  34.0 0.6 collective-permute-start.7
  34.6 2.2 %collective-permute-done.8 = f16[272,256]{1,0:T(8,128)(2,1)S(1)} collective-permute-done((f16[272,256]{1,0:T(8,128)(2,1)S(1)}, f16[272,256]{1,0:T(8,128)(2,1)S(1)}, u32[]{:S(2)}, u32[]{:S(2)}) %collective-permute-start.8) | collective-permute-done | bytes 139296 | tf_op jit(solution)/shard_map/ppermute | solution.py:339
  36.8 1.7 %collective-permute-done.6 = f16[272,256]{1,0:T(8,128)(2,1)S(1)} collective-permute-done((f16[272,256]{1,0:T(8,128)(2,1)S(1)}, f16[272,256]{1,0:T(8,128)(2,1)S(1)}, u32[]{:S(2)}, u32[]{:S(2)}) %collective-permute-start.6) | collective-permute-done | bytes 139296 | tf_op jit(solution)/shard_map/ppermute | solution.py:339
  38.6 0.6 collective-permute-done.7
  39.2 0.1 broadcast_select_fusion.16
  39.2 0.1 broadcast_select_fusion.21
  39.3 0.1 broadcast_select_fusion.14
  39.5 4.3 %grads.1 = (bf16[4,512,256]{2,1,0:T(8,128)(2,1)S(1)}, bf16[4,512,256]{2,1,0:T(8,128)(2,1)S(1)}, bf16[2,4,64,128]{3,2,1,0:T(8,128)(2,1)S(1)}, bf16[2,4,64,128]{3,...) custom-call(s32[2]{0:T(128)S(1)} %pad_add_fusion.9.place, ...), custom_call_target="tpu_custom_call" | custom-call | flops 3221225472 | bytes 12582912 | tf_op jit(solution)/shard_map/grads/pallas_call | solution.py:285
  43.8 0.1 select_multiply_fusion
  44.0 0.1 collective-permute-start.9
  44.0 0.5 collective-permute-start.13
  44.5 0.8 %collective-permute-start.14 = (bf16[2,4,64,128]{3,2,1,0:T(8,128)(2,1)S(1)}, bf16[2,4,64,128]{3,2,1,0:T(8,128)(2,1)S(1)}, u32[]{:S(2)}, u32[]{:S(2)}) collective-permute-start(bf16[2,4,64,128]{3,2,1,0:T(8,128)(2,1)S(1)} %get-tuple-element.47), channel_id=1, source_target_pairs={{1,2},{2,1},{5,6},{6,5},{9,10},{10,9},{13,14},{14,13},{17,18},{18,... | collective-permute-start | bytes 393224 | tf_op jit(solution)/shard_map/ppermute | solution.py:347
  45.4 0.2 collective-permute-done.9
  45.7 0.1 fusion.2
  45.8 0.1 select_multiply_fusion.1
  46.0 1.5 %collective-permute-start.10 = (f16[304,128]{1,0:T(8,128)(2,1)S(1)}, f16[304,128]{1,0:T(8,128)(2,1)S(1)}, u32[]{:S(2)}, u32[]{:S(2)}) collective-permute-start(f16[304,128]{1,0:T(8,128)(2,1)S(1)} %get-tuple-element.42), channel_id=1, source_target_pairs={{0,4},{1,5},{2,6},{3,7},{4,0},{5,1},{6,2},{7,3},{8,12},{9,13},{10,... | collective-permute-start | bytes 233480 | tf_op jit(solution)/shard_map/ppermute | solution.py:339
  47.5 2.7 %collective-permute-start.11 = (f16[304,128]{1,0:T(8,128)(2,1)S(1)}, f16[304,128]{1,0:T(8,128)(2,1)S(1)}, u32[]{:S(2)}, u32[]{:S(2)}) collective-permute-start(f16[304,128]{1,0:T(8,128)(2,1)S(1)} %get-tuple-element.43), channel_id=1, source_target_pairs={{0,2},{1,3},{2,0},{3,1},{4,6},{5,7},{6,4},{7,5},{8,10},{9,11},{10,... | collective-permute-start | bytes 233480 | tf_op jit(solution)/shard_map/ppermute | solution.py:339
  50.2 3.6 %output.1 = bf16[4,16,64,128]{3,2,1,0:T(8,128)(2,1)} custom-call(s32[2]{0:T(128)S(1)} %pad_add_fusion.9.place, bf16[4,8,64,256]{3,2,1,0:T(8,128)(2,1)S(1)} %bitcast.155, bf16[2,4,64,128]{3,2,1,0:T(8,128)(2,1)S(1)} %collective-permute-done.13.first, bf16[2,4,64,128]{3,2,1,0:T(8,128)(2,1)S(1)} %collective-permute-done.14.second, ...), custom_call_target="tpu_custom_call" | custom-call | flops 1610612736 | bytes 4194304 | tf_op jit(solution)/shard_map/output/pallas_call | solution.py:318
  53.9 1.6 %collective-permute-done.12 = f16[304,128]{1,0:T(8,128)(2,1)S(1)} collective-permute-done((f16[304,128]{1,0:T(8,128)(2,1)S(1)}, f16[304,128]{1,0:T(8,128)(2,1)S(1)}, u32[]{:S(2)}, u32[]{:S(2)}) %collective-permute-start.12) | collective-permute-done | bytes 77856 | tf_op jit(solution)/shard_map/ppermute | solution.py:339
  55.5 0.1 fusion.17
  55.6 4.2 %collective-permute-start.17 = (f16[304,128]{1,0:T(8,128)(2,1)S(1)}, f16[304,128]{1,0:T(8,128)(2,1)S(1)}, u32[]{:S(2)}, u32[]{:S(2)}) collective-permute-start(f16[304,128]{1,0:T(8,128)(2,1)S(1)} %add_convert_fusion.2), channel_id=1, source_target_pairs={{0,24},{1,25},{2,26},{3,27},{4,28},{5,29},{6,30},{7,31},{8,16},{9,... | collective-permute-start | bytes 233480 | tf_op jit(solution)/shard_map/ppermute | solution.py:339
  59.8 0.6 collective-permute-start.15
  60.5 3.6 %grad_frames.1 = bf16[4,16,64,128]{3,2,1,0:T(8,128)(2,1)} custom-call(s32[2]{0:T(128)S(1)} %pad_add_fusion.9.place, bf16[4,8,64,256]{3,2,1,0:T(8,128)(2,1)S(1)} %bitcast.154, bf16[2,4,64,128]{3,2,1,0:T(8,128)(2,1)S(1)} %collective-permute-done.13.first, bf16[2,4,64,128]{3,2,1,0:T(8,128)(2,1)S(1)} %collective-permute-done.14.second, ...), custom_call_target="tpu_custom_call" | custom-call | flops 1610612736 | bytes 4194304 | tf_op jit(solution)/shard_map/grad_frames/pallas_call | solution.py:318
  64.1 1.9 %collective-permute-done.16 = f16[304,128]{1,0:T(8,128)(2,1)S(1)} collective-permute-done((f16[304,128]{1,0:T(8,128)(2,1)S(1)}, f16[304,128]{1,0:T(8,128)(2,1)S(1)}, u32[]{:S(2)}, u32[]{:S(2)}) %collective-permute-start.16) | collective-permute-done | bytes 77856 | tf_op jit(solution)/shard_map/ppermute | solution.py:339
  66.0 0.1 fusion.14
  66.1 1.5 %collective-permute-start.20 = (f16[304,128]{1,0:T(8,128)(2,1)S(1)}, f16[304,128]{1,0:T(8,128)(2,1)S(1)}, u32[]{:S(2)}, u32[]{:S(2)}) collective-permute-start(f16[304,128]{1,0:T(8,128)(2,1)S(1)} %add_convert_fusion.1), channel_id=1, source_target_pairs={{0,4},{1,5},{2,6},{3,7},{4,0},{5,1},{6,2},{7,3},{8,12},{9,13},{10,... | collective-permute-start | bytes 233480 | tf_op jit(solution)/shard_map/ppermute | solution.py:339
  67.7 0.1 collective-permute-start.19
  67.8 1.9 %collective-permute-start.18 = (f16[304,128]{1,0:T(8,128)(2,1)S(1)}, f16[304,128]{1,0:T(8,128)(2,1)S(1)}, u32[]{:S(2)}, u32[]{:S(2)}) collective-permute-start(f16[304,128]{1,0:T(8,128)(2,1)S(1)} %add_convert_fusion.1), channel_id=1, source_target_pairs={{0,6},{1,7},{2,4},{3,5},{4,2},{5,3},{6,0},{7,1},{8,14},{9,15},{10,... | collective-permute-start | bytes 233480 | tf_op jit(solution)/shard_map/ppermute | solution.py:339
  69.7 0.9 %collective-permute-done.20 = f16[304,128]{1,0:T(8,128)(2,1)S(1)} collective-permute-done((f16[304,128]{1,0:T(8,128)(2,1)S(1)}, f16[304,128]{1,0:T(8,128)(2,1)S(1)}, u32[]{:S(2)}, u32[]{:S(2)}) %collective-permute-start.20) | collective-permute-done | bytes 77856 | tf_op jit(solution)/shard_map/ppermute | solution.py:339
  70.6 2.7 %collective-permute-done.19 = f16[304,128]{1,0:T(8,128)(2,1)S(1)} collective-permute-done((f16[304,128]{1,0:T(8,128)(2,1)S(1)}, f16[304,128]{1,0:T(8,128)(2,1)S(1)}, u32[]{:S(2)}, u32[]{:S(2)}) %collective-permute-start.19) | collective-permute-done | bytes 77856 | tf_op jit(solution)/shard_map/ppermute | solution.py:339
  73.3 0.1 broadcast_select_fusion.9
  73.4 0.1 broadcast_select_fusion.3
  73.5 0.1 pad_maximum_fusion.4
  73.6 0.1 collective-permute-start.21
  73.7 1.6 %collective-permute-done.21 = f16[1216,128]{1,0:T(8,128)(2,1)S(1)} collective-permute-done((f16[1216,128]{1,0:T(8,128)(2,1)S(1)}, f16[1216,128]{1,0:T(8,128)(2,1)S(1)}, u32[]{:S(2)}, u32[]{:S(2)}) %collective-permute-start.21) | collective-permute-done | bytes 311328 | tf_op jit(solution)/shard_map/ppermute | solution.py:339
  75.3 0.2 broadcast_select_fusion
  75.5 0.9 %fusion.1 = f32[4,288,128]{2,1,0:T(8,128)} fusion(f32[4,304,128]{2,1,0:T(8,128)S(1)} %convert.2, f32[4,128]{1,0:T(4,128)S(1)} %bitcast.190), kind=kLoop, calls=%fused_computation.5 | loop fusion | flops 294912 | bytes 1181696 | tf_op jit(solution)/shard_map/mul | solution.py:575
  76.4 0.9 %fusion = f32[4,288,128]{2,1,0:T(8,128)} fusion(f32[4,304,128]{2,1,0:T(8,128)S(1)} %convert.3, f32[4,128]{1,0:T(4,128)S(1)} %bitcast.191), kind=kLoop, calls=%fused_computation.3 | loop fusion | flops 294912 | bytes 1181696 | tf_op jit(solution)/shard_map/mul | solution.py:575
  (69 shorter events, 0.9 us)
Async XLA Ops:
  1.8 7.2 %collective-permute-start.1 = (bf16[2,4,64,128]{3,2,1,0:T(8,128)(2,1)S(1)}, bf16[2,4,64,128]{3,2,1,0:T(8,128)(2,1)S(1)}, u32[]{:S(2)}, u32[]{:S(2)}) collective-permute-start(bf16[2,4,64,128]{3,2,1,0:T(8,128)(2,1)S(1)} %get-tuple-element.145), channel_id=1, source_target_pairs={{1,2},{2,1},{5,6},{6,5},{9,10},{10,9},{13,14},{14,13},{17,18},{18,... | collective-permute-start | bytes 393224 | tf_op jit(solution)/shard_map/ppermute | solution.py:347
  2.5 6.5 %collective-permute-start = (bf16[2,4,64,128]{3,2,1,0:T(8,128)(2,1)S(1)}, bf16[2,4,64,128]{3,2,1,0:T(8,128)(2,1)S(1)}, u32[]{:S(2)}, u32[]{:S(2)}) collective-permute-start(bf16[2,4,64,128]{3,2,1,0:T(8,128)(2,1)S(1)} %get-tuple-element.146), channel_id=1, source_target_pairs={{0,1},{1,0},{2,3},{3,2},{4,5},{5,4},{6,7},{7,6},{8,9},{9,8},{10,11... | collective-permute-start | bytes 393224 | tf_op jit(solution)/shard_map/ppermute | solution.py:339
  6.9 1.8 %copy-start.2 = (bf16[3,3,128,128]{3,2,1,0:T(8,128)(2,1)S(1)}, bf16[3,3,128,128]{3,2,1,0:T(8,128)(2,1)}, u32[]{:S(2)}) copy-start(bf16[3,3,128,128]{3,2,1,0:T(8,128)(2,1)} %weight.2) | copy-start | bytes 884740
  6.9 1.8 %copy-start.3 = (bf16[3,3,128,128]{3,2,1,0:T(8,128)(2,1)S(1)}, bf16[3,3,128,128]{3,2,1,0:T(8,128)(2,1)}, u32[]{:S(2)}) copy-start(bf16[3,3,128,128]{3,2,1,0:T(8,128)(2,1)} %weight.3) | copy-start | bytes 884740
  6.9 1.9 %copy-start.4 = (f32[4,128]{1,0:T(4,128)S(1)}, f32[4,128]{1,0:T(4,128)}, u32[]{:S(2)}) copy-start(f32[4,128]{1,0:T(4,128)} %log_decay.5) | copy-start | bytes 6148
  14.4 6.1 %collective-permute-start.4 = (f16[272,256]{1,0:T(8,128)(2,1)S(1)}, f16[272,256]{1,0:T(8,128)(2,1)S(1)}, u32[]{:S(2)}, u32[]{:S(2)}) collective-permute-start(f16[272,256]{1,0:T(8,128)(2,1)S(1)} %get-tuple-element.166), channel_id=1, source_target_pairs={{0,4},{1,5},{2,6},{3,7},{4,0},{5,1},{6,2},{7,3},{8,12},{9,13},{10,... | collective-permute-start | bytes 417800 | tf_op jit(solution)/shard_map/ppermute | solution.py:339
  15.9 6.5 %collective-permute-start.3 = (f16[272,256]{1,0:T(8,128)(2,1)S(1)}, f16[272,256]{1,0:T(8,128)(2,1)S(1)}, u32[]{:S(2)}, u32[]{:S(2)}) collective-permute-start(f16[272,256]{1,0:T(8,128)(2,1)S(1)} %get-tuple-element.167), channel_id=1, source_target_pairs={{0,8},{1,9},{2,10},{3,11},{4,12},{5,13},{6,14},{7,15},{8,0},{9,1},... | collective-permute-start | bytes 417800 | tf_op jit(solution)/shard_map/ppermute | solution.py:339
  17.5 7.1 %collective-permute-start.2 = (f16[272,256]{1,0:T(8,128)(2,1)S(1)}, f16[272,256]{1,0:T(8,128)(2,1)S(1)}, u32[]{:S(2)}, u32[]{:S(2)}) collective-permute-start(f16[272,256]{1,0:T(8,128)(2,1)S(1)} %get-tuple-element.168), channel_id=1, source_target_pairs={{0,12},{1,13},{2,14},{3,15},{4,8},{5,9},{6,10},{7,11},{8,4},{9,5},... | collective-permute-start | bytes 417800 | tf_op jit(solution)/shard_map/ppermute | solution.py:339
  25.1 5.5 %collective-permute-start.5 = (f16[144,256]{1,0:T(8,128)(2,1)S(1)}, f16[144,256]{1,0:T(8,128)(2,1)S(1)}, u32[]{:S(2)}, u32[]{:S(2)}) collective-permute-start(f16[144,256]{1,0:T(8,128)(2,1)S(1)} %add_convert_fusion.3), channel_id=1, source_target_pairs={{0,16},{1,17},{2,18},{3,19},{4,20},{5,21},{6,22},{7,23},{8,24},{9,... | collective-permute-start | bytes 221192 | tf_op jit(solution)/shard_map/ppermute | solution.py:339
  31.0 5.8 %collective-permute-start.8 = (f16[272,256]{1,0:T(8,128)(2,1)S(1)}, f16[272,256]{1,0:T(8,128)(2,1)S(1)}, u32[]{:S(2)}, u32[]{:S(2)}) collective-permute-start(f16[272,256]{1,0:T(8,128)(2,1)S(1)} %get-tuple-element.169), channel_id=1, source_target_pairs={{0,4},{1,5},{2,6},{3,7},{4,0},{5,1},{6,2},{7,3},{8,12},{9,13},{10,... | collective-permute-start | bytes 417800 | tf_op jit(solution)/shard_map/ppermute | solution.py:339
  32.6 6.0 %collective-permute-start.6 = (f16[272,256]{1,0:T(8,128)(2,1)S(1)}, f16[272,256]{1,0:T(8,128)(2,1)S(1)}, u32[]{:S(2)}, u32[]{:S(2)}) collective-permute-start(f16[272,256]{1,0:T(8,128)(2,1)S(1)} %get-tuple-element.170), channel_id=1, source_target_pairs={{0,12},{1,13},{2,14},{3,15},{4,8},{5,9},{6,10},{7,11},{8,4},{9,5},... | collective-permute-start | bytes 417800 | tf_op jit(solution)/shard_map/ppermute | solution.py:339
  34.0 5.2 %collective-permute-start.7 = (f16[272,256]{1,0:T(8,128)(2,1)S(1)}, f16[272,256]{1,0:T(8,128)(2,1)S(1)}, u32[]{:S(2)}, u32[]{:S(2)}) collective-permute-start(f16[272,256]{1,0:T(8,128)(2,1)S(1)} %get-tuple-element.171), channel_id=1, source_target_pairs={{0,8},{1,9},{2,10},{3,11},{4,12},{5,13},{6,14},{7,15},{8,0},{9,1},... | collective-permute-start | bytes 417800 | tf_op jit(solution)/shard_map/ppermute | solution.py:339
  44.0 1.7 %collective-permute-start.9 = (f16[1168,128]{1,0:T(8,128)(2,1)S(1)}, f16[1168,128]{1,0:T(8,128)(2,1)S(1)}, u32[]{:S(2)}, u32[]{:S(2)}) collective-permute-start(f16[1168,128]{1,0:T(8,128)(2,1)S(1)} %add_convert_fusion), channel_id=1, source_target_pairs={{0,1},{1,0},{2,3},{3,2},{4,5},{5,4},{6,7},{7,6},{8,9},{9,8},{10,11... | collective-permute-start | bytes 897032 | tf_op jit(solution)/shard_map/ppermute | solution.py:339
  44.0 6.2 %collective-permute-start.13 = (bf16[2,4,64,128]{3,2,1,0:T(8,128)(2,1)S(1)}, bf16[2,4,64,128]{3,2,1,0:T(8,128)(2,1)S(1)}, u32[]{:S(2)}, u32[]{:S(2)}) collective-permute-start(bf16[2,4,64,128]{3,2,1,0:T(8,128)(2,1)S(1)} %get-tuple-element.46), channel_id=1, source_target_pairs={{0,1},{1,0},{2,3},{3,2},{4,5},{5,4},{6,7},{7,6},{8,9},{9,8},{10,11... | collective-permute-start | bytes 393224 | tf_op jit(solution)/shard_map/ppermute | solution.py:339
  44.5 5.7 %collective-permute-start.14 = (bf16[2,4,64,128]{3,2,1,0:T(8,128)(2,1)S(1)}, bf16[2,4,64,128]{3,2,1,0:T(8,128)(2,1)S(1)}, u32[]{:S(2)}, u32[]{:S(2)}) collective-permute-start(bf16[2,4,64,128]{3,2,1,0:T(8,128)(2,1)S(1)} %get-tuple-element.47), channel_id=1, source_target_pairs={{1,2},{2,1},{5,6},{6,5},{9,10},{10,9},{13,14},{14,13},{17,18},{18,... | collective-permute-start | bytes 393224 | tf_op jit(solution)/shard_map/ppermute | solution.py:347
  45.7 4.6 %copy-start = (bf16[4,16,64,128]{3,2,1,0:T(8,128)(2,1)S(1)}, bf16[4,16,64,128]{3,2,1,0:T(8,128)(2,1)}, u32[]{:S(2)}) copy-start(bf16[4,16,64,128]{3,2,1,0:T(8,128)(2,1)} %direct.2) | copy-start | bytes 3145732
  45.7 4.5 %copy-start.5 = (f32[128]{0:T(128)S(1)}, f32[128]{0:T(128)}, u32[]{:S(2)}) copy-start(f32[128]{0:T(128)} %param.10) | copy-start | bytes 1540
  46.0 7.9 %collective-permute-start.10 = (f16[304,128]{1,0:T(8,128)(2,1)S(1)}, f16[304,128]{1,0:T(8,128)(2,1)S(1)}, u32[]{:S(2)}, u32[]{:S(2)}) collective-permute-start(f16[304,128]{1,0:T(8,128)(2,1)S(1)} %get-tuple-element.42), channel_id=1, source_target_pairs={{0,4},{1,5},{2,6},{3,7},{4,0},{5,1},{6,2},{7,3},{8,12},{9,13},{10,... | collective-permute-start | bytes 233480 | tf_op jit(solution)/shard_map/ppermute | solution.py:339
  47.5 6.4 %collective-permute-start.11 = (f16[304,128]{1,0:T(8,128)(2,1)S(1)}, f16[304,128]{1,0:T(8,128)(2,1)S(1)}, u32[]{:S(2)}, u32[]{:S(2)}) collective-permute-start(f16[304,128]{1,0:T(8,128)(2,1)S(1)} %get-tuple-element.43), channel_id=1, source_target_pairs={{0,2},{1,3},{2,0},{3,1},{4,6},{5,7},{6,4},{7,5},{8,10},{9,11},{10,... | collective-permute-start | bytes 233480 | tf_op jit(solution)/shard_map/ppermute | solution.py:339
  50.2 5.3 %collective-permute-start.12 = (f16[304,128]{1,0:T(8,128)(2,1)S(1)}, f16[304,128]{1,0:T(8,128)(2,1)S(1)}, u32[]{:S(2)}, u32[]{:S(2)}) collective-permute-start(f16[304,128]{1,0:T(8,128)(2,1)S(1)} %get-tuple-element.44), channel_id=1, source_target_pairs={{0,6},{1,7},{2,4},{3,5},{4,2},{5,3},{6,0},{7,1},{8,14},{9,15},{10,... | collective-permute-start | bytes 233480 | tf_op jit(solution)/shard_map/ppermute | solution.py:339
  53.9 6.6 %copy-start.1 = (bf16[4,16,64,128]{3,2,1,0:T(8,128)(2,1)S(1)}, bf16[4,16,64,128]{3,2,1,0:T(8,128)(2,1)}, u32[]{:S(2)}) copy-start(bf16[4,16,64,128]{3,2,1,0:T(8,128)(2,1)} %direct.3) | copy-start | bytes 3145732
  55.6 8.5 %collective-permute-start.17 = (f16[304,128]{1,0:T(8,128)(2,1)S(1)}, f16[304,128]{1,0:T(8,128)(2,1)S(1)}, u32[]{:S(2)}, u32[]{:S(2)}) collective-permute-start(f16[304,128]{1,0:T(8,128)(2,1)S(1)} %add_convert_fusion.2), channel_id=1, source_target_pairs={{0,24},{1,25},{2,26},{3,27},{4,28},{5,29},{6,30},{7,31},{8,16},{9,... | collective-permute-start | bytes 233480 | tf_op jit(solution)/shard_map/ppermute | solution.py:339
  59.8 6.2 %collective-permute-start.16 = (f16[304,128]{1,0:T(8,128)(2,1)S(1)}, f16[304,128]{1,0:T(8,128)(2,1)S(1)}, u32[]{:S(2)}, u32[]{:S(2)}) collective-permute-start(f16[304,128]{1,0:T(8,128)(2,1)S(1)} %add_convert_fusion.2), channel_id=1, source_target_pairs={{0,16},{1,17},{2,18},{3,19},{4,20},{5,21},{6,22},{7,23},{8,24},{9,... | collective-permute-start | bytes 233480 | tf_op jit(solution)/shard_map/ppermute | solution.py:339
  59.8 6.2 %collective-permute-start.15 = (f16[304,128]{1,0:T(8,128)(2,1)S(1)}, f16[304,128]{1,0:T(8,128)(2,1)S(1)}, u32[]{:S(2)}, u32[]{:S(2)}) collective-permute-start(f16[304,128]{1,0:T(8,128)(2,1)S(1)} %add_convert_fusion.2), channel_id=1, source_target_pairs={{0,8},{1,9},{2,10},{3,11},{4,12},{5,13},{6,14},{7,15},{8,0},{9,1},... | collective-permute-start | bytes 233480 | tf_op jit(solution)/shard_map/ppermute | solution.py:339
  66.1 4.5 %collective-permute-start.20 = (f16[304,128]{1,0:T(8,128)(2,1)S(1)}, f16[304,128]{1,0:T(8,128)(2,1)S(1)}, u32[]{:S(2)}, u32[]{:S(2)}) collective-permute-start(f16[304,128]{1,0:T(8,128)(2,1)S(1)} %add_convert_fusion.1), channel_id=1, source_target_pairs={{0,4},{1,5},{2,6},{3,7},{4,0},{5,1},{6,2},{7,3},{8,12},{9,13},{10,... | collective-permute-start | bytes 233480 | tf_op jit(solution)/shard_map/ppermute | solution.py:339
  67.7 5.6 %collective-permute-start.19 = (f16[304,128]{1,0:T(8,128)(2,1)S(1)}, f16[304,128]{1,0:T(8,128)(2,1)S(1)}, u32[]{:S(2)}, u32[]{:S(2)}) collective-permute-start(f16[304,128]{1,0:T(8,128)(2,1)S(1)} %add_convert_fusion.1), channel_id=1, source_target_pairs={{0,2},{1,3},{2,0},{3,1},{4,6},{5,7},{6,4},{7,5},{8,10},{9,11},{10,... | collective-permute-start | bytes 233480 | tf_op jit(solution)/shard_map/ppermute | solution.py:339
  67.8 5.5 %collective-permute-start.18 = (f16[304,128]{1,0:T(8,128)(2,1)S(1)}, f16[304,128]{1,0:T(8,128)(2,1)S(1)}, u32[]{:S(2)}, u32[]{:S(2)}) collective-permute-start(f16[304,128]{1,0:T(8,128)(2,1)S(1)} %add_convert_fusion.1), channel_id=1, source_target_pairs={{0,6},{1,7},{2,4},{3,5},{4,2},{5,3},{6,0},{7,1},{8,14},{9,15},{10,... | collective-permute-start | bytes 233480 | tf_op jit(solution)/shard_map/ppermute | solution.py:339
  73.6 1.7 %collective-permute-start.21 = (f16[1216,128]{1,0:T(8,128)(2,1)S(1)}, f16[1216,128]{1,0:T(8,128)(2,1)S(1)}, u32[]{:S(2)}, u32[]{:S(2)}) collective-permute-start(f16[1216,128]{1,0:T(8,128)(2,1)S(1)} %pad_maximum_fusion.4), channel_id=1, source_target_pairs={{0,1},{1,0},{2,3},{3,2},{4,5},{5,4},{6,7},{7,6},{8,9},{9,8},{10,11... | collective-permute-start | bytes 933896 | tf_op jit(solution)/shard_map/ppermute | solution.py:339

commit v6 on v5

--- a/solution.py
+++ b/solution.py
@@ -522,7 +522,6 @@
     inflow_bf = inflow_bf.reshape(times, half, cols, 2 * ch)
     *messages, states_bf = lax.optimization_barrier((*messages, states_bf))
     received = [swap(m, *mask(d + 1)) for d, m in enumerate(messages)]
-    output = output_call(place, states_bf, first, second, w_out, gain, frames, False)
     for got in received:
         got, got_scale = unpacked(got)
         value = value + got
@@ -541,7 +540,7 @@
     for n in range(0, len(left), 2):
         group = left[n : n + 2]
         message = packed(value, scale, scale)
-        message, output, waiting = lax.optimization_barrier((message, output, waiting))
+        message, states_bf, waiting = lax.optimization_barrier((message, states_bf, waiting))
         terms = [message]
         for d in range(1, 2 ** len(group)):
             chosen = [b for k, b in enumerate(group) if d >> k & 1]
@@ -552,11 +551,13 @@
                 (a[0] + b[0], jnp.maximum(a[1], b[1])) for a, b in zip(terms[::2], terms[1::2])
             ]
         value, scale = terms[0]
+
+    output = output_call(place, states_bf, first, second, w_out, gain, frames, False)
+
+    message = packed(value, scale, scale)
+    message, output, waiting = lax.optimization_barrier((message, output, waiting))
+    gathered = [message] + [swap(message, *mask(d)) for d in range(1, parts)]
     grad_frames = output_call(place, waiting, first, second, w_in, gain, cotangent, True)
-
-    message = packed(value, scale, scale)
-    message, grad_frames = lax.optimization_barrier((message, grad_frames))
-    gathered = [message] + [swap(message, *mask(d)) for d in range(1, parts)]
     for _, high in bits:
         gathered = [
             (jnp.where(high, b, a), jnp.where(high, a, b))
@@ -564,15 +565,17 @@
         ]
         gathered = [jnp.concatenate(pair, 0) for pair in gathered]
     (mine,) = gathered
-    mine = lax.optimization_barrier(mine)
+    mine, grad_frames = lax.optimization_barrier((mine, grad_frames))
     theirs = swap(mine, 0, 1)
     factor = 1.0 / math.sqrt(
         times * lax.axis_size("tm") * rows * lax.axis_size("tile") * cols
     )
-    results = []
-    for chosen in (jnp.where(odd, theirs, mine), jnp.where(odd, mine, theirs)):
-        whole, _ = unpacked(chosen.reshape(parts, -1, ch))
-        results.append((whole * factor).reshape(3, 3, ch, ch))
+    mine, _ = unpacked(mine.reshape(parts, -1, ch))
+    theirs, _ = unpacked(theirs.reshape(parts, -1, ch))
+    results = [
+        (jnp.where(odd, a, b) * factor).reshape(3, 3, ch, ch)
+        for a, b in ((theirs, mine), (mine, theirs))
+    ]
     return (output, grad_frames, results[0], results[1])
 
 

time: 77.5 us -> 74.3 us (0.959)
  starting transfers between devices: 28.9 us -> 27.6 us
  waiting for transfers between devices: 22.9 us -> 21.8 us
  other arithmetic: 6.37 us -> 5.53 us
    ppermute x20, starting transfers between devices: 27.4 us -> 26.1 us  [swap(): lax.ppermute(value, ('tm', 'tile'), [(i, i ^ mask) for i in range(count)])]
    ppermute x20, waiting for transfers between devices: 22.9 us -> 21.8 us  [swap(): lax.ppermute(value, ('tm', 'tile'), [(i, i ^ mask) for i in range(count)])]
    mul x2 -> x1, other arithmetic: 1.74 us -> 1.14 us  [shards(): jnp.where(odd, a, b) * factor]
  transfers between devices with their start and end apart: 22 -> 22, of which waited for: 13 -> 12; matrix products, arithmetic and copies ran while one was open for 3% -> 3% of each run, Pallas kernels for 10% -> 10%
where the time goes in v6:
time: 74.3 us; the launch traced here: 74.1 us
  starting transfers between devices  27.6 us (37%)
  waiting for transfers between devices  21.8 us (29%)
  Pallas kernels  16.8 us (23%)
  other arithmetic  5.53 us (7%)
  between operations  1.33 us (2%)
  local copies, waits for them, and re-layouts  1 us (1%)
    ppermute x20, starting transfers between devices, swap(): lax.ppermute(value, ('tm', 'tile'), [(i, i ^ mask) for i in range(count)])  26.1 us
    ppermute x20, waiting for transfers between devices, swap(): lax.ppermute(value, ('tm', 'tile'), [(i, i ^ mask) for i in range(count)])  21.8 us
    pallas_call x2, Pallas kernels, output_call(): pl.pallas_call(functools.partial(output_kernel, flip=flip), in_specs=[pl....  7.23 us
    pallas_call x1, Pallas kernels, drive_call(): pl.pallas_call(drive_kernel, in_specs=[pl.BlockSpec(memory_space=pltpu.SM...  5.06 us
    pallas_call x1, Pallas kernels, grads_call(): pl.pallas_call(grads_kernel, in_specs=[pl.BlockSpec(memory_space=pltpu.SM...  4.33 us
    another operation x1, other arithmetic, shards(): fields = jnp.stack([frames, cotangent])  1.79 us
    ppermute x2, starting transfers between devices, swap_across(): return lax.ppermute(value, 'tile', pairs)  1.51 us
  transfers between devices with their start and end apart: 22, of which 12 were waited for; matrix products, arithmetic and copies ran while one was open for 3% of the time, Pallas kernels for 10%

profile of v6, /device:TPU:0, one launch (start us, length us, event | category | flops | bytes accessed | tf_op | source)
XLA Modules:
  0.0 74.1 jit_solution(17571892167743814068)
XLA Ops:
  0.6 0.1 pad_add_fusion.9.place
  0.8 1.0 %slice_bitcast_fusion.2 = (bf16[1,4,64,128]{3,2,1,0:T(8,128)(2,1)S(1)}, bf16[1,4,64,128]{3,2,1,0:T(8,128)(2,1)S(1)}, bf16[1,4,64,128]{3,2,1,0:T(8,128)(2,1)S(1)}, bf16[1,4,64,128]{3,2,1,0:T(8,128)(2,1)S(1)}) fusion(bf16[4,16,64,128]{3,2,1,0:T(8,128)(2,1)} %direct.3, bf16[4,16,64,128]{3,2,1,0:T(8,128)(2,1)} %direct.2), kind=kLoop, calls=%fused_computation.138 | loop fusion | bytes 524288 | tf_op jit(solution)/shard_map/stack;squeeze | solution.py:480
  1.8 0.7 collective-permute-start.1
  2.5 4.4 %collective-permute-start = (bf16[2,4,64,128]{3,2,1,0:T(8,128)(2,1)S(1)}, bf16[2,4,64,128]{3,2,1,0:T(8,128)(2,1)S(1)}, u32[]{:S(2)}, u32[]{:S(2)}) collective-permute-start(bf16[2,4,64,128]{3,2,1,0:T(8,128)(2,1)S(1)} %get-tuple-element.152), channel_id=1, source_target_pairs={{0,1},{1,0},{2,3},{3,2},{4,5},{5,4},{6,7},{7,6},{8,9},{9,8},{10,11... | collective-permute-start | bytes 393224 | tf_op jit(solution)/shard_map/ppermute | solution.py:339
  6.9 1.8 %pad_maximum_fusion.fields = bf16[2,4,16,64,128]{4,3,2,1,0:T(8,128)(2,1)S(1)} fusion(bf16[1,4,16,64,128]{4,3,2,1,0:T(8,128)(2,1)} %bitcast.148, bf16[1,4,16,64,128]{4,3,2,1,0:T(8,128)(2,1)} %bitcast.147), kind=kLoop, calls=%fused_computation | loop fusion | flops 1048576 | bytes 4194304 | tf_op jit(solution)/shard_map/stack | solution.py:485
  8.7 0.1 pad_maximum_fusion.1.weights
  8.8 0.2 blocks.1
  9.0 5.1 %drive.1 = (f32[4,512,256]{2,1,0:T(8,128)S(1)}, f32[4,512,256]{2,1,0:T(8,128)S(1)}, f32[512,256]{1,0:T(8,128)S(1)}, bf16[3,4,576,256]{3,2,1,0:T(8,128)(2,1)S(1)}...) custom-call(s32[2]{0:T(128)S(1)} %pad_add_fusion.9.place, ...), custom_call_target="tpu_custom_call" | custom-call | flops 3221225472 | bytes 12582912 | tf_op jit(solution)/shard_map/drive/pallas_call | solution.py:180
  14.2 0.1 select_multiply_fusion.13
  14.2 0.1 select_multiply_fusion.14
  14.3 0.1 fusion.3
  14.4 1.6 %collective-permute-start.4 = (f16[272,256]{1,0:T(8,128)(2,1)S(1)}, f16[272,256]{1,0:T(8,128)(2,1)S(1)}, u32[]{:S(2)}, u32[]{:S(2)}) collective-permute-start(f16[272,256]{1,0:T(8,128)(2,1)S(1)} %get-tuple-element.172), channel_id=1, source_target_pairs={{0,4},{1,5},{2,6},{3,7},{4,0},{5,1},{6,2},{7,3},{8,12},{9,13},{10,... | collective-permute-start | bytes 417800 | tf_op jit(solution)/shard_map/ppermute | solution.py:339
  15.9 1.6 %collective-permute-start.3 = (f16[272,256]{1,0:T(8,128)(2,1)S(1)}, f16[272,256]{1,0:T(8,128)(2,1)S(1)}, u32[]{:S(2)}, u32[]{:S(2)}) collective-permute-start(f16[272,256]{1,0:T(8,128)(2,1)S(1)} %get-tuple-element.173), channel_id=1, source_target_pairs={{0,8},{1,9},{2,10},{3,11},{4,12},{5,13},{6,14},{7,15},{8,0},{9,1},... | collective-permute-start | bytes 417800 | tf_op jit(solution)/shard_map/ppermute | solution.py:339
  17.5 0.4 collective-permute-start.2
  17.9 2.5 %collective-permute-done.4 = f16[272,256]{1,0:T(8,128)(2,1)S(1)} collective-permute-done((f16[272,256]{1,0:T(8,128)(2,1)S(1)}, f16[272,256]{1,0:T(8,128)(2,1)S(1)}, u32[]{:S(2)}, u32[]{:S(2)}) %collective-permute-start.4) | collective-permute-done | bytes 139296 | tf_op jit(solution)/shard_map/ppermute | solution.py:339
  20.5 2.0 %collective-permute-done.3 = f16[272,256]{1,0:T(8,128)(2,1)S(1)} collective-permute-done((f16[272,256]{1,0:T(8,128)(2,1)S(1)}, f16[272,256]{1,0:T(8,128)(2,1)S(1)}, u32[]{:S(2)}, u32[]{:S(2)}) %collective-permute-start.3) | collective-permute-done | bytes 139296 | tf_op jit(solution)/shard_map/ppermute | solution.py:339
  22.5 2.1 %collective-permute-done.2 = f16[272,256]{1,0:T(8,128)(2,1)S(1)} collective-permute-done((f16[272,256]{1,0:T(8,128)(2,1)S(1)}, f16[272,256]{1,0:T(8,128)(2,1)S(1)}, u32[]{:S(2)}, u32[]{:S(2)}) %collective-permute-start.2) | collective-permute-done | bytes 139296 | tf_op jit(solution)/shard_map/ppermute | solution.py:339
  24.7 0.3 select_multiply_fusion.12
  25.0 2.7 %collective-permute-start.5 = (f16[144,256]{1,0:T(8,128)(2,1)S(1)}, f16[144,256]{1,0:T(8,128)(2,1)S(1)}, u32[]{:S(2)}, u32[]{:S(2)}) collective-permute-start(f16[144,256]{1,0:T(8,128)(2,1)S(1)} %add_convert_fusion.3), channel_id=1, source_target_pairs={{0,16},{1,17},{2,18},{3,19},{4,20},{5,21},{6,22},{7,23},{8,24},{9,... | collective-permute-start | bytes 221192 | tf_op jit(solution)/shard_map/ppermute | solution.py:339
  27.7 2.8 %collective-permute-done.5 = f16[144,256]{1,0:T(8,128)(2,1)S(1)} collective-permute-done((f16[144,256]{1,0:T(8,128)(2,1)S(1)}, f16[144,256]{1,0:T(8,128)(2,1)S(1)}, u32[]{:S(2)}, u32[]{:S(2)}) %collective-permute-start.5) | collective-permute-done | bytes 73760 | tf_op jit(solution)/shard_map/ppermute | solution.py:339
  30.5 0.1 select_multiply_fusion.9
  30.7 0.1 select_multiply_fusion.8
  30.7 0.1 select_multiply_fusion.6
  30.9 0.1 fusion.6
  31.0 1.6 %collective-permute-start.8 = (f16[272,256]{1,0:T(8,128)(2,1)S(1)}, f16[272,256]{1,0:T(8,128)(2,1)S(1)}, u32[]{:S(2)}, u32[]{:S(2)}) collective-permute-start(f16[272,256]{1,0:T(8,128)(2,1)S(1)} %get-tuple-element.175), channel_id=1, source_target_pairs={{0,4},{1,5},{2,6},{3,7},{4,0},{5,1},{6,2},{7,3},{8,12},{9,13},{10,... | collective-permute-start | bytes 417800 | tf_op jit(solution)/shard_map/ppermute | solution.py:339
  32.5 1.4 %collective-permute-start.6 = (f16[272,256]{1,0:T(8,128)(2,1)S(1)}, f16[272,256]{1,0:T(8,128)(2,1)S(1)}, u32[]{:S(2)}, u32[]{:S(2)}) collective-permute-start(f16[272,256]{1,0:T(8,128)(2,1)S(1)} %get-tuple-element.176), channel_id=1, source_target_pairs={{0,12},{1,13},{2,14},{3,15},{4,8},{5,9},{6,10},{7,11},{8,4},{9,5},... | collective-permute-start | bytes 417800 | tf_op jit(solution)/shard_map/ppermute | solution.py:339
  33.9 0.6 collective-permute-start.7
  34.5 2.2 %collective-permute-done.8 = f16[272,256]{1,0:T(8,128)(2,1)S(1)} collective-permute-done((f16[272,256]{1,0:T(8,128)(2,1)S(1)}, f16[272,256]{1,0:T(8,128)(2,1)S(1)}, u32[]{:S(2)}, u32[]{:S(2)}) %collective-permute-start.8) | collective-permute-done | bytes 139296 | tf_op jit(solution)/shard_map/ppermute | solution.py:339
  36.8 1.7 %collective-permute-done.6 = f16[272,256]{1,0:T(8,128)(2,1)S(1)} collective-permute-done((f16[272,256]{1,0:T(8,128)(2,1)S(1)}, f16[272,256]{1,0:T(8,128)(2,1)S(1)}, u32[]{:S(2)}, u32[]{:S(2)}) %collective-permute-start.6) | collective-permute-done | bytes 139296 | tf_op jit(solution)/shard_map/ppermute | solution.py:339
  38.5 0.6 collective-permute-done.7
  39.1 0.1 broadcast_select_fusion.14
  39.2 0.1 broadcast_select_fusion.19
  39.3 0.1 broadcast_select_fusion.12
  39.4 4.3 %grads.1 = (bf16[4,512,256]{2,1,0:T(8,128)(2,1)S(1)}, bf16[4,512,256]{2,1,0:T(8,128)(2,1)S(1)}, bf16[2,4,64,128]{3,2,1,0:T(8,128)(2,1)S(1)}, bf16[2,4,64,128]{3,...) custom-call(s32[2]{0:T(128)S(1)} %pad_add_fusion.9.place, ...), custom_call_target="tpu_custom_call" | custom-call | flops 3221225472 | bytes 12582912 | tf_op jit(solution)/shard_map/grads/pallas_call | solution.py:285
  43.8 0.1 select_multiply_fusion.2
  43.9 0.1 collective-permute-start.9
  44.0 1.6 %collective-permute-done.9 = f16[1168,128]{1,0:T(8,128)(2,1)S(1)} collective-permute-done((f16[1168,128]{1,0:T(8,128)(2,1)S(1)}, f16[1168,128]{1,0:T(8,128)(2,1)S(1)}, u32[]{:S(2)}, u32[]{:S(2)}) %collective-permute-start.9) | collective-permute-done | bytes 299040 | tf_op jit(solution)/shard_map/ppermute | solution.py:339
  45.6 0.1 fusion
  45.7 0.0 copy-start
  45.7 0.0 copy-start.5
  45.8 0.1 select_multiply_fusion.3
  45.9 1.5 %collective-permute-start.10 = (f16[304,128]{1,0:T(8,128)(2,1)S(1)}, f16[304,128]{1,0:T(8,128)(2,1)S(1)}, u32[]{:S(2)}, u32[]{:S(2)}) collective-permute-start(f16[304,128]{1,0:T(8,128)(2,1)S(1)} %get-tuple-element.45), channel_id=1, source_target_pairs={{0,4},{1,5},{2,6},{3,7},{4,0},{5,1},{6,2},{7,3},{8,12},{9,13},{10,... | collective-permute-start | bytes 233480 | tf_op jit(solution)/shard_map/ppermute | solution.py:339
  47.4 0.2 collective-permute-start.11
  47.5 1.9 %collective-permute-start.12 = (f16[304,128]{1,0:T(8,128)(2,1)S(1)}, f16[304,128]{1,0:T(8,128)(2,1)S(1)}, u32[]{:S(2)}, u32[]{:S(2)}) collective-permute-start(f16[304,128]{1,0:T(8,128)(2,1)S(1)} %get-tuple-element.47), channel_id=1, source_target_pairs={{0,6},{1,7},{2,4},{3,5},{4,2},{5,3},{6,0},{7,1},{8,14},{9,15},{10,... | collective-permute-start | bytes 233480 | tf_op jit(solution)/shard_map/ppermute | solution.py:339
  49.4 0.8 %collective-permute-start.17 = (bf16[2,4,64,128]{3,2,1,0:T(8,128)(2,1)S(1)}, bf16[2,4,64,128]{3,2,1,0:T(8,128)(2,1)S(1)}, u32[]{:S(2)}, u32[]{:S(2)}) collective-permute-start(bf16[2,4,64,128]{3,2,1,0:T(8,128)(2,1)S(1)} %get-tuple-element.53), channel_id=1, source_target_pairs={{1,2},{2,1},{5,6},{6,5},{9,10},{10,9},{13,14},{14,13},{17,18},{18,... | collective-permute-start | bytes 393224 | tf_op jit(solution)/shard_map/ppermute | solution.py:347
  50.3 0.1 collective-permute-done.10
  50.3 3.0 %collective-permute-done.11 = f16[304,128]{1,0:T(8,128)(2,1)S(1)} collective-permute-done((f16[304,128]{1,0:T(8,128)(2,1)S(1)}, f16[304,128]{1,0:T(8,128)(2,1)S(1)}, u32[]{:S(2)}, u32[]{:S(2)}) %collective-permute-start.11) | collective-permute-done | bytes 77856 | tf_op jit(solution)/shard_map/ppermute | solution.py:339
  53.4 0.1 fusion.15
  53.5 4.1 %collective-permute-start.15 = (f16[304,128]{1,0:T(8,128)(2,1)S(1)}, f16[304,128]{1,0:T(8,128)(2,1)S(1)}, u32[]{:S(2)}, u32[]{:S(2)}) collective-permute-start(f16[304,128]{1,0:T(8,128)(2,1)S(1)} %add_convert_fusion.2), channel_id=1, source_target_pairs={{0,24},{1,25},{2,26},{3,27},{4,28},{5,29},{6,30},{7,31},{8,16},{9,... | collective-permute-start | bytes 233480 | tf_op jit(solution)/shard_map/ppermute | solution.py:339
  57.6 0.6 collective-permute-start.13
  58.3 0.0 copy-start.1
  58.3 3.6 %output.1 = bf16[4,16,64,128]{3,2,1,0:T(8,128)(2,1)} custom-call(s32[2]{0:T(128)S(1)} %pad_add_fusion.9.place, bf16[4,8,64,256]{3,2,1,0:T(8,128)(2,1)S(1)} %bitcast.155, bf16[2,4,64,128]{3,2,1,0:T(8,128)(2,1)S(1)} %collective-permute-done.16.first, bf16[2,4,64,128]{3,2,1,0:T(8,128)(2,1)S(1)} %collective-permute-done.17.second, ...), custom_call_target="tpu_custom_call" | custom-call | flops 1610612736 | bytes 4194304 | tf_op jit(solution)/shard_map/output/pallas_call | solution.py:318
  61.9 1.7 %collective-permute-done.14 = f16[304,128]{1,0:T(8,128)(2,1)S(1)} collective-permute-done((f16[304,128]{1,0:T(8,128)(2,1)S(1)}, f16[304,128]{1,0:T(8,128)(2,1)S(1)}, u32[]{:S(2)}, u32[]{:S(2)}) %collective-permute-start.14) | collective-permute-done | bytes 77856 | tf_op jit(solution)/shard_map/ppermute | solution.py:339
  63.7 0.1 fusion.12
  63.8 1.0 %collective-permute-start.20 = (f16[304,128]{1,0:T(8,128)(2,1)S(1)}, f16[304,128]{1,0:T(8,128)(2,1)S(1)}, u32[]{:S(2)}, u32[]{:S(2)}) collective-permute-start(f16[304,128]{1,0:T(8,128)(2,1)S(1)} %add_convert_fusion.1), channel_id=1, source_target_pairs={{0,4},{1,5},{2,6},{3,7},{4,0},{5,1},{6,2},{7,3},{8,12},{9,13},{10,... | collective-permute-start | bytes 233480 | tf_op jit(solution)/shard_map/ppermute | solution.py:339
  64.8 0.6 collective-permute-start.19
  65.4 1.9 %collective-permute-start.18 = (f16[304,128]{1,0:T(8,128)(2,1)S(1)}, f16[304,128]{1,0:T(8,128)(2,1)S(1)}, u32[]{:S(2)}, u32[]{:S(2)}) collective-permute-start(f16[304,128]{1,0:T(8,128)(2,1)S(1)} %add_convert_fusion.1), channel_id=1, source_target_pairs={{0,6},{1,7},{2,4},{3,5},{4,2},{5,3},{6,0},{7,1},{8,14},{9,15},{10,... | collective-permute-start | bytes 233480 | tf_op jit(solution)/shard_map/ppermute | solution.py:339
  67.3 3.6 %grad_frames.1 = bf16[4,16,64,128]{3,2,1,0:T(8,128)(2,1)} custom-call(s32[2]{0:T(128)S(1)} %pad_add_fusion.9.place, bf16[4,8,64,256]{3,2,1,0:T(8,128)(2,1)S(1)} %bitcast.154, bf16[2,4,64,128]{3,2,1,0:T(8,128)(2,1)S(1)} %collective-permute-done.16.first, bf16[2,4,64,128]{3,2,1,0:T(8,128)(2,1)S(1)} %collective-permute-done.17.second, ...), custom_call_target="tpu_custom_call" | custom-call | flops 1610612736 | bytes 4194304 | tf_op jit(solution)/shard_map/grad_frames/pallas_call | solution.py:318
  70.9 0.1 broadcast_select_fusion.7
  71.0 0.1 broadcast_select_fusion.1
  71.1 0.1 pad_maximum_fusion.4
  71.2 0.1 collective-permute-start.21
  71.4 1.5 %collective-permute-done.21 = f16[1216,128]{1,0:T(8,128)(2,1)S(1)} collective-permute-done((f16[1216,128]{1,0:T(8,128)(2,1)S(1)}, f16[1216,128]{1,0:T(8,128)(2,1)S(1)}, u32[]{:S(2)}, u32[]{:S(2)}) %collective-permute-start.21) | collective-permute-done | bytes 311328 | tf_op jit(solution)/shard_map/ppermute | solution.py:339
  73.0 1.1 %select_multiply_fusion = (f32[4,288,128]{2,1,0:T(8,128)}, f32[4,288,128]{2,1,0:T(8,128)}) fusion(f32[4,304,128]{2,1,0:T(8,128)S(1)} %convert.2, f32[4,304,128]{2,1,0:T(8,128)S(1)} %convert.3, f32[4,128]{1,0:T(4,128)S(1)} %bitcast.190, f32[4,128]{1,0:T(4,128)S(1)} %bitcast.191, pred[128]{0:T(512)(128)(4,1)S(1)} %get-tuple-element.170), kind=kLoop, calls=%fused_computation.7 | loop fusion | flops 884736 | bytes 2363520 | tf_op jit(solution)/shard_map/mul | solution.py:576
  (67 shorter events, 0.9 us)
Async XLA Ops:
  1.8 7.2 %collective-permute-start.1 = (bf16[2,4,64,128]{3,2,1,0:T(8,128)(2,1)S(1)}, bf16[2,4,64,128]{3,2,1,0:T(8,128)(2,1)S(1)}, u32[]{:S(2)}, u32[]{:S(2)}) collective-permute-start(bf16[2,4,64,128]{3,2,1,0:T(8,128)(2,1)S(1)} %get-tuple-element.151), channel_id=1, source_target_pairs={{1,2},{2,1},{5,6},{6,5},{9,10},{10,9},{13,14},{14,13},{17,18},{18,... | collective-permute-start | bytes 393224 | tf_op jit(solution)/shard_map/ppermute | solution.py:347
  2.5 6.5 %collective-permute-start = (bf16[2,4,64,128]{3,2,1,0:T(8,128)(2,1)S(1)}, bf16[2,4,64,128]{3,2,1,0:T(8,128)(2,1)S(1)}, u32[]{:S(2)}, u32[]{:S(2)}) collective-permute-start(bf16[2,4,64,128]{3,2,1,0:T(8,128)(2,1)S(1)} %get-tuple-element.152), channel_id=1, source_target_pairs={{0,1},{1,0},{2,3},{3,2},{4,5},{5,4},{6,7},{7,6},{8,9},{9,8},{10,11... | collective-permute-start | bytes 393224 | tf_op jit(solution)/shard_map/ppermute | solution.py:339
  6.9 1.8 %copy-start.2 = (bf16[3,3,128,128]{3,2,1,0:T(8,128)(2,1)S(1)}, bf16[3,3,128,128]{3,2,1,0:T(8,128)(2,1)}, u32[]{:S(2)}) copy-start(bf16[3,3,128,128]{3,2,1,0:T(8,128)(2,1)} %weight.2) | copy-start | bytes 884740
  6.9 1.8 %copy-start.3 = (bf16[3,3,128,128]{3,2,1,0:T(8,128)(2,1)S(1)}, bf16[3,3,128,128]{3,2,1,0:T(8,128)(2,1)}, u32[]{:S(2)}) copy-start(bf16[3,3,128,128]{3,2,1,0:T(8,128)(2,1)} %weight.3) | copy-start | bytes 884740
  6.9 1.9 %copy-start.4 = (f32[4,128]{1,0:T(4,128)S(1)}, f32[4,128]{1,0:T(4,128)}, u32[]{:S(2)}) copy-start(f32[4,128]{1,0:T(4,128)} %log_decay.5) | copy-start | bytes 6148
  14.4 6.1 %collective-permute-start.4 = (f16[272,256]{1,0:T(8,128)(2,1)S(1)}, f16[272,256]{1,0:T(8,128)(2,1)S(1)}, u32[]{:S(2)}, u32[]{:S(2)}) collective-permute-start(f16[272,256]{1,0:T(8,128)(2,1)S(1)} %get-tuple-element.172), channel_id=1, source_target_pairs={{0,4},{1,5},{2,6},{3,7},{4,0},{5,1},{6,2},{7,3},{8,12},{9,13},{10,... | collective-permute-start | bytes 417800 | tf_op jit(solution)/shard_map/ppermute | solution.py:339
  15.9 6.5 %collective-permute-start.3 = (f16[272,256]{1,0:T(8,128)(2,1)S(1)}, f16[272,256]{1,0:T(8,128)(2,1)S(1)}, u32[]{:S(2)}, u32[]{:S(2)}) collective-permute-start(f16[272,256]{1,0:T(8,128)(2,1)S(1)} %get-tuple-element.173), channel_id=1, source_target_pairs={{0,8},{1,9},{2,10},{3,11},{4,12},{5,13},{6,14},{7,15},{8,0},{9,1},... | collective-permute-start | bytes 417800 | tf_op jit(solution)/shard_map/ppermute | solution.py:339
  17.5 7.1 %collective-permute-start.2 = (f16[272,256]{1,0:T(8,128)(2,1)S(1)}, f16[272,256]{1,0:T(8,128)(2,1)S(1)}, u32[]{:S(2)}, u32[]{:S(2)}) collective-permute-start(f16[272,256]{1,0:T(8,128)(2,1)S(1)} %get-tuple-element.174), channel_id=1, source_target_pairs={{0,12},{1,13},{2,14},{3,15},{4,8},{5,9},{6,10},{7,11},{8,4},{9,5},... | collective-permute-start | bytes 417800 | tf_op jit(solution)/shard_map/ppermute | solution.py:339
  25.0 5.5 %collective-permute-start.5 = (f16[144,256]{1,0:T(8,128)(2,1)S(1)}, f16[144,256]{1,0:T(8,128)(2,1)S(1)}, u32[]{:S(2)}, u32[]{:S(2)}) collective-permute-start(f16[144,256]{1,0:T(8,128)(2,1)S(1)} %add_convert_fusion.3), channel_id=1, source_target_pairs={{0,16},{1,17},{2,18},{3,19},{4,20},{5,21},{6,22},{7,23},{8,24},{9,... | collective-permute-start | bytes 221192 | tf_op jit(solution)/shard_map/ppermute | solution.py:339
  31.0 5.8 %collective-permute-start.8 = (f16[272,256]{1,0:T(8,128)(2,1)S(1)}, f16[272,256]{1,0:T(8,128)(2,1)S(1)}, u32[]{:S(2)}, u32[]{:S(2)}) collective-permute-start(f16[272,256]{1,0:T(8,128)(2,1)S(1)} %get-tuple-element.175), channel_id=1, source_target_pairs={{0,4},{1,5},{2,6},{3,7},{4,0},{5,1},{6,2},{7,3},{8,12},{9,13},{10,... | collective-permute-start | bytes 417800 | tf_op jit(solution)/shard_map/ppermute | solution.py:339
  32.5 6.0 %collective-permute-start.6 = (f16[272,256]{1,0:T(8,128)(2,1)S(1)}, f16[272,256]{1,0:T(8,128)(2,1)S(1)}, u32[]{:S(2)}, u32[]{:S(2)}) collective-permute-start(f16[272,256]{1,0:T(8,128)(2,1)S(1)} %get-tuple-element.176), channel_id=1, source_target_pairs={{0,12},{1,13},{2,14},{3,15},{4,8},{5,9},{6,10},{7,11},{8,4},{9,5},... | collective-permute-start | bytes 417800 | tf_op jit(solution)/shard_map/ppermute | solution.py:339
  33.9 5.2 %collective-permute-start.7 = (f16[272,256]{1,0:T(8,128)(2,1)S(1)}, f16[272,256]{1,0:T(8,128)(2,1)S(1)}, u32[]{:S(2)}, u32[]{:S(2)}) collective-permute-start(f16[272,256]{1,0:T(8,128)(2,1)S(1)} %get-tuple-element.177), channel_id=1, source_target_pairs={{0,8},{1,9},{2,10},{3,11},{4,12},{5,13},{6,14},{7,15},{8,0},{9,1},... | collective-permute-start | bytes 417800 | tf_op jit(solution)/shard_map/ppermute | solution.py:339
  43.9 1.7 %collective-permute-start.9 = (f16[1168,128]{1,0:T(8,128)(2,1)S(1)}, f16[1168,128]{1,0:T(8,128)(2,1)S(1)}, u32[]{:S(2)}, u32[]{:S(2)}) collective-permute-start(f16[1168,128]{1,0:T(8,128)(2,1)S(1)} %add_convert_fusion), channel_id=1, source_target_pairs={{0,1},{1,0},{2,3},{3,2},{4,5},{5,4},{6,7},{7,6},{8,9},{9,8},{10,11... | collective-permute-start | bytes 897032 | tf_op jit(solution)/shard_map/ppermute | solution.py:339
  45.7 12.5 %copy-start = (bf16[4,16,64,128]{3,2,1,0:T(8,128)(2,1)S(1)}, bf16[4,16,64,128]{3,2,1,0:T(8,128)(2,1)}, u32[]{:S(2)}) copy-start(bf16[4,16,64,128]{3,2,1,0:T(8,128)(2,1)} %direct.2) | copy-start | bytes 3145732
  45.7 12.5 %copy-start.5 = (f32[128]{0:T(128)S(1)}, f32[128]{0:T(128)}, u32[]{:S(2)}) copy-start(f32[128]{0:T(128)} %param.10) | copy-start | bytes 1540
  45.9 4.5 %collective-permute-start.10 = (f16[304,128]{1,0:T(8,128)(2,1)S(1)}, f16[304,128]{1,0:T(8,128)(2,1)S(1)}, u32[]{:S(2)}, u32[]{:S(2)}) collective-permute-start(f16[304,128]{1,0:T(8,128)(2,1)S(1)} %get-tuple-element.45), channel_id=1, source_target_pairs={{0,4},{1,5},{2,6},{3,7},{4,0},{5,1},{6,2},{7,3},{8,12},{9,13},{10,... | collective-permute-start | bytes 233480 | tf_op jit(solution)/shard_map/ppermute | solution.py:339
  47.4 6.0 %collective-permute-start.11 = (f16[304,128]{1,0:T(8,128)(2,1)S(1)}, f16[304,128]{1,0:T(8,128)(2,1)S(1)}, u32[]{:S(2)}, u32[]{:S(2)}) collective-permute-start(f16[304,128]{1,0:T(8,128)(2,1)S(1)} %get-tuple-element.46), channel_id=1, source_target_pairs={{0,2},{1,3},{2,0},{3,1},{4,6},{5,7},{6,4},{7,5},{8,10},{9,11},{10,... | collective-permute-start | bytes 233480 | tf_op jit(solution)/shard_map/ppermute | solution.py:339
  47.5 5.8 %collective-permute-start.12 = (f16[304,128]{1,0:T(8,128)(2,1)S(1)}, f16[304,128]{1,0:T(8,128)(2,1)S(1)}, u32[]{:S(2)}, u32[]{:S(2)}) collective-permute-start(f16[304,128]{1,0:T(8,128)(2,1)S(1)} %get-tuple-element.47), channel_id=1, source_target_pairs={{0,6},{1,7},{2,4},{3,5},{4,2},{5,3},{6,0},{7,1},{8,14},{9,15},{10,... | collective-permute-start | bytes 233480 | tf_op jit(solution)/shard_map/ppermute | solution.py:339
  49.4 8.8 %collective-permute-start.16 = (bf16[2,4,64,128]{3,2,1,0:T(8,128)(2,1)S(1)}, bf16[2,4,64,128]{3,2,1,0:T(8,128)(2,1)S(1)}, u32[]{:S(2)}, u32[]{:S(2)}) collective-permute-start(bf16[2,4,64,128]{3,2,1,0:T(8,128)(2,1)S(1)} %get-tuple-element.52), channel_id=1, source_target_pairs={{0,1},{1,0},{2,3},{3,2},{4,5},{5,4},{6,7},{7,6},{8,9},{9,8},{10,11... | collective-permute-start | bytes 393224 | tf_op jit(solution)/shard_map/ppermute | solution.py:339
  49.4 8.8 %collective-permute-start.17 = (bf16[2,4,64,128]{3,2,1,0:T(8,128)(2,1)S(1)}, bf16[2,4,64,128]{3,2,1,0:T(8,128)(2,1)S(1)}, u32[]{:S(2)}, u32[]{:S(2)}) collective-permute-start(bf16[2,4,64,128]{3,2,1,0:T(8,128)(2,1)S(1)} %get-tuple-element.53), channel_id=1, source_target_pairs={{1,2},{2,1},{5,6},{6,5},{9,10},{10,9},{13,14},{14,13},{17,18},{18,... | collective-permute-start | bytes 393224 | tf_op jit(solution)/shard_map/ppermute | solution.py:347
  53.5 8.4 %collective-permute-start.15 = (f16[304,128]{1,0:T(8,128)(2,1)S(1)}, f16[304,128]{1,0:T(8,128)(2,1)S(1)}, u32[]{:S(2)}, u32[]{:S(2)}) collective-permute-start(f16[304,128]{1,0:T(8,128)(2,1)S(1)} %add_convert_fusion.2), channel_id=1, source_target_pairs={{0,24},{1,25},{2,26},{3,27},{4,28},{5,29},{6,30},{7,31},{8,16},{9,... | collective-permute-start | bytes 233480 | tf_op jit(solution)/shard_map/ppermute | solution.py:339
  57.6 6.0 %collective-permute-start.14 = (f16[304,128]{1,0:T(8,128)(2,1)S(1)}, f16[304,128]{1,0:T(8,128)(2,1)S(1)}, u32[]{:S(2)}, u32[]{:S(2)}) collective-permute-start(f16[304,128]{1,0:T(8,128)(2,1)S(1)} %add_convert_fusion.2), channel_id=1, source_target_pairs={{0,16},{1,17},{2,18},{3,19},{4,20},{5,21},{6,22},{7,23},{8,24},{9,... | collective-permute-start | bytes 233480 | tf_op jit(solution)/shard_map/ppermute | solution.py:339
  57.6 6.1 %collective-permute-start.13 = (f16[304,128]{1,0:T(8,128)(2,1)S(1)}, f16[304,128]{1,0:T(8,128)(2,1)S(1)}, u32[]{:S(2)}, u32[]{:S(2)}) collective-permute-start(f16[304,128]{1,0:T(8,128)(2,1)S(1)} %add_convert_fusion.2), channel_id=1, source_target_pairs={{0,8},{1,9},{2,10},{3,11},{4,12},{5,13},{6,14},{7,15},{8,0},{9,1},... | collective-permute-start | bytes 233480 | tf_op jit(solution)/shard_map/ppermute | solution.py:339
  58.3 9.0 %copy-start.1 = (bf16[4,16,64,128]{3,2,1,0:T(8,128)(2,1)S(1)}, bf16[4,16,64,128]{3,2,1,0:T(8,128)(2,1)}, u32[]{:S(2)}) copy-start(bf16[4,16,64,128]{3,2,1,0:T(8,128)(2,1)} %direct.3) | copy-start | bytes 3145732
  63.8 7.2 %collective-permute-start.20 = (f16[304,128]{1,0:T(8,128)(2,1)S(1)}, f16[304,128]{1,0:T(8,128)(2,1)S(1)}, u32[]{:S(2)}, u32[]{:S(2)}) collective-permute-start(f16[304,128]{1,0:T(8,128)(2,1)S(1)} %add_convert_fusion.1), channel_id=1, source_target_pairs={{0,4},{1,5},{2,6},{3,7},{4,0},{5,1},{6,2},{7,3},{8,12},{9,13},{10,... | collective-permute-start | bytes 233480 | tf_op jit(solution)/shard_map/ppermute | solution.py:339
  64.8 6.2 %collective-permute-start.19 = (f16[304,128]{1,0:T(8,128)(2,1)S(1)}, f16[304,128]{1,0:T(8,128)(2,1)S(1)}, u32[]{:S(2)}, u32[]{:S(2)}) collective-permute-start(f16[304,128]{1,0:T(8,128)(2,1)S(1)} %add_convert_fusion.1), channel_id=1, source_target_pairs={{0,2},{1,3},{2,0},{3,1},{4,6},{5,7},{6,4},{7,5},{8,10},{9,11},{10,... | collective-permute-start | bytes 233480 | tf_op jit(solution)/shard_map/ppermute | solution.py:339
  65.4 5.5 %collective-permute-start.18 = (f16[304,128]{1,0:T(8,128)(2,1)S(1)}, f16[304,128]{1,0:T(8,128)(2,1)S(1)}, u32[]{:S(2)}, u32[]{:S(2)}) collective-permute-start(f16[304,128]{1,0:T(8,128)(2,1)S(1)} %add_convert_fusion.1), channel_id=1, source_target_pairs={{0,6},{1,7},{2,4},{3,5},{4,2},{5,3},{6,0},{7,1},{8,14},{9,15},{10,... | collective-permute-start | bytes 233480 | tf_op jit(solution)/shard_map/ppermute | solution.py:339
  71.2 1.7 %collective-permute-start.21 = (f16[1216,128]{1,0:T(8,128)(2,1)S(1)}, f16[1216,128]{1,0:T(8,128)(2,1)S(1)}, u32[]{:S(2)}, u32[]{:S(2)}) collective-permute-start(f16[1216,128]{1,0:T(8,128)(2,1)S(1)} %pad_maximum_fusion.4), channel_id=1, source_target_pairs={{0,1},{1,0},{2,3},{3,2},{4,5},{5,4},{6,7},{7,6},{8,9},{9,8},{10,11... | collective-permute-start | bytes 933896 | tf_op jit(solution)/shard_map/ppermute | solution.py:339

commit v7 on v6

--- a/solution.py
+++ b/solution.py
@@ -60,17 +60,19 @@
 
 def conv_pairs(taps, blocks, rows_out, cols, flip):
     dims = (((1,), (1,)), ((), ())) if flip else (((1,), (0,)), ((), ()))
-    total = None
-    for j in range(3):
-        for b in range(2):
-            part = lax.dot_general(
-                taps[j][b * cols : b * cols + rows_out],
-                blocks[j, b],
-                dims,
-                preferred_element_type=F32,
-            )
-            total = part if total is None else total + part
-    return total
+    step = rows_out if flip else math.gcd(rows_out, 128)
+    results = []
+    for row in range(0, rows_out, step):
+        total = None
+        for j in range(3):
+            for b in range(2):
+                start = b * cols + row
+                part = lax.dot_general(
+                    taps[j][start : start + step], blocks[j, b], dims, preferred_element_type=F32
+                )
+                total = part if total is None else total + part
+        results.append(total)
+    return jnp.concatenate(results, 0)
 
 
 def pick_halos(first, second, index, odd, times):
@@ -296,20 +298,27 @@
     )(place, states, adjoints, state_in, adjoint_in, log_decay, frame_taps, cot_taps)
 
 
-def output_kernel(place, field, first, second, weight, skip, direct, out, pairs, blocks, *, flip):
+def output_kernel(
+    place, field, first, second, weight, skip, direct, out, pairs, blocks, near, sems, *, flip
+):
     times, half, cols, width = field.shape
     ch = width // 2
     fill_weights(blocks, weight, flip)
     top, bottom = pick_halos(first, second, int(flip), lax.rem(place[0], 2) == 1, times)
     fill_pairs_from_pairs(pairs, field, top, bottom)
     gain = skip[...]
+    stores = []
     for t in range(times):
         taps = column_taps(pairs[t].reshape((half + 1) * cols, width), cols)
         value = conv_pairs(taps, blocks, half * cols, cols, flip).reshape(half, cols, width)
         for i in range(half):
             for c in range(2):
                 base = gain * direct[t, 2 * i + c].astype(F32)
-                out[t, 2 * i + c] = (value[i, :, c * ch : (c + 1) * ch] + base).astype(BF16)
+                near[t, 2 * i + c] = (value[i, :, c * ch : (c + 1) * ch] + base).astype(BF16)
+        stores.append(pltpu.make_async_copy(near.at[t], out.at[t], sems.at[t]))
+        stores[-1].start()
+    for copy in stores:
+        copy.wait()
 
 
 def output_call(place, field, first, second, weight, skip, direct, flip):
@@ -319,10 +328,13 @@
         functools.partial(output_kernel, flip=flip),
         in_specs=[pl.BlockSpec(memory_space=pltpu.SMEM)]
         + [pl.BlockSpec(memory_space=pltpu.VMEM)] * 6,
+        out_specs=pl.BlockSpec(memory_space=pltpu.HBM),
         out_shape=jax.ShapeDtypeStruct(direct.shape, BF16),
         scratch_shapes=[
             pltpu.VMEM((times, half + 1, cols, width), BF16),
             pltpu.VMEM((3, 2, width, width), BF16),
+            pltpu.VMEM(direct.shape, BF16),
+            pltpu.SemaphoreType.DMA((times,)),
         ],
         compiler_params=pltpu.CompilerParams(vmem_limit_bytes=VMEM_LIMIT),
         cost_estimate=pl.CostEstimate(

time: 74.3 us -> 74.3 us (level)
  transfers between devices with their start and end apart: 22 -> 22, of which waited for: 12 -> 12; matrix products, arithmetic and copies ran while one was open for 3% -> 3% of each run, Pallas kernels for 10% -> 9%
where the time goes in v7:
time: 74.3 us; the launch traced here: 74 us
  starting transfers between devices  27.6 us (37%)
  waiting for transfers between devices  22.2 us (30%)
  Pallas kernels  16.3 us (22%)
  other arithmetic  5.53 us (7%)
  between operations  1.37 us (2%)
  local copies, waits for them, and re-layouts  1 us (1%)
    ppermute x20, starting transfers between devices, swap(): lax.ppermute(value, ('tm', 'tile'), [(i, i ^ mask) for i in range(count)])  26.1 us
    ppermute x20, waiting for transfers between devices, swap(): lax.ppermute(value, ('tm', 'tile'), [(i, i ^ mask) for i in range(count)])  22.2 us
    pallas_call x2, Pallas kernels, output_call(): pl.pallas_call(functools.partial(output_kernel, flip=flip), in_specs=[pl....  6.72 us
    pallas_call x1, Pallas kernels, drive_call(): pl.pallas_call(drive_kernel, in_specs=[pl.BlockSpec(memory_space=pltpu.SM...  5.07 us
    pallas_call x1, Pallas kernels, grads_call(): pl.pallas_call(grads_kernel, in_specs=[pl.BlockSpec(memory_space=pltpu.SM...  4.33 us
    another operation x1, other arithmetic, shards(): fields = jnp.stack([frames, cotangent])  1.79 us
    ppermute x2, starting transfers between devices, swap_across(): return lax.ppermute(value, 'tile', pairs)  1.51 us
  transfers between devices with their start and end apart: 22, of which 12 were waited for; matrix products, arithmetic and copies ran while one was open for 3% of the time, Pallas kernels for 9%

profile of v7, /device:TPU:0, one launch (start us, length us, event | category | flops | bytes accessed | tf_op | source)
XLA Modules:
  0.0 74.0 jit_solution(17953224393247356070)
XLA Ops:
  0.6 0.1 pad_add_fusion.9.place
  0.8 1.0 %slice_bitcast_fusion.2 = (bf16[1,4,64,128]{3,2,1,0:T(8,128)(2,1)S(1)}, bf16[1,4,64,128]{3,2,1,0:T(8,128)(2,1)S(1)}, bf16[1,4,64,128]{3,2,1,0:T(8,128)(2,1)S(1)}, bf16[1,4,64,128]{3,2,1,0:T(8,128)(2,1)S(1)}) fusion(bf16[4,16,64,128]{3,2,1,0:T(8,128)(2,1)} %direct.3, bf16[4,16,64,128]{3,2,1,0:T(8,128)(2,1)} %direct.2), kind=kLoop, calls=%fused_computation.138 | loop fusion | bytes 524288 | tf_op jit(solution)/shard_map/stack;squeeze | solution.py:492
  1.8 0.7 collective-permute-start.1
  2.5 4.4 %collective-permute-start = (bf16[2,4,64,128]{3,2,1,0:T(8,128)(2,1)S(1)}, bf16[2,4,64,128]{3,2,1,0:T(8,128)(2,1)S(1)}, u32[]{:S(2)}, u32[]{:S(2)}) collective-permute-start(bf16[2,4,64,128]{3,2,1,0:T(8,128)(2,1)S(1)} %get-tuple-element.152), channel_id=1, source_target_pairs={{0,1},{1,0},{2,3},{3,2},{4,5},{5,4},{6,7},{7,6},{8,9},{9,8},{10,11... | collective-permute-start | bytes 393224 | tf_op jit(solution)/shard_map/ppermute | solution.py:351
  6.9 1.8 %pad_maximum_fusion.fields = bf16[2,4,16,64,128]{4,3,2,1,0:T(8,128)(2,1)S(1)} fusion(bf16[1,4,16,64,128]{4,3,2,1,0:T(8,128)(2,1)} %bitcast.148, bf16[1,4,16,64,128]{4,3,2,1,0:T(8,128)(2,1)} %bitcast.147), kind=kLoop, calls=%fused_computation | loop fusion | flops 1048576 | bytes 4194304 | tf_op jit(solution)/shard_map/stack | solution.py:497
  8.7 0.1 pad_maximum_fusion.1.weights
  8.8 0.2 blocks.1
  9.0 5.1 %drive.1 = (f32[4,512,256]{2,1,0:T(8,128)S(1)}, f32[4,512,256]{2,1,0:T(8,128)S(1)}, f32[512,256]{1,0:T(8,128)S(1)}, bf16[3,4,576,256]{3,2,1,0:T(8,128)(2,1)S(1)}...) custom-call(s32[2]{0:T(128)S(1)} %pad_add_fusion.9.place, ...), custom_call_target="tpu_custom_call" | custom-call | flops 3221225472 | bytes 12582912 | tf_op jit(solution)/shard_map/drive/pallas_call | solution.py:182
  14.2 0.1 select_multiply_fusion.13
  14.2 0.1 select_multiply_fusion.14
  14.3 0.1 fusion.3
  14.4 1.6 %collective-permute-start.4 = (f16[272,256]{1,0:T(8,128)(2,1)S(1)}, f16[272,256]{1,0:T(8,128)(2,1)S(1)}, u32[]{:S(2)}, u32[]{:S(2)}) collective-permute-start(f16[272,256]{1,0:T(8,128)(2,1)S(1)} %get-tuple-element.172), channel_id=1, source_target_pairs={{0,4},{1,5},{2,6},{3,7},{4,0},{5,1},{6,2},{7,3},{8,12},{9,13},{10,... | collective-permute-start | bytes 417800 | tf_op jit(solution)/shard_map/ppermute | solution.py:351
  15.9 1.6 %collective-permute-start.3 = (f16[272,256]{1,0:T(8,128)(2,1)S(1)}, f16[272,256]{1,0:T(8,128)(2,1)S(1)}, u32[]{:S(2)}, u32[]{:S(2)}) collective-permute-start(f16[272,256]{1,0:T(8,128)(2,1)S(1)} %get-tuple-element.173), channel_id=1, source_target_pairs={{0,8},{1,9},{2,10},{3,11},{4,12},{5,13},{6,14},{7,15},{8,0},{9,1},... | collective-permute-start | bytes 417800 | tf_op jit(solution)/shard_map/ppermute | solution.py:351
  17.5 0.4 collective-permute-start.2
  17.9 2.5 %collective-permute-done.4 = f16[272,256]{1,0:T(8,128)(2,1)S(1)} collective-permute-done((f16[272,256]{1,0:T(8,128)(2,1)S(1)}, f16[272,256]{1,0:T(8,128)(2,1)S(1)}, u32[]{:S(2)}, u32[]{:S(2)}) %collective-permute-start.4) | collective-permute-done | bytes 139296 | tf_op jit(solution)/shard_map/ppermute | solution.py:351
  20.5 2.0 %collective-permute-done.3 = f16[272,256]{1,0:T(8,128)(2,1)S(1)} collective-permute-done((f16[272,256]{1,0:T(8,128)(2,1)S(1)}, f16[272,256]{1,0:T(8,128)(2,1)S(1)}, u32[]{:S(2)}, u32[]{:S(2)}) %collective-permute-start.3) | collective-permute-done | bytes 139296 | tf_op jit(solution)/shard_map/ppermute | solution.py:351
  22.5 2.1 %collective-permute-done.2 = f16[272,256]{1,0:T(8,128)(2,1)S(1)} collective-permute-done((f16[272,256]{1,0:T(8,128)(2,1)S(1)}, f16[272,256]{1,0:T(8,128)(2,1)S(1)}, u32[]{:S(2)}, u32[]{:S(2)}) %collective-permute-start.2) | collective-permute-done | bytes 139296 | tf_op jit(solution)/shard_map/ppermute | solution.py:351
  24.8 0.3 select_multiply_fusion.12
  25.0 2.7 %collective-permute-start.5 = (f16[144,256]{1,0:T(8,128)(2,1)S(1)}, f16[144,256]{1,0:T(8,128)(2,1)S(1)}, u32[]{:S(2)}, u32[]{:S(2)}) collective-permute-start(f16[144,256]{1,0:T(8,128)(2,1)S(1)} %add_convert_fusion.3), channel_id=1, source_target_pairs={{0,16},{1,17},{2,18},{3,19},{4,20},{5,21},{6,22},{7,23},{8,24},{9,... | collective-permute-start | bytes 221192 | tf_op jit(solution)/shard_map/ppermute | solution.py:351
  27.7 2.8 %collective-permute-done.5 = f16[144,256]{1,0:T(8,128)(2,1)S(1)} collective-permute-done((f16[144,256]{1,0:T(8,128)(2,1)S(1)}, f16[144,256]{1,0:T(8,128)(2,1)S(1)}, u32[]{:S(2)}, u32[]{:S(2)}) %collective-permute-start.5) | collective-permute-done | bytes 73760 | tf_op jit(solution)/shard_map/ppermute | solution.py:351
  30.6 0.1 select_multiply_fusion.9
  30.7 0.1 select_multiply_fusion.8
  30.8 0.1 select_multiply_fusion.6
  30.9 0.1 fusion.6
  31.0 1.6 %collective-permute-start.8 = (f16[272,256]{1,0:T(8,128)(2,1)S(1)}, f16[272,256]{1,0:T(8,128)(2,1)S(1)}, u32[]{:S(2)}, u32[]{:S(2)}) collective-permute-start(f16[272,256]{1,0:T(8,128)(2,1)S(1)} %get-tuple-element.175), channel_id=1, source_target_pairs={{0,4},{1,5},{2,6},{3,7},{4,0},{5,1},{6,2},{7,3},{8,12},{9,13},{10,... | collective-permute-start | bytes 417800 | tf_op jit(solution)/shard_map/ppermute | solution.py:351
  32.5 1.4 %collective-permute-start.6 = (f16[272,256]{1,0:T(8,128)(2,1)S(1)}, f16[272,256]{1,0:T(8,128)(2,1)S(1)}, u32[]{:S(2)}, u32[]{:S(2)}) collective-permute-start(f16[272,256]{1,0:T(8,128)(2,1)S(1)} %get-tuple-element.176), channel_id=1, source_target_pairs={{0,12},{1,13},{2,14},{3,15},{4,8},{5,9},{6,10},{7,11},{8,4},{9,5},... | collective-permute-start | bytes 417800 | tf_op jit(solution)/shard_map/ppermute | solution.py:351
  33.9 0.6 collective-permute-start.7
  34.5 2.2 %collective-permute-done.8 = f16[272,256]{1,0:T(8,128)(2,1)S(1)} collective-permute-done((f16[272,256]{1,0:T(8,128)(2,1)S(1)}, f16[272,256]{1,0:T(8,128)(2,1)S(1)}, u32[]{:S(2)}, u32[]{:S(2)}) %collective-permute-start.8) | collective-permute-done | bytes 139296 | tf_op jit(solution)/shard_map/ppermute | solution.py:351
  36.8 1.7 %collective-permute-done.6 = f16[272,256]{1,0:T(8,128)(2,1)S(1)} collective-permute-done((f16[272,256]{1,0:T(8,128)(2,1)S(1)}, f16[272,256]{1,0:T(8,128)(2,1)S(1)}, u32[]{:S(2)}, u32[]{:S(2)}) %collective-permute-start.6) | collective-permute-done | bytes 139296 | tf_op jit(solution)/shard_map/ppermute | solution.py:351
  38.5 0.6 collective-permute-done.7
  39.1 0.1 broadcast_select_fusion.14
  39.2 0.1 broadcast_select_fusion.19
  39.3 0.1 broadcast_select_fusion.12
  39.4 4.3 %grads.1 = (bf16[4,512,256]{2,1,0:T(8,128)(2,1)S(1)}, bf16[4,512,256]{2,1,0:T(8,128)(2,1)S(1)}, bf16[2,4,64,128]{3,2,1,0:T(8,128)(2,1)S(1)}, bf16[2,4,64,128]{3,...) custom-call(s32[2]{0:T(128)S(1)} %pad_add_fusion.9.place, ...), custom_call_target="tpu_custom_call" | custom-call | flops 3221225472 | bytes 12582912 | tf_op jit(solution)/shard_map/grads/pallas_call | solution.py:287
  43.8 0.1 select_multiply_fusion.2
  43.9 0.1 collective-permute-start.9
  44.0 1.6 %collective-permute-done.9 = f16[1168,128]{1,0:T(8,128)(2,1)S(1)} collective-permute-done((f16[1168,128]{1,0:T(8,128)(2,1)S(1)}, f16[1168,128]{1,0:T(8,128)(2,1)S(1)}, u32[]{:S(2)}, u32[]{:S(2)}) %collective-permute-start.9) | collective-permute-done | bytes 299040 | tf_op jit(solution)/shard_map/ppermute | solution.py:351
  45.6 0.1 fusion
  45.7 0.0 copy-start
  45.7 0.0 copy-start.5
  45.8 0.1 select_multiply_fusion.3
  45.9 1.5 %collective-permute-start.10 = (f16[304,128]{1,0:T(8,128)(2,1)S(1)}, f16[304,128]{1,0:T(8,128)(2,1)S(1)}, u32[]{:S(2)}, u32[]{:S(2)}) collective-permute-start(f16[304,128]{1,0:T(8,128)(2,1)S(1)} %get-tuple-element.45), channel_id=1, source_target_pairs={{0,4},{1,5},{2,6},{3,7},{4,0},{5,1},{6,2},{7,3},{8,12},{9,13},{10,... | collective-permute-start | bytes 233480 | tf_op jit(solution)/shard_map/ppermute | solution.py:351
  47.4 0.2 collective-permute-start.11
  47.6 1.9 %collective-permute-start.12 = (f16[304,128]{1,0:T(8,128)(2,1)S(1)}, f16[304,128]{1,0:T(8,128)(2,1)S(1)}, u32[]{:S(2)}, u32[]{:S(2)}) collective-permute-start(f16[304,128]{1,0:T(8,128)(2,1)S(1)} %get-tuple-element.47), channel_id=1, source_target_pairs={{0,6},{1,7},{2,4},{3,5},{4,2},{5,3},{6,0},{7,1},{8,14},{9,15},{10,... | collective-permute-start | bytes 233480 | tf_op jit(solution)/shard_map/ppermute | solution.py:351
  49.4 0.8 %collective-permute-start.17 = (bf16[2,4,64,128]{3,2,1,0:T(8,128)(2,1)S(1)}, bf16[2,4,64,128]{3,2,1,0:T(8,128)(2,1)S(1)}, u32[]{:S(2)}, u32[]{:S(2)}) collective-permute-start(bf16[2,4,64,128]{3,2,1,0:T(8,128)(2,1)S(1)} %get-tuple-element.53), channel_id=1, source_target_pairs={{1,2},{2,1},{5,6},{6,5},{9,10},{10,9},{13,14},{14,13},{17,18},{18,... | collective-permute-start | bytes 393224 | tf_op jit(solution)/shard_map/ppermute | solution.py:359
  50.3 0.1 collective-permute-done.10
  50.3 3.0 %collective-permute-done.11 = f16[304,128]{1,0:T(8,128)(2,1)S(1)} collective-permute-done((f16[304,128]{1,0:T(8,128)(2,1)S(1)}, f16[304,128]{1,0:T(8,128)(2,1)S(1)}, u32[]{:S(2)}, u32[]{:S(2)}) %collective-permute-start.11) | collective-permute-done | bytes 77856 | tf_op jit(solution)/shard_map/ppermute | solution.py:351
  53.4 0.1 fusion.15
  53.5 4.1 %collective-permute-start.15 = (f16[304,128]{1,0:T(8,128)(2,1)S(1)}, f16[304,128]{1,0:T(8,128)(2,1)S(1)}, u32[]{:S(2)}, u32[]{:S(2)}) collective-permute-start(f16[304,128]{1,0:T(8,128)(2,1)S(1)} %add_convert_fusion.2), channel_id=1, source_target_pairs={{0,24},{1,25},{2,26},{3,27},{4,28},{5,29},{6,30},{7,31},{8,16},{9,... | collective-permute-start | bytes 233480 | tf_op jit(solution)/shard_map/ppermute | solution.py:351
  57.6 0.6 collective-permute-start.13
  58.3 0.0 copy-start.1
  58.3 3.2 %output.1 = bf16[4,16,64,128]{3,2,1,0:T(8,128)(2,1)} custom-call(s32[2]{0:T(128)S(1)} %pad_add_fusion.9.place, bf16[4,8,64,256]{3,2,1,0:T(8,128)(2,1)S(1)} %bitcast.155, bf16[2,4,64,128]{3,2,1,0:T(8,128)(2,1)S(1)} %collective-permute-done.16.first, bf16[2,4,64,128]{3,2,1,0:T(8,128)(2,1)S(1)} %collective-permute-done.17.second, ...), custom_call_target="tpu_custom_call" | custom-call | flops 1610612736 | bytes 4194304 | tf_op jit(solution)/shard_map/output/pallas_call | solution.py:327
  61.6 2.1 %collective-permute-done.14 = f16[304,128]{1,0:T(8,128)(2,1)S(1)} collective-permute-done((f16[304,128]{1,0:T(8,128)(2,1)S(1)}, f16[304,128]{1,0:T(8,128)(2,1)S(1)}, u32[]{:S(2)}, u32[]{:S(2)}) %collective-permute-start.14) | collective-permute-done | bytes 77856 | tf_op jit(solution)/shard_map/ppermute | solution.py:351
  63.7 0.1 fusion.12
  63.8 1.0 %collective-permute-start.20 = (f16[304,128]{1,0:T(8,128)(2,1)S(1)}, f16[304,128]{1,0:T(8,128)(2,1)S(1)}, u32[]{:S(2)}, u32[]{:S(2)}) collective-permute-start(f16[304,128]{1,0:T(8,128)(2,1)S(1)} %add_convert_fusion.1), channel_id=1, source_target_pairs={{0,4},{1,5},{2,6},{3,7},{4,0},{5,1},{6,2},{7,3},{8,12},{9,13},{10,... | collective-permute-start | bytes 233480 | tf_op jit(solution)/shard_map/ppermute | solution.py:351
  64.8 0.6 collective-permute-start.19
  65.4 1.9 %collective-permute-start.18 = (f16[304,128]{1,0:T(8,128)(2,1)S(1)}, f16[304,128]{1,0:T(8,128)(2,1)S(1)}, u32[]{:S(2)}, u32[]{:S(2)}) collective-permute-start(f16[304,128]{1,0:T(8,128)(2,1)S(1)} %add_convert_fusion.1), channel_id=1, source_target_pairs={{0,6},{1,7},{2,4},{3,5},{4,2},{5,3},{6,0},{7,1},{8,14},{9,15},{10,... | collective-permute-start | bytes 233480 | tf_op jit(solution)/shard_map/ppermute | solution.py:351
  67.3 3.5 %grad_frames.1 = bf16[4,16,64,128]{3,2,1,0:T(8,128)(2,1)} custom-call(s32[2]{0:T(128)S(1)} %pad_add_fusion.9.place, bf16[4,8,64,256]{3,2,1,0:T(8,128)(2,1)S(1)} %bitcast.154, bf16[2,4,64,128]{3,2,1,0:T(8,128)(2,1)S(1)} %collective-permute-done.16.first, bf16[2,4,64,128]{3,2,1,0:T(8,128)(2,1)S(1)} %collective-permute-done.17.second, ...), custom_call_target="tpu_custom_call" | custom-call | flops 1610612736 | bytes 4194304 | tf_op jit(solution)/shard_map/grad_frames/pallas_call | solution.py:327
  70.9 0.1 broadcast_select_fusion.7
  71.0 0.1 broadcast_select_fusion.1
  71.1 0.1 pad_maximum_fusion.4
  71.2 0.1 collective-permute-start.21
  71.3 1.5 %collective-permute-done.21 = f16[1216,128]{1,0:T(8,128)(2,1)S(1)} collective-permute-done((f16[1216,128]{1,0:T(8,128)(2,1)S(1)}, f16[1216,128]{1,0:T(8,128)(2,1)S(1)}, u32[]{:S(2)}, u32[]{:S(2)}) %collective-permute-start.21) | collective-permute-done | bytes 311328 | tf_op jit(solution)/shard_map/ppermute | solution.py:351
  72.9 1.1 %select_multiply_fusion = (f32[4,288,128]{2,1,0:T(8,128)}, f32[4,288,128]{2,1,0:T(8,128)}) fusion(f32[4,304,128]{2,1,0:T(8,128)S(1)} %convert.2, f32[4,304,128]{2,1,0:T(8,128)S(1)} %convert.3, f32[4,128]{1,0:T(4,128)S(1)} %bitcast.190, f32[4,128]{1,0:T(4,128)S(1)} %bitcast.191, pred[128]{0:T(512)(128)(4,1)S(1)} %get-tuple-element.170), kind=kLoop, calls=%fused_computation.7 | loop fusion | flops 884736 | bytes 2363520 | tf_op jit(solution)/shard_map/mul | solution.py:588
  (67 shorter events, 0.9 us)
Async XLA Ops:
  1.8 7.2 %collective-permute-start.1 = (bf16[2,4,64,128]{3,2,1,0:T(8,128)(2,1)S(1)}, bf16[2,4,64,128]{3,2,1,0:T(8,128)(2,1)S(1)}, u32[]{:S(2)}, u32[]{:S(2)}) collective-permute-start(bf16[2,4,64,128]{3,2,1,0:T(8,128)(2,1)S(1)} %get-tuple-element.151), channel_id=1, source_target_pairs={{1,2},{2,1},{5,6},{6,5},{9,10},{10,9},{13,14},{14,13},{17,18},{18,... | collective-permute-start | bytes 393224 | tf_op jit(solution)/shard_map/ppermute | solution.py:359
  2.5 6.5 %collective-permute-start = (bf16[2,4,64,128]{3,2,1,0:T(8,128)(2,1)S(1)}, bf16[2,4,64,128]{3,2,1,0:T(8,128)(2,1)S(1)}, u32[]{:S(2)}, u32[]{:S(2)}) collective-permute-start(bf16[2,4,64,128]{3,2,1,0:T(8,128)(2,1)S(1)} %get-tuple-element.152), channel_id=1, source_target_pairs={{0,1},{1,0},{2,3},{3,2},{4,5},{5,4},{6,7},{7,6},{8,9},{9,8},{10,11... | collective-permute-start | bytes 393224 | tf_op jit(solution)/shard_map/ppermute | solution.py:351
  6.9 1.8 %copy-start.2 = (bf16[3,3,128,128]{3,2,1,0:T(8,128)(2,1)S(1)}, bf16[3,3,128,128]{3,2,1,0:T(8,128)(2,1)}, u32[]{:S(2)}) copy-start(bf16[3,3,128,128]{3,2,1,0:T(8,128)(2,1)} %weight.2) | copy-start | bytes 884740
  6.9 1.8 %copy-start.3 = (bf16[3,3,128,128]{3,2,1,0:T(8,128)(2,1)S(1)}, bf16[3,3,128,128]{3,2,1,0:T(8,128)(2,1)}, u32[]{:S(2)}) copy-start(bf16[3,3,128,128]{3,2,1,0:T(8,128)(2,1)} %weight.3) | copy-start | bytes 884740
  6.9 1.9 %copy-start.4 = (f32[4,128]{1,0:T(4,128)S(1)}, f32[4,128]{1,0:T(4,128)}, u32[]{:S(2)}) copy-start(f32[4,128]{1,0:T(4,128)} %log_decay.5) | copy-start | bytes 6148
  14.4 6.1 %collective-permute-start.4 = (f16[272,256]{1,0:T(8,128)(2,1)S(1)}, f16[272,256]{1,0:T(8,128)(2,1)S(1)}, u32[]{:S(2)}, u32[]{:S(2)}) collective-permute-start(f16[272,256]{1,0:T(8,128)(2,1)S(1)} %get-tuple-element.172), channel_id=1, source_target_pairs={{0,4},{1,5},{2,6},{3,7},{4,0},{5,1},{6,2},{7,3},{8,12},{9,13},{10,... | collective-permute-start | bytes 417800 | tf_op jit(solution)/shard_map/ppermute | solution.py:351
  15.9 6.5 %collective-permute-start.3 = (f16[272,256]{1,0:T(8,128)(2,1)S(1)}, f16[272,256]{1,0:T(8,128)(2,1)S(1)}, u32[]{:S(2)}, u32[]{:S(2)}) collective-permute-start(f16[272,256]{1,0:T(8,128)(2,1)S(1)} %get-tuple-element.173), channel_id=1, source_target_pairs={{0,8},{1,9},{2,10},{3,11},{4,12},{5,13},{6,14},{7,15},{8,0},{9,1},... | collective-permute-start | bytes 417800 | tf_op jit(solution)/shard_map/ppermute | solution.py:351
  17.5 7.1 %collective-permute-start.2 = (f16[272,256]{1,0:T(8,128)(2,1)S(1)}, f16[272,256]{1,0:T(8,128)(2,1)S(1)}, u32[]{:S(2)}, u32[]{:S(2)}) collective-permute-start(f16[272,256]{1,0:T(8,128)(2,1)S(1)} %get-tuple-element.174), channel_id=1, source_target_pairs={{0,12},{1,13},{2,14},{3,15},{4,8},{5,9},{6,10},{7,11},{8,4},{9,5},... | collective-permute-start | bytes 417800 | tf_op jit(solution)/shard_map/ppermute | solution.py:351
  25.0 5.5 %collective-permute-start.5 = (f16[144,256]{1,0:T(8,128)(2,1)S(1)}, f16[144,256]{1,0:T(8,128)(2,1)S(1)}, u32[]{:S(2)}, u32[]{:S(2)}) collective-permute-start(f16[144,256]{1,0:T(8,128)(2,1)S(1)} %add_convert_fusion.3), channel_id=1, source_target_pairs={{0,16},{1,17},{2,18},{3,19},{4,20},{5,21},{6,22},{7,23},{8,24},{9,... | collective-permute-start | bytes 221192 | tf_op jit(solution)/shard_map/ppermute | solution.py:351
  31.0 5.8 %collective-permute-start.8 = (f16[272,256]{1,0:T(8,128)(2,1)S(1)}, f16[272,256]{1,0:T(8,128)(2,1)S(1)}, u32[]{:S(2)}, u32[]{:S(2)}) collective-permute-start(f16[272,256]{1,0:T(8,128)(2,1)S(1)} %get-tuple-element.175), channel_id=1, source_target_pairs={{0,4},{1,5},{2,6},{3,7},{4,0},{5,1},{6,2},{7,3},{8,12},{9,13},{10,... | collective-permute-start | bytes 417800 | tf_op jit(solution)/shard_map/ppermute | solution.py:351
  32.5 6.0 %collective-permute-start.6 = (f16[272,256]{1,0:T(8,128)(2,1)S(1)}, f16[272,256]{1,0:T(8,128)(2,1)S(1)}, u32[]{:S(2)}, u32[]{:S(2)}) collective-permute-start(f16[272,256]{1,0:T(8,128)(2,1)S(1)} %get-tuple-element.176), channel_id=1, source_target_pairs={{0,12},{1,13},{2,14},{3,15},{4,8},{5,9},{6,10},{7,11},{8,4},{9,5},... | collective-permute-start | bytes 417800 | tf_op jit(solution)/shard_map/ppermute | solution.py:351
  33.9 5.2 %collective-permute-start.7 = (f16[272,256]{1,0:T(8,128)(2,1)S(1)}, f16[272,256]{1,0:T(8,128)(2,1)S(1)}, u32[]{:S(2)}, u32[]{:S(2)}) collective-permute-start(f16[272,256]{1,0:T(8,128)(2,1)S(1)} %get-tuple-element.177), channel_id=1, source_target_pairs={{0,8},{1,9},{2,10},{3,11},{4,12},{5,13},{6,14},{7,15},{8,0},{9,1},... | collective-permute-start | bytes 417800 | tf_op jit(solution)/shard_map/ppermute | solution.py:351
  43.9 1.7 %collective-permute-start.9 = (f16[1168,128]{1,0:T(8,128)(2,1)S(1)}, f16[1168,128]{1,0:T(8,128)(2,1)S(1)}, u32[]{:S(2)}, u32[]{:S(2)}) collective-permute-start(f16[1168,128]{1,0:T(8,128)(2,1)S(1)} %add_convert_fusion), channel_id=1, source_target_pairs={{0,1},{1,0},{2,3},{3,2},{4,5},{5,4},{6,7},{7,6},{8,9},{9,8},{10,11... | collective-permute-start | bytes 897032 | tf_op jit(solution)/shard_map/ppermute | solution.py:351
  45.7 12.5 %copy-start = (bf16[4,16,64,128]{3,2,1,0:T(8,128)(2,1)S(1)}, bf16[4,16,64,128]{3,2,1,0:T(8,128)(2,1)}, u32[]{:S(2)}) copy-start(bf16[4,16,64,128]{3,2,1,0:T(8,128)(2,1)} %direct.2) | copy-start | bytes 3145732
  45.7 12.5 %copy-start.5 = (f32[128]{0:T(128)S(1)}, f32[128]{0:T(128)}, u32[]{:S(2)}) copy-start(f32[128]{0:T(128)} %param.10) | copy-start | bytes 1540
  45.9 4.5 %collective-permute-start.10 = (f16[304,128]{1,0:T(8,128)(2,1)S(1)}, f16[304,128]{1,0:T(8,128)(2,1)S(1)}, u32[]{:S(2)}, u32[]{:S(2)}) collective-permute-start(f16[304,128]{1,0:T(8,128)(2,1)S(1)} %get-tuple-element.45), channel_id=1, source_target_pairs={{0,4},{1,5},{2,6},{3,7},{4,0},{5,1},{6,2},{7,3},{8,12},{9,13},{10,... | collective-permute-start | bytes 233480 | tf_op jit(solution)/shard_map/ppermute | solution.py:351
  47.4 6.0 %collective-permute-start.11 = (f16[304,128]{1,0:T(8,128)(2,1)S(1)}, f16[304,128]{1,0:T(8,128)(2,1)S(1)}, u32[]{:S(2)}, u32[]{:S(2)}) collective-permute-start(f16[304,128]{1,0:T(8,128)(2,1)S(1)} %get-tuple-element.46), channel_id=1, source_target_pairs={{0,2},{1,3},{2,0},{3,1},{4,6},{5,7},{6,4},{7,5},{8,10},{9,11},{10,... | collective-permute-start | bytes 233480 | tf_op jit(solution)/shard_map/ppermute | solution.py:351
  47.6 5.8 %collective-permute-start.12 = (f16[304,128]{1,0:T(8,128)(2,1)S(1)}, f16[304,128]{1,0:T(8,128)(2,1)S(1)}, u32[]{:S(2)}, u32[]{:S(2)}) collective-permute-start(f16[304,128]{1,0:T(8,128)(2,1)S(1)} %get-tuple-element.47), channel_id=1, source_target_pairs={{0,6},{1,7},{2,4},{3,5},{4,2},{5,3},{6,0},{7,1},{8,14},{9,15},{10,... | collective-permute-start | bytes 233480 | tf_op jit(solution)/shard_map/ppermute | solution.py:351
  49.4 8.8 %collective-permute-start.16 = (bf16[2,4,64,128]{3,2,1,0:T(8,128)(2,1)S(1)}, bf16[2,4,64,128]{3,2,1,0:T(8,128)(2,1)S(1)}, u32[]{:S(2)}, u32[]{:S(2)}) collective-permute-start(bf16[2,4,64,128]{3,2,1,0:T(8,128)(2,1)S(1)} %get-tuple-element.52), channel_id=1, source_target_pairs={{0,1},{1,0},{2,3},{3,2},{4,5},{5,4},{6,7},{7,6},{8,9},{9,8},{10,11... | collective-permute-start | bytes 393224 | tf_op jit(solution)/shard_map/ppermute | solution.py:351
  49.4 8.8 %collective-permute-start.17 = (bf16[2,4,64,128]{3,2,1,0:T(8,128)(2,1)S(1)}, bf16[2,4,64,128]{3,2,1,0:T(8,128)(2,1)S(1)}, u32[]{:S(2)}, u32[]{:S(2)}) collective-permute-start(bf16[2,4,64,128]{3,2,1,0:T(8,128)(2,1)S(1)} %get-tuple-element.53), channel_id=1, source_target_pairs={{1,2},{2,1},{5,6},{6,5},{9,10},{10,9},{13,14},{14,13},{17,18},{18,... | collective-permute-start | bytes 393224 | tf_op jit(solution)/shard_map/ppermute | solution.py:359
  53.5 8.0 %collective-permute-start.15 = (f16[304,128]{1,0:T(8,128)(2,1)S(1)}, f16[304,128]{1,0:T(8,128)(2,1)S(1)}, u32[]{:S(2)}, u32[]{:S(2)}) collective-permute-start(f16[304,128]{1,0:T(8,128)(2,1)S(1)} %add_convert_fusion.2), channel_id=1, source_target_pairs={{0,24},{1,25},{2,26},{3,27},{4,28},{5,29},{6,30},{7,31},{8,16},{9,... | collective-permute-start | bytes 233480 | tf_op jit(solution)/shard_map/ppermute | solution.py:351
  57.6 6.0 %collective-permute-start.14 = (f16[304,128]{1,0:T(8,128)(2,1)S(1)}, f16[304,128]{1,0:T(8,128)(2,1)S(1)}, u32[]{:S(2)}, u32[]{:S(2)}) collective-permute-start(f16[304,128]{1,0:T(8,128)(2,1)S(1)} %add_convert_fusion.2), channel_id=1, source_target_pairs={{0,16},{1,17},{2,18},{3,19},{4,20},{5,21},{6,22},{7,23},{8,24},{9,... | collective-permute-start | bytes 233480 | tf_op jit(solution)/shard_map/ppermute | solution.py:351
  57.6 6.0 %collective-permute-start.13 = (f16[304,128]{1,0:T(8,128)(2,1)S(1)}, f16[304,128]{1,0:T(8,128)(2,1)S(1)}, u32[]{:S(2)}, u32[]{:S(2)}) collective-permute-start(f16[304,128]{1,0:T(8,128)(2,1)S(1)} %add_convert_fusion.2), channel_id=1, source_target_pairs={{0,8},{1,9},{2,10},{3,11},{4,12},{5,13},{6,14},{7,15},{8,0},{9,1},... | collective-permute-start | bytes 233480 | tf_op jit(solution)/shard_map/ppermute | solution.py:351
  58.3 9.0 %copy-start.1 = (bf16[4,16,64,128]{3,2,1,0:T(8,128)(2,1)S(1)}, bf16[4,16,64,128]{3,2,1,0:T(8,128)(2,1)}, u32[]{:S(2)}) copy-start(bf16[4,16,64,128]{3,2,1,0:T(8,128)(2,1)} %direct.3) | copy-start | bytes 3145732
  63.8 7.1 %collective-permute-start.20 = (f16[304,128]{1,0:T(8,128)(2,1)S(1)}, f16[304,128]{1,0:T(8,128)(2,1)S(1)}, u32[]{:S(2)}, u32[]{:S(2)}) collective-permute-start(f16[304,128]{1,0:T(8,128)(2,1)S(1)} %add_convert_fusion.1), channel_id=1, source_target_pairs={{0,4},{1,5},{2,6},{3,7},{4,0},{5,1},{6,2},{7,3},{8,12},{9,13},{10,... | collective-permute-start | bytes 233480 | tf_op jit(solution)/shard_map/ppermute | solution.py:351
  64.8 6.1 %collective-permute-start.19 = (f16[304,128]{1,0:T(8,128)(2,1)S(1)}, f16[304,128]{1,0:T(8,128)(2,1)S(1)}, u32[]{:S(2)}, u32[]{:S(2)}) collective-permute-start(f16[304,128]{1,0:T(8,128)(2,1)S(1)} %add_convert_fusion.1), channel_id=1, source_target_pairs={{0,2},{1,3},{2,0},{3,1},{4,6},{5,7},{6,4},{7,5},{8,10},{9,11},{10,... | collective-permute-start | bytes 233480 | tf_op jit(solution)/shard_map/ppermute | solution.py:351
  65.4 5.4 %collective-permute-start.18 = (f16[304,128]{1,0:T(8,128)(2,1)S(1)}, f16[304,128]{1,0:T(8,128)(2,1)S(1)}, u32[]{:S(2)}, u32[]{:S(2)}) collective-permute-start(f16[304,128]{1,0:T(8,128)(2,1)S(1)} %add_convert_fusion.1), channel_id=1, source_target_pairs={{0,6},{1,7},{2,4},{3,5},{4,2},{5,3},{6,0},{7,1},{8,14},{9,15},{10,... | collective-permute-start | bytes 233480 | tf_op jit(solution)/shard_map/ppermute | solution.py:351
  71.2 1.7 %collective-permute-start.21 = (f16[1216,128]{1,0:T(8,128)(2,1)S(1)}, f16[1216,128]{1,0:T(8,128)(2,1)S(1)}, u32[]{:S(2)}, u32[]{:S(2)}) collective-permute-start(f16[1216,128]{1,0:T(8,128)(2,1)S(1)} %pad_maximum_fusion.4), channel_id=1, source_target_pairs={{0,1},{1,0},{2,3},{3,2},{4,5},{5,4},{6,7},{7,6},{8,9},{9,8},{10,11... | collective-permute-start | bytes 933896 | tf_op jit(solution)/shard_map/ppermute | solution.py:351
